TPU v7x, 256 devices: a whole 4x4x8 slice. The times are simulated.
256 devices in a mesh: grp: 2 (over core), seq: 16 (over x, y), head: 8 (over z).
Axes of the slice: x: 4, y: 4, z: 8, core: 2. Of those that a mesh axis runs over, the one named last changes fastest.
Arguments:
- prompt_q: bfloat16 [2, 3072, 8192], P('grp', 'seq', 'head'), may hold values from -8 to 8
- prompt_kv: bfloat16 [2, 3072, 2048], P('grp', 'seq', 'head'), may hold values from -24 to 24
- sectioned: bfloat16 [2, 512, 32, 2048], P('grp', 'seq', None, 'head'), may hold values from -6 to 6
- handoff_dest: int32 [2, 512, 1], P('grp', 'seq'), may hold values from 0 to 15; in each aligned block of 32 rows (0 to 31, 32 to 63, ..., all dimensions but the last counted through in order) at most 4 rows name the same one
- dec_q: bfloat16 [2, 32, 2, 8192], P('grp', 'seq', None, 'head'), may hold values from -8 to 8
- dec_new: bfloat16 [2, 32, 2, 2048], P('grp', 'seq', None, 'head'), may hold values from -24 to 24
- cache: bfloat16 [2, 32, 1024, 2048], P('grp', 'seq', None, 'head'), may hold values from -24 to 24
- cache_len: int32 [2, 32], P('grp', 'seq'), may hold values from 1 to 1024, 16384 in all within a row
- output_weight: bfloat16 [8192, 8192], P('head', 'seq'), may hold values from -0.09375 to 0.09375
Outputs:
- prompt_attn: bfloat16 [2, 3072, 8192], P('grp', 'seq', 'head')
- arrived: bfloat16 [2, 1024, 32, 2048], P('grp', 'seq', None, 'head')
- decode_out: bfloat16 [2, 64, 8192], P('grp', 'head', 'seq')
Inputs may be any that keep to these rules, and one draw needn't show every extreme that they name: `handoff_dest`: among the rows of one device, at most 4 name the same shard, a bound that some block reaches of them.
All inputs are finite; a program needn't handle non-finite values. No bound on the sum of `cache_len` on one device may be relied on, other than what follows from the above.
Results may differ from a plain program's by a relative error of at most 0.019.
Values may be sent and summed in bfloat16 or wider, within the bound.
No kernel may reach another device: no remote copies, remote signals or barrier semaphores. Data moves between devices by JAX's collectives and lax.ppermute only.
A program may use at most 64 MiB of HBM per device.

v0:
```python
import math

import jax
import jax.numpy as jnp
from jax import lax
from jax.sharding import PartitionSpec as P

QUERY_PER_KEY = 8
HEAD_WIDTH = 128


def per_device(
    prompt_q, prompt_kv, sectioned, handoff_dest, dec_q, dec_new, cache, cache_len, output_weight
):
    score_scale = 1.0 / math.sqrt(HEAD_WIDTH)
    heads_kv = prompt_kv.shape[2] // (2 * HEAD_WIDTH)
    length = prompt_q.shape[1]
    shard_index = lax.axis_index("seq")
    query_rows = prompt_q[0].reshape(length, heads_kv, QUERY_PER_KEY, HEAD_WIDTH)
    query_pos = shard_index * length + jnp.arange(length, dtype=jnp.int32)
    last_pos = shard_index * length + length - 1
    initial = (
        jnp.full((heads_kv, QUERY_PER_KEY, length), -1e30, jnp.float32),
        jnp.zeros((heads_kv, QUERY_PER_KEY, length), jnp.float32),
        jnp.zeros((heads_kv, QUERY_PER_KEY, length, HEAD_WIDTH), jnp.float32),
    )
    state_now = initial
    block_piece = lax.all_gather(prompt_kv, "seq", axis=1, tiled=True)
    piece_start = jnp.int32(0)
    row_count = block_piece.shape[1]
    piece_pairs = block_piece[0].reshape(row_count, heads_kv, 2, HEAD_WIDTH)
    for sub_begin in range(0, row_count, 1536):
        sub_pairs = piece_pairs[sub_begin : sub_begin + 1536]
        sub_width = sub_pairs.shape[0]
        sub_first = piece_start + sub_begin

        def update(old_state):
            running_max, running_sum, accumulated = old_state
            key_pos = sub_first + jnp.arange(sub_width, dtype=jnp.int32)
            scores = (
                jnp.einsum(
                    "pjqd,kjd->jqpk",
                    query_rows,
                    sub_pairs[:, :, 0, :],
                    preferred_element_type=jnp.float32,
                )
                * score_scale
            )
            visible = key_pos[None, :] <= query_pos[:, None]
            scores = jnp.where(visible, scores, -jnp.inf)
            fresh_max = jnp.maximum(running_max, jnp.max(scores, axis=-1))
            exp_scores = jnp.exp(scores - fresh_max[..., None])
            shrink = jnp.exp(running_max - fresh_max)
            new_sum = running_sum * shrink + jnp.sum(exp_scores, axis=-1)
            weights = exp_scores.astype(jnp.bfloat16)
            new_acc = accumulated * shrink[..., None] + jnp.einsum(
                "jqpk,kjd->jqpd", weights, sub_pairs[:, :, 1, :], preferred_element_type=jnp.float32
            )
            return (fresh_max, new_sum, new_acc)

        state_now = lax.cond(sub_first > last_pos, lambda kept_state: kept_state, update, state_now)
    running_max, running_sum, accumulated = state_now
    prompt_attn = (
        (accumulated / running_sum[..., None])
        .transpose(2, 0, 1, 3)
        .reshape(1, length, heads_kv * QUERY_PER_KEY * HEAD_WIDTH)
        .astype(jnp.bfloat16)
    )
    shard_count = lax.axis_size("seq")
    block_count = sectioned.shape[1]
    per_target = 2 * block_count // shard_count
    targets = handoff_dest[0, :, 0]
    hit_table = (targets[:, None] == jnp.arange(shard_count, dtype=jnp.int32)[None, :]).astype(
        jnp.int32
    )
    block_rank = jnp.sum((jnp.cumsum(hit_table, axis=0) - 1) * hit_table, axis=1)
    slot_index = targets * per_target + block_rank
    selector = (
        jnp.arange(shard_count * per_target, dtype=jnp.int32)[:, None] == slot_index[None, :]
    ).astype(jnp.bfloat16)
    flat_blocks = sectioned[0].reshape(block_count, sectioned.shape[2] * sectioned.shape[3])
    outgoing = jnp.dot(selector, flat_blocks, preferred_element_type=jnp.float32).astype(
        jnp.bfloat16
    )
    outgoing = outgoing.reshape(shard_count * per_target, sectioned.shape[2], sectioned.shape[3])
    group_index = lax.axis_index("grp")
    empty_part = jnp.zeros_like(outgoing)
    send_buffer = jnp.where(
        group_index == 0,
        jnp.concatenate([empty_part, outgoing], axis=0),
        jnp.concatenate([outgoing, empty_part], axis=0),
    )
    received = lax.all_to_all(send_buffer, ("grp", "seq"), split_axis=0, concat_axis=0, tiled=True)
    landed = lax.dynamic_slice_in_dim(
        received, (1 - group_index) * shard_count * per_target, shard_count * per_target, 0
    )
    arrived = landed[None]
    req_rows = dec_q.shape[1]
    step_count = dec_q.shape[2]
    capacity = cache.shape[2]
    dec_queries = dec_q[0].reshape(req_rows, step_count, heads_kv, QUERY_PER_KEY, HEAD_WIDTH)
    cache_written = cache[0].reshape(req_rows, capacity, heads_kv, 2, HEAD_WIDTH)
    latest_entry = dec_new[0].reshape(req_rows, step_count, heads_kv, 2, HEAD_WIDTH)
    cache_scores = (
        jnp.einsum(
            "rthqd,rchd->rhqtc",
            dec_queries,
            cache_written[:, :, :, 0, :],
            preferred_element_type=jnp.float32,
        )
        * score_scale
    )
    new_scores = (
        jnp.einsum(
            "rthqd,rshd->rhqts",
            dec_queries,
            latest_entry[:, :, :, 0, :],
            preferred_element_type=jnp.float32,
        )
        * score_scale
    )
    live_mask = jnp.arange(capacity, dtype=jnp.int32)[None, :] < cache_len[0][:, None]
    causal = (
        jnp.arange(step_count, dtype=jnp.int32)[None, :]
        <= jnp.arange(step_count, dtype=jnp.int32)[:, None]
    )
    cache_scores = jnp.where(live_mask[:, None, None, None, :], cache_scores, -jnp.inf)
    new_scores = jnp.where(causal[None, None, None], new_scores, -jnp.inf)
    row_max = jnp.maximum(jnp.max(cache_scores, axis=-1), jnp.max(new_scores, axis=-1))
    cache_weights = jnp.exp(cache_scores - row_max[..., None])
    new_weights = jnp.exp(new_scores - row_max[..., None])
    weight_sum = jnp.sum(cache_weights, axis=-1) + jnp.sum(new_weights, axis=-1)
    weighted = jnp.einsum(
        "rhqtc,rchd->rthqd",
        cache_weights.astype(jnp.bfloat16),
        cache_written[:, :, :, 1, :],
        preferred_element_type=jnp.float32,
    )
    weighted = weighted + jnp.einsum(
        "rhqts,rshd->rthqd",
        new_weights.astype(jnp.bfloat16),
        latest_entry[:, :, :, 1, :],
        preferred_element_type=jnp.float32,
    )
    attn_rows = (weighted / weight_sum.transpose(0, 3, 1, 2)[..., None]).astype(jnp.bfloat16)
    attn_rows = attn_rows.reshape(req_rows * step_count, heads_kv * QUERY_PER_KEY * HEAD_WIDTH)
    gathered = lax.all_gather(attn_rows, "seq", axis=0, tiled=True)
    all_rows = gathered.shape[0]
    my_share = all_rows // lax.axis_size("head")
    summed = lax.psum(
        jnp.dot(gathered, output_weight, preferred_element_type=jnp.float32).astype(jnp.bfloat16),
        "head",
    ).astype(jnp.float32)
    my_rows = lax.dynamic_slice_in_dim(summed, lax.axis_index("head") * my_share, my_share, 0)
    decode_out = my_rows.astype(jnp.bfloat16)[None]
    return (prompt_attn, arrived, decode_out)


def solution(mesh):
    placed = (
        P("grp", "seq", "head"),
        P("grp", "seq", "head"),
        P("grp", "seq", None, "head"),
        P("grp", "seq", None),
        P("grp", "seq", None, "head"),
        P("grp", "seq", None, "head"),
        P("grp", "seq", None, "head"),
        P("grp", "seq"),
        P("head", "seq"),
    )
    return jax.shard_map(
        per_device,
        mesh=mesh,
        in_specs=placed,
        out_specs=(P("grp", "seq", "head"), P("grp", "seq", None, "head"), P("grp", "head", "seq")),
        check_vma=False,
    )
```

profile of v0, /device:TPU:6, one launch (start us, length us, event | category | flops | bytes accessed | tf_op | source)
XLA Modules:
  0.0 143.4 jit_solution(3397540471717112199)
XLA Ops:
  8.1 1.6 %copy.39 = bf16[1,2,1024,256]{2,3,1,0:T(8,128)(2,1)S(1)} copy(bf16[1,2,1024,256]{3,2,1,0:T(8,128)(2,1)} %param.19) | data formatting | bytes 2097152 | tf_op args[6]
  10.4 0.7 iota_compare_fusion.4
  13.1 23.6 %all-gather = bf16[16,4,1024]{2,1,0:T(4,128)(2,1)S(1)} all-gather(bf16[1,4,1024]{2,1,0:T(4,128)(2,1)S(1)} %reshape.260), channel_id=1, replica_groups=mesh['grp'=2,'seq'=16,'head'=8] {'seq'}, dimensions={0}, use_global_device_ids=true | all-gather | bytes 139264 | tf_op jit(solution)/shard_map/all_gather | solution.py:147
  36.7 0.9 convolution_convert_fusion.1
  39.0 1.3 copy.59
  40.4 0.8 select_reduce_fusion
  42.6 1.5 %pad_select_fusion = bf16[128,32,256]{2,1,0:T(8,128)(2,1)} fusion(bf16[64,32,256]{2,1,0:T(8,128)(2,1)S(1)} %bitcast.223, pred[]{:T(512)S(6)} %eq.14), kind=kLoop, calls=%fused_computation.47 | loop fusion | flops 1048576 | bytes 3145729 | tf_op jit(solution)/shard_map/jit(_where)/select_n | solution.py:88
  44.1 5.8 %all-to-all-start = ((bf16[128,32,256]{2,1,0:T(8,128)(2,1)}), bf16[128,32,256]{2,1,0:T(8,128)(2,1)S(1)}, u32[]{:S(2)}, u32[]{:S(2)}) async-start(bf16[128,32,256]{2,1,0:T(8,128)(2,1)} %pad_select_fusion), calls=%async_computation | async-start | bytes 4194304 | tf_op jit(solution)/shard_map/all_to_all | solution.py:93
  49.9 1.1 copy.58
  51.0 59.4 %all-reduce.4.cloned.1.call-done = bf16[64,512]{1,0:T(8,128)(2,1)} async-done(((bf16[64,512]{1,0:T(8,128)(2,1)}), bf16[64,512]{1,0:T(8,128)(2,1)}) %all-reduce.4.cloned.1.call-update) | async-done | bytes 65552 | tf_op jit(solution)/shard_map/psum | solution.py:150
  110.4 1.3 fusion.54
  111.7 1.0 dynamic-slice_bitcast_fusion
  112.7 9.8 %conditional.2 = (f32[1,8,192]{2,1,0:T(8,128)S(1)}, f32[1,8,192]{2,1,0:T(8,128)S(1)}, f32[1,8,192,128]{3,2,1,0:T(8,128)}) conditional(s32[]{:T(128)} %convert_element_type.55, (s32[192]{0:T(256)S(1)}, bf16[1,3072,256]{2,1,0:T(8,128)(2,1)}, bf16[192,1,8,128]{3,2,0,1:T(8,128)(2,1)S(1)}) %tuple.50, () %tuple.24), branch_computations={%region_0.3_spmd, %region_3.4_spmd} | conditional | flops 1234411008 | bytes 36254488 | solution.py:61
  113.0 1.7 %copy.34 = bf16[1,3072,256]{1,2,0:T(8,128)(2,1)S(1)} copy(bf16[1,3072,256]{2,1,0:T(8,128)(2,1)} %get-tuple-element.58) | data formatting | bytes 3145728 | tf_op jit(solution)/shard_map
  114.7 1.8 %fusion.2 = (f32[8,192]{1,0:T(8,128)S(1)}, f32[1536,192,8]{0,1,2:T(8,128)S(1)}) fusion(pred[192,1536]{1,0:T(8,128)(4,1)S(1)} %iota_compare_fusion, bf16[192,1,8,128]{3,2,0,1:T(8,128)(2,1)S(1)} %get-tuple-element.59, bf16[1536,1,2,128]{0,3,2,1:T(8,128)(2,1)S(1)} %bitcast.228), kind=kOutput, calls=%fused_computation.4 | convolution fusion | flops 611056128 | bytes 10524672 | tf_op jit(solution)/shard_map/cond/branch_0_fun/pjqd,kjd->jqpk/dot_general | solution.py:41
  116.6 2.5 %fusion.1 = f32[8,192]{1,0:T(8,128)S(1)} fusion(f32[1536,192,8]{0,1,2:T(8,128)S(1)} %get-tuple-element.75, f32[8,192]{1,0:T(8,128)S(1)} %get-tuple-element.73, pred[192,1536]{1,0:T(8,128)(4,1)S(1)} %iota_compare_fusion), kind=kLoop, calls=%fused_computation.3 | loop fusion | flops 9435648 | bytes 9744384 | tf_op jit(solution)/shard_map/cond/branch_0_fun/reduce_sum | solution.py:54
  119.1 3.4 %fusion.10 = f32[1,8,192,128]{3,2,1,0:T(8,128)} fusion(f32[1536,192,8]{0,1,2:T(8,128)S(1)} %get-tuple-element.75, f32[8,192]{1,0:T(8,128)S(1)} %get-tuple-element.73, pred[192,1536]{1,0:T(8,128)(4,1)S(1)} %iota_compare_fusion, bf16[1536,1,2,128]{0,3,2,1:T(8,128)(2,1)S(1)} %bitcast.229, f32[8,192]{1,0:T(8,128)S(1)} %get-tuple-element.72), kind=kOutput, calls=%fused_computation.9 | convolution fusion | flops 613613568 | bytes 10928128 | tf_op jit(solution)/shard_map/cond/branch_0_fun/jqpk,kjd->jqpd/dot_general | solution.py:56
  122.5 10.8 %conditional.3 = ((f32[1,8,192]{2,1,0:T(8,128)S(1)}, f32[1,8,192,128]{3,2,1,0:T(8,128)})) conditional(s32[]{:T(128)} %convert_element_type.54, (s32[192]{0:T(256)S(1)}, bf16[1,3072,256]{2,1,0:T(8,128)(2,1)}, bf16[192,1,8,128]{3,2,0,1:T(8,128)(2,1)S(1)}, f32[1,8,192]{2,1,0:T(8,128)S(1)}, f32[1,8,192]{2,1,0:T(8,128)S(1)}, ...), branch_computations={%region_4.7_spmd, %region_7.8_spmd} | conditional | flops 1234607616 | bytes 37065496 | solution.py:61
  122.8 1.7 %copy.36 = bf16[1,3072,256]{1,2,0:T(8,128)(2,1)S(1)} copy(bf16[1,3072,256]{2,1,0:T(8,128)(2,1)} %get-tuple-element.61) | data formatting | bytes 3145728 | tf_op jit(solution)/shard_map
  124.5 1.8 %fusion.21 = (f32[8,192]{1,0:T(8,128)S(1)}, f32[1536,192,8]{0,1,2:T(8,128)S(1)}) fusion(pred[192,1536]{1,0:T(8,128)(4,1)S(1)} %broadcast_compare_fusion, bf16[192,1,8,128]{3,2,0,1:T(8,128)(2,1)S(1)} %get-tuple-element.62, bf16[1536,1,2,128]{0,3,2,1:T(8,128)(2,1)S(1)} %bitcast.230), kind=kOutput, calls=%fused_computation.26 | convolution fusion | flops 611056128 | bytes 10524672 | tf_op jit(solution)/shard_map/cond/branch_0_fun/pjqd,kjd->jqpk/dot_general | solution.py:41
  126.4 2.5 %fusion.20 = f32[8,192]{1,0:T(8,128)S(1)} fusion(f32[1536,192,8]{0,1,2:T(8,128)S(1)} %get-tuple-element.71, f32[8,192]{1,0:T(8,128)S(1)} %get-tuple-element.69, pred[192,1536]{1,0:T(8,128)(4,1)S(1)} %broadcast_compare_fusion), kind=kLoop, calls=%fused_computation.25 | loop fusion | flops 9435648 | bytes 9744384 | tf_op jit(solution)/shard_map/cond/branch_0_fun/reduce_sum | solution.py:54
  128.9 4.4 %fusion.29 = f32[1,8,192,128]{3,2,1,0:T(8,128)} fusion(f32[1536,192,8]{0,1,2:T(8,128)S(1)} %get-tuple-element.71, f32[8,192]{1,0:T(8,128)S(1)} %get-tuple-element.69, pred[192,1536]{1,0:T(8,128)(4,1)S(1)} %broadcast_compare_fusion, f32[1,8,192,128]{3,2,1,0:T(8,128)} %get-tuple-element.34, bf16[1536,1,2,128]{0,3,2,1:T(8,128)(2,1)S(1)} %bitcast.231, ...), kind=kOutput, calls=%fused_computation.31 | convolution fusion | flops 613810176 | bytes 11714560 | tf_op jit(solution)/shard_map/cond/branch_0_fun/jqpk,kjd->jqpd/dot_general | solution.py:56
  133.3 1.4 fusion.46
  135.0 0.9 convert_element_type.58
  (39 shorter events, 6.4 us)
Async XLA Ops:
  8.0 28.7 %copy-start = (bf16[1024,512]{1,0:T(8,128)(2,1)S(1)}, bf16[1024,512]{1,0:T(8,128)(2,1)}, u32[]{:S(2)}) copy-start(bf16[1024,512]{1,0:T(8,128)(2,1)} %param.21) | copy-start | bytes 3145732
  8.0 102.4 %all-reduce.4.cloned.1.call-start = ((), (), s32[]{:S(2)}) async-start(), calls=%async_computation.2 | async-start | bytes 131072 | tf_op jit(solution)/shard_map/psum | solution.py:150
  37.7 75.0 %all-gather.3.cloned.1.call-start = ((), (), s32[]{:S(2)}) async-start(), calls=%async_computation.1 | async-start | bytes 1671168 | tf_op jit(solution)/shard_map/all_gather | solution.py:28
  44.1 67.6 %all-to-all-start = ((bf16[128,32,256]{2,1,0:T(8,128)(2,1)}), bf16[128,32,256]{2,1,0:T(8,128)(2,1)S(1)}, u32[]{:S(2)}, u32[]{:S(2)}) async-start(bf16[128,32,256]{2,1,0:T(8,128)(2,1)} %pad_select_fusion), calls=%async_computation | async-start | bytes 4194304 | tf_op jit(solution)/shard_map/all_to_all | solution.py:93
Sparse Core Ops, SparseCore 0:
  37.8 72.5 all-reduce.3
Sparse Core Ops, SparseCore 1:
  40.6 64.9 all-gather.2
where the time goes:
time: 144 us; the launch traced here: 143 us
  waiting for transfers between devices  59.9 us (42%)
  blocking collectives  23.6 us (16%)
  between operations  15.6 us (11%)
  matrix products  13.6 us (9%)
  other arithmetic  13.1 us (9%)
  local copies, waits for them, and re-layouts  11.5 us (8%)
  starting transfers between devices  5.91 us (4%)
    psum x1, waiting for transfers between devices, per_device(): lax.psum(jnp.dot(gathered, output_weight, preferred_element_type=jnp.floa...  59.4 us
    all_gather x1, blocking collectives, per_device(): gathered = lax.all_gather(attn_rows, 'seq', axis=0, tiled=True)  23.6 us
    dot_general x2, matrix products, update(): jnp.einsum('jqpk,kjd->jqpd', weights, sub_pairs[:, :, 1, :], preferred_el...  7.78 us
    all_to_all x1, starting transfers between devices, per_device(): lax.all_to_all(send_buffer, ('grp', 'seq'), split_axis=0, concat_axis=0,...  5.83 us
    reduce_sum x2, other arithmetic, update(): new_sum = running_sum * shrink + jnp.sum(exp_scores, axis=-1)  5.05 us
    unnamed x8, local copies, waits for them, and re-layouts  4.31 us
    another operation x3, local copies, waits for them, and re-layouts  4.14 us
    dot_general x2, matrix products, update(): jnp.einsum('pjqd,kjd->jqpk', query_rows, sub_pairs[:, :, 0, :], preferred...  3.63 us
  transfers between devices with their start and end apart: 3, of which 1 were waited for; matrix products, arithmetic and copies ran while one was open for 6% of the time, Pallas kernels for 0%

commit v1 on v0

v1 whole, which is shorter than its diff:
```python
import math

import jax
import jax.numpy as jnp
from jax import lax
from jax.experimental import pallas as pl
from jax.experimental.pallas import tpu as pltpu
from jax.sharding import PartitionSpec as P

QUERY_PER_KEY = 8
HEAD_WIDTH = 128
SCORE_SCALE = 1.0 / math.sqrt(HEAD_WIDTH)
EXP2_SCALE = SCORE_SCALE * math.log2(math.e)
LOWEST = -3.0e38
SLOTS = 4
BLOCKS_PER_CHUNK = 4

NT = (((1,), (1,)), ((), ()))
NN = (((1,), (0,)), ((), ()))


def dot(a, b, dims=NN):
    return lax.dot_general(a, b, dims, preferred_element_type=jnp.float32)


def prompt_kernel(shard_ref, q_ref, kv_ref, out_ref, val, acc, top):
    shard = shard_ref[0]
    length = q_ref.shape[0]
    chunk = BLOCKS_PER_CHUNK * length
    val[:, HEAD_WIDTH:] = jnp.ones((chunk, HEAD_WIDTH), jnp.bfloat16)

    def step(at, masked, first):
        kv = kv_ref[pl.ds(at * BLOCKS_PER_CHUNK, BLOCKS_PER_CHUNK)].reshape(chunk, 2 * HEAD_WIDTH)
        keys = kv[:, :HEAD_WIDTH]
        val[:, :HEAD_WIDTH] = kv[:, HEAD_WIDTH:]
        if masked:
            key_pos = at * chunk + lax.broadcasted_iota(jnp.int32, (length, chunk), 1)
            query_pos = shard * length + lax.broadcasted_iota(jnp.int32, (length, chunk), 0)
            visible = key_pos <= query_pos
        for head in range(QUERY_PER_KEY):
            rows = pl.ds(head * length, length)
            q = q_ref[:, head * HEAD_WIDTH : (head + 1) * HEAD_WIDTH]
            scores = dot(q, keys, NT)
            if masked:
                scores = jnp.where(visible, scores, LOWEST)
            peak = jnp.max(scores, axis=1, keepdims=True)
            if not first:
                old = top[rows, :]
                peak = jnp.maximum(old[:, :1], peak)
            weights = jnp.exp2((scores - peak) * EXP2_SCALE).astype(jnp.bfloat16)
            part = dot(weights, val[...])
            if not first:
                part = acc[rows, :] * jnp.exp2((old[:, :1] - peak) * EXP2_SCALE) + part
            if masked:
                out_ref[:, head * HEAD_WIDTH : (head + 1) * HEAD_WIDTH] = (
                    part[:, :HEAD_WIDTH] / part[:, HEAD_WIDTH:]
                ).astype(jnp.bfloat16)
            else:
                acc[rows, :] = part
                top[rows, :] = jnp.broadcast_to(peak, (length, HEAD_WIDTH))

    last = shard // BLOCKS_PER_CHUNK

    @pl.when(last == 0)
    def _():
        step(0, True, True)

    @pl.when(last > 0)
    def _():
        step(0, False, True)

        @pl.loop(1, last)
        def _(at):
            step(at, False, False)

        step(last, True, False)


def prompt_attention(shard, q, kv):
    length = q.shape[0]
    rows = QUERY_PER_KEY * length
    chunk = BLOCKS_PER_CHUNK * length
    whole = pl.BlockSpec(memory_space=pltpu.VMEM)
    return pl.pallas_call(
        prompt_kernel,
        out_shape=jax.ShapeDtypeStruct(q.shape, jnp.bfloat16),
        in_specs=[pl.BlockSpec(memory_space=pltpu.SMEM), whole, whole],
        out_specs=whole,
        scratch_shapes=[
            pltpu.VMEM((chunk, 2 * HEAD_WIDTH), jnp.bfloat16),
            pltpu.VMEM((rows, 2 * HEAD_WIDTH), jnp.float32),
            pltpu.VMEM((rows, HEAD_WIDTH), jnp.float32),
        ],
        compiler_params=pltpu.CompilerParams(vmem_limit_bytes=24 << 20),
        cost_estimate=pl.CostEstimate(
            flops=6 * rows * 16 * length * HEAD_WIDTH,
            bytes_accessed=2 * (2 * q.size + kv.size),
            transcendentals=rows * 16 * length,
        ),
        name="prompt_attention",
    )(shard, q, kv)


def decode_kernel(len_ref, q_ref, new_ref, cache_ref, out_ref, q_rows, fresh, out_rows):
    requests, steps, _ = q_ref.shape
    capacity = cache_ref.shape[1]
    rows = QUERY_PER_KEY * steps
    for req in range(requests):
        for head in range(QUERY_PER_KEY):
            q_rows[head * steps : (head + 1) * steps, :] = q_ref[
                req, :, head * HEAD_WIDTH : (head + 1) * HEAD_WIDTH
            ].astype(jnp.float32)
        q = q_rows[...].astype(jnp.bfloat16)
        fresh[...] = jnp.zeros_like(fresh)
        fresh[:steps, :] = new_ref[req].astype(jnp.float32)
        new = fresh[...].astype(jnp.bfloat16)
        kv = cache_ref[req]
        scores = dot(q, kv[:, :HEAD_WIDTH], NT)
        position = lax.broadcasted_iota(jnp.int32, (rows, capacity), 1)
        scores = jnp.where(position < len_ref[0, req], scores, LOWEST)
        new_scores = dot(q, new[:, :HEAD_WIDTH], NT)
        width = new.shape[0]
        new_pos = lax.broadcasted_iota(jnp.int32, (rows, width), 1)
        step = lax.broadcasted_iota(jnp.int32, (rows, width), 0) % steps
        new_scores = jnp.where(new_pos <= step, new_scores, LOWEST)
        peak = jnp.maximum(
            jnp.max(scores, axis=1, keepdims=True), jnp.max(new_scores, axis=1, keepdims=True)
        )
        weights = jnp.exp2((scores - peak) * EXP2_SCALE)
        new_weights = jnp.exp2((new_scores - peak) * EXP2_SCALE)
        total = jnp.sum(weights, axis=1, keepdims=True) + jnp.sum(new_weights, axis=1, keepdims=True)
        summed = dot(weights.astype(jnp.bfloat16), kv[:, HEAD_WIDTH:])
        summed = summed + dot(new_weights.astype(jnp.bfloat16), new[:, HEAD_WIDTH:])
        result = summed / total
        for head in range(QUERY_PER_KEY):
            out_rows[
                req * steps : (req + 1) * steps, head * HEAD_WIDTH : (head + 1) * HEAD_WIDTH
            ] = result[head * steps : (head + 1) * steps, :]
    out_ref[...] = out_rows[...].astype(jnp.bfloat16)


def decode_attention(lengths, q, new, cache):
    requests, steps, width = q.shape
    whole = pl.BlockSpec(memory_space=pltpu.VMEM)
    return pl.pallas_call(
        decode_kernel,
        out_shape=jax.ShapeDtypeStruct((requests * steps, width), jnp.bfloat16),
        in_specs=[pl.BlockSpec(memory_space=pltpu.SMEM), whole, whole, whole],
        out_specs=whole,
        scratch_shapes=[
            pltpu.VMEM((QUERY_PER_KEY * steps, HEAD_WIDTH), jnp.float32),
            pltpu.VMEM((HEAD_WIDTH, 2 * HEAD_WIDTH), jnp.float32),
            pltpu.VMEM((requests * steps, width), jnp.float32),
        ],
        compiler_params=pltpu.CompilerParams(vmem_limit_bytes=16 << 20),
        cost_estimate=pl.CostEstimate(
            flops=4 * q.size * cache.shape[1], bytes_accessed=2 * cache.size, transcendentals=0
        ),
        name="decode_attention",
    )(lengths, q, new, cache)


def place_kernel(dest_ref, blocks_ref, out_ref, count):
    targets = out_ref.shape[0] // SLOTS
    for target in range(targets):
        count[target] = 0
    out_ref[...] = jnp.zeros_like(out_ref)

    @pl.loop(0, blocks_ref.shape[0])
    def _(block):
        target = dest_ref[0, block]
        rank = count[target]
        count[target] = rank + 1
        slot = jnp.minimum(target * SLOTS + rank, targets * SLOTS - 1)
        out_ref[pl.ds(slot, 1)] = blocks_ref[pl.ds(block, 1)]


def place_blocks(dest, blocks, targets):
    whole = pl.BlockSpec(memory_space=pltpu.VMEM)
    shape = (targets * SLOTS,) + blocks.shape[1:]
    return pl.pallas_call(
        place_kernel,
        out_shape=jax.ShapeDtypeStruct(shape, blocks.dtype),
        in_specs=[pl.BlockSpec(memory_space=pltpu.SMEM), whole],
        out_specs=whole,
        scratch_shapes=[pltpu.SMEM((targets,), jnp.int32)],
        compiler_params=pltpu.CompilerParams(vmem_limit_bytes=16 << 20),
        cost_estimate=pl.CostEstimate(flops=0, bytes_accessed=6 * blocks.size, transcendentals=0),
        name="place_blocks",
    )(dest, blocks)


def project_kernel(rows_ref, weight_ref, out_ref, rows):
    sources, height, _ = rows_ref.shape
    for source in range(sources):
        rows[source * height : (source + 1) * height, :] = rows_ref[source].astype(jnp.float32)
    out_ref[...] = dot(rows[...].astype(jnp.bfloat16), weight_ref[...]).astype(jnp.bfloat16)


def project(rows, weight):
    sources, height, width = rows.shape
    whole = pl.BlockSpec(memory_space=pltpu.VMEM)
    return pl.pallas_call(
        project_kernel,
        out_shape=jax.ShapeDtypeStruct((sources * height, weight.shape[1]), jnp.bfloat16),
        in_specs=[whole, whole],
        out_specs=whole,
        scratch_shapes=[pltpu.VMEM((sources * height, width), jnp.float32)],
        compiler_params=pltpu.CompilerParams(vmem_limit_bytes=16 << 20),
        cost_estimate=pl.CostEstimate(
            flops=2 * sources * height * weight.size, bytes_accessed=2 * weight.size, transcendentals=0
        ),
        name="project",
    )(rows, weight)


def per_device(
    prompt_q, prompt_kv, sectioned, handoff_dest, dec_q, dec_new, cache, cache_len, output_weight
):
    shards = lax.axis_size("seq")
    shard = lax.axis_index("seq").reshape(1)
    swap = [(0, 1), (1, 0)]

    spread = jnp.broadcast_to(prompt_kv, (shards,) + prompt_kv.shape[1:])
    all_kv = lax.all_to_all(spread, "seq", 0, 0, tiled=True)
    prompt_attn = prompt_attention(shard, prompt_q[0], all_kv)

    other_dest = lax.ppermute(handoff_dest.reshape(1, -1), "grp", swap)
    other_blocks = lax.ppermute(sectioned[0], "grp", swap)
    outgoing = place_blocks(other_dest, other_blocks, shards)
    arrived = lax.all_to_all(outgoing, "seq", 0, 0, tiled=True)

    rows = decode_attention(cache_len, dec_q[0], dec_new[0], cache[0])
    rows = jnp.broadcast_to(rows[None], (shards,) + rows.shape)
    rows = lax.all_to_all(rows, "seq", 0, 0, tiled=True)
    partial = project(rows, output_weight)
    ranks = lax.axis_size("head")
    parts = lax.all_to_all(
        partial.reshape(ranks, partial.shape[0] // ranks, partial.shape[1]), "head", 0, 0, tiled=True
    )
    decode_out = jnp.sum(parts.astype(jnp.float32), axis=0).astype(jnp.bfloat16)
    return (prompt_attn[None], arrived[None], decode_out[None])


def solution(mesh):
    placed = (
        P("grp", "seq", "head"),
        P("grp", "seq", "head"),
        P("grp", "seq", None, "head"),
        P("grp", "seq", None),
        P("grp", "seq", None, "head"),
        P("grp", "seq", None, "head"),
        P("grp", "seq", None, "head"),
        P("grp", "seq"),
        P("head", "seq"),
    )
    return jax.shard_map(
        per_device,
        mesh=mesh,
        in_specs=placed,
        out_specs=(P("grp", "seq", "head"), P("grp", "seq", None, "head"), P("grp", "head", "seq")),
        check_vma=False,
    )
```

time: 144 us -> 82.3 us (0.57)
  waiting for transfers between devices: 59.9 us -> 19.6 us
  between operations: 15.6 us -> 0.71 us
  matrix products: 13.6 us -> 0 us
  Pallas kernels: 0 us -> 12.9 us
  other arithmetic: 13.1 us -> 0.61 us
  starting transfers between devices: 5.91 us -> 12.1 us
  blocking collectives: 23.6 us -> 29.7 us
  local copies, waits for them, and re-layouts: 11.5 us -> 5.69 us
    psum x1 -> x0, waiting for transfers between devices: 59.4 us -> none  [per_device(): lax.psum(jnp.dot(gathered, output_weight, preferred_element_type=jnp.floa...]
    all_to_all x0 -> x2, blocking collectives: none -> 29.7 us  [the longest x1 16.6 us: per_device(): lax.all_to_all(partial.reshape(ranks, partial.shape[0] // ranks, partial....]
    all_gather x1 -> x0, blocking collectives: 23.6 us -> none  [per_device(): gathered = lax.all_gather(attn_rows, 'seq', axis=0, tiled=True)]
    all_to_all x1 -> x2, waiting for transfers between devices: 0.01 us -> 18.2 us  [the longest x1 14.8 us: per_device(): all_kv = lax.all_to_all(spread, 'seq', 0, 0, tiled=True)]
    dot_general x10 -> x0, matrix products: 13.6 us -> none  [the longest x2 7.78 us: update(): jnp.einsum('jqpk,kjd->jqpd', weights, sub_pairs[:, :, 1, :], preferred_el...]
    pallas_call x0 -> x4, Pallas kernels: none -> 12.9 us  [the longest x1 9.35 us: prompt_attention(): pl.pallas_call(prompt_kernel, out_shape=jax.ShapeDtypeStruct(q.shape, jnp...]
    all_to_all x1 -> x2, starting transfers between devices: 5.83 us -> 11.6 us  [the longest x1 5.79 us: per_device(): arrived = lax.all_to_all(outgoing, 'seq', 0, 0, tiled=True)]
    reduce_sum x4 -> x1, other arithmetic: 6.07 us -> 0.61 us  [per_device(): decode_out = jnp.sum(parts.astype(jnp.float32), axis=0).astype(jnp.bfloat16)]
  transfers between devices with their start and end apart: 3 -> 4, of which waited for: 1 -> 3; matrix products, arithmetic and copies ran while one was open for 6% -> 1% of each run, Pallas kernels for 0% -> 14%
where the time goes in v1:
time: 82.3 us; the launch traced here: 81.4 us
  blocking collectives  29.7 us (36%)
  waiting for transfers between devices  19.6 us (24%)
  Pallas kernels  12.9 us (16%)
  starting transfers between devices  12.1 us (15%)
  local copies, waits for them, and re-layouts  5.69 us (7%)
    all_to_all x1, blocking collectives, per_device(): lax.all_to_all(partial.reshape(ranks, partial.shape[0] // ranks, partial....  16.6 us
    all_to_all x1, waiting for transfers between devices, per_device(): all_kv = lax.all_to_all(spread, 'seq', 0, 0, tiled=True)  14.8 us
    all_to_all x1, blocking collectives, per_device(): rows = lax.all_to_all(rows, 'seq', 0, 0, tiled=True)  13.1 us
    pallas_call x1, Pallas kernels, prompt_attention(): pl.pallas_call(prompt_kernel, out_shape=jax.ShapeDtypeStruct(q.shape, jnp...  9.35 us
    all_to_all x1, starting transfers between devices, per_device(): arrived = lax.all_to_all(outgoing, 'seq', 0, 0, tiled=True)  5.79 us
    all_to_all x1, starting transfers between devices, per_device(): all_kv = lax.all_to_all(spread, 'seq', 0, 0, tiled=True)  5.77 us
    unnamed x19, local copies, waits for them, and re-layouts  4.33 us
    all_to_all x1, waiting for transfers between devices, per_device(): arrived = lax.all_to_all(outgoing, 'seq', 0, 0, tiled=True)  3.44 us
  transfers between devices with their start and end apart: 4, of which 3 were waited for; matrix products, arithmetic and copies ran while one was open for 1% of the time, Pallas kernels for 14%

profile of v1, /device:TPU:6, one launch (start us, length us, event | category | flops | bytes accessed | tf_op | source)
XLA Modules:
  0.0 81.4 jit_solution(17386018952069377630)
XLA Ops:
  0.6 0.0 copy-start
  0.7 1.3 %copy-done.1 = bf16[1,2,1024,256]{3,2,1,0:T(8,128)(2,1)S(1)} copy-done((bf16[1,2,1024,256]{3,2,1,0:T(8,128)(2,1)S(1)}, bf16[1,2,1024,256]{3,2,1,0:T(8,128)(2,1)}, u32[]{:S(2)}) %copy-start.1) | copy-done | bytes 1048600
  2.0 0.7 copy-done.2
  2.7 0.7 copy-done.3
  3.3 0.7 copy-done.4
  4.0 1.3 %decode_attention.1 = bf16[4,1024]{1,0:T(4,128)(2,1)S(1)} custom-call(s32[1,2]{1,0:T(1,128)S(1)} %copy-done.4, bf16[2,2,1024]{2,1,0:T(2,128)(2,1)S(1)} %bitcast.14, bf16[2,2,256]{2,1,0:T(2,128)(2,1)S(1)} %bitcast.15, bf16[2,1024,256]{2,1,0:T(8,128)(2,1)S(1)} %bitcast.12), custom_call_target="tpu_custom_call" | custom-call | flops 16777216 | bytes 1048576 | tf_op jit(solution)/shard_map/decode_attention/pallas_call | solution.py:145
  5.4 13.1 %all_to_all.20.rows_ref = bf16[16,4,1024]{2,1,0:T(4,128)(2,1)S(1)} all-to-all(bf16[16,4,1024]{2,1,0:T(4,128)(2,1)S(1)} %broadcast_in_dim.26), channel_id=1, replica_groups=mesh['grp'=2,'seq'=16,'head'=8] {'seq'}, dimensions={0} | all-to-all | bytes 262144 | tf_op jit(solution)/shard_map/all_to_all | solution.py:235
  18.5 0.3 project.1
  18.8 16.6 %all_to_all.21 = bf16[8,8,512]{2,1,0:T(8,128)(2,1)S(1)} all-to-all(bf16[8,8,512]{2,1,0:T(8,128)(2,1)S(1)} %bitcast.13), channel_id=1, replica_groups=mesh['grp'=2,'seq'=16,'head'=8] {'head'}, dimensions={0} | all-to-all | bytes 131072 | tf_op jit(solution)/shard_map/all_to_all | solution.py:238
  35.4 1.3 %broadcast_in_dim.23 = bf16[16,192,256]{2,1,0:T(8,128)(2,1)} broadcast(bf16[192,256]{1,0:T(8,128)(2,1)S(1)} %bitcast.18), dimensions={1,2} | broadcast | bytes 1671168 | tf_op jit(solution)/shard_map/broadcast_in_dim | solution.py:224
  36.8 5.8 %all-to-all-start = ((bf16[16,192,256]{2,1,0:T(8,128)(2,1)}), bf16[16,192,256]{2,1,0:T(8,128)(2,1)S(1)}, u32[]{:S(2)}, u32[]{:S(2)}) async-start(bf16[16,192,256]{2,1,0:T(8,128)(2,1)} %broadcast_in_dim.23), calls=%async_computation | async-start | bytes 3145728 | tf_op jit(solution)/shard_map/all_to_all | solution.py:225
  42.5 0.1 collective-permute-start.1
  42.6 0.0 copy-done.8
  42.6 0.0 copy-start.5
  42.7 0.5 collective-permute-start
  43.1 1.4 %collective-permute-done.dest_ref = s32[1,32]{1,0:T(1,128)S(1)} collective-permute-done((s32[1,32]{1,0:T(1,128)S(1)}, s32[1,32]{1,0:T(1,128)S(1)}, u32[]{:S(2)}, u32[]{:S(2)}) %collective-permute-start) | collective-permute-done | bytes 160 | tf_op jit(solution)/shard_map/ppermute | solution.py:228
  44.5 0.0 collective-permute-done.1.blocks_ref
  44.5 1.9 %place_blocks.1 = bf16[64,32,256]{2,1,0:T(8,128)(2,1)} custom-call(s32[1,32]{1,0:T(1,128)S(1)} %collective-permute-done.dest_ref, bf16[32,32,256]{2,1,0:T(8,128)(2,1)S(1)} %collective-permute-done.1.blocks_ref), custom_call_target="tpu_custom_call" | custom-call | bytes 1572864 | tf_op jit(solution)/shard_map/place_blocks/pallas_call | solution.py:181
  46.5 14.8 %all-to-all-done.kv_ref = bf16[16,192,256]{2,1,0:T(8,128)(2,1)S(1)} async-done(((bf16[16,192,256]{2,1,0:T(8,128)(2,1)}), bf16[16,192,256]{2,1,0:T(8,128)(2,1)S(1)}, u32[]{:S(2)}, u32[]{:S(2)}) %all-to-all-start) | async-done | bytes 1572896 | tf_op jit(solution)/shard_map/all_to_all | solution.py:225
  61.3 5.8 %all-to-all-start.1 = ((bf16[64,32,256]{2,1,0:T(8,128)(2,1)}), bf16[64,32,256]{2,1,0:T(8,128)(2,1)S(1)}, u32[]{:S(2)}, u32[]{:S(2)}) async-start(bf16[64,32,256]{2,1,0:T(8,128)(2,1)} %place_blocks.1), calls=%async_computation.1 | async-start | bytes 2097152 | tf_op jit(solution)/shard_map/all_to_all | solution.py:231
  67.0 0.6 reduce_sum.12
  67.7 9.4 %prompt_attention.1 = bf16[192,1024]{1,0:T(8,128)(2,1)} custom-call(s32[1]{0:T(128)} %bitcast.shard_ref, bf16[192,1024]{1,0:T(8,128)(2,1)S(1)} %bitcast.16, bf16[16,192,256]{2,1,0:T(8,128)(2,1)S(1)} %all-to-all-done.kv_ref), custom_call_target="tpu_custom_call" | custom-call | flops 3623878656 | bytes 2359296 | tf_op jit(solution)/shard_map/prompt_attention/pallas_call | solution.py:84
  77.0 3.4 %all-to-all-done.1 = bf16[64,32,256]{2,1,0:T(8,128)(2,1)S(1)} async-done(((bf16[64,32,256]{2,1,0:T(8,128)(2,1)}), bf16[64,32,256]{2,1,0:T(8,128)(2,1)S(1)}, u32[]{:S(2)}, u32[]{:S(2)}) %all-to-all-start.1) | async-done | bytes 1048608 | tf_op jit(solution)/shard_map/all_to_all | solution.py:231
  80.4 1.0 %copy.13 = bf16[1,64,32,256]{3,2,1,0:T(8,128)(2,1)} copy(bf16[1,64,32,256]{3,2,1,0:T(8,128)(2,1)S(1)} %bitcast.17) | data formatting | bytes 2097152
  (12 shorter events, 0.1 us)
Async XLA Ops:
  0.6 17.8 %copy-start = (bf16[1024,512]{1,0:T(8,128)(2,1)S(1)}, bf16[1024,512]{1,0:T(8,128)(2,1)}, u32[]{:S(2)}) copy-start(bf16[1024,512]{1,0:T(8,128)(2,1)} %weight_ref.1) | copy-start | bytes 3145732
  0.6 1.3 %copy-start.1 = (bf16[1,2,1024,256]{3,2,1,0:T(8,128)(2,1)S(1)}, bf16[1,2,1024,256]{3,2,1,0:T(8,128)(2,1)}, u32[]{:S(2)}) copy-start(bf16[1,2,1024,256]{3,2,1,0:T(8,128)(2,1)} %param.15) | copy-start | bytes 3145732
  2.0 0.7 copy-start.2
  2.7 0.7 copy-start.3
  3.3 0.7 copy-start.4
  4.0 31.4 %copy-start.6 = (bf16[1,192,256]{2,1,0:T(8,128)(2,1)S(1)}, bf16[1,192,256]{2,1,0:T(8,128)(2,1)}, u32[]{:S(2)}) copy-start(bf16[1,192,256]{2,1,0:T(8,128)(2,1)} %param.10) | copy-start | bytes 294916
  36.8 5.8 %copy-start.7 = (bf16[1,32,32,256]{3,2,1,0:T(8,128)(2,1)S(1)}, bf16[1,32,32,256]{3,2,1,0:T(8,128)(2,1)}, u32[]{:S(2)}) copy-start(bf16[1,32,32,256]{3,2,1,0:T(8,128)(2,1)} %param.11) | copy-start | bytes 1572868
  36.8 5.9 %copy-start.8 = (s32[1,32,1]{1,2,0:T(1,128)S(1)}, s32[1,32,1]{1,2,0:T(1,128)}, u32[]{:S(2)}) copy-start(s32[1,32,1]{1,2,0:T(1,128)} %param.12) | copy-start | bytes 388
  36.8 24.5 %all-to-all-start = ((bf16[16,192,256]{2,1,0:T(8,128)(2,1)}), bf16[16,192,256]{2,1,0:T(8,128)(2,1)S(1)}, u32[]{:S(2)}, u32[]{:S(2)}) async-start(bf16[16,192,256]{2,1,0:T(8,128)(2,1)} %broadcast_in_dim.23), calls=%async_computation | async-start | bytes 3145728 | tf_op jit(solution)/shard_map/all_to_all | solution.py:225
  42.5 2.0 %collective-permute-start.1 = (bf16[32,32,256]{2,1,0:T(8,128)(2,1)S(1)}, bf16[32,32,256]{2,1,0:T(8,128)(2,1)S(1)}, u32[]{:S(2)}, u32[]{:S(2)}) collective-permute-start(bf16[32,32,256]{2,1,0:T(8,128)(2,1)S(1)} %bitcast.20), channel_id=1, source_target_pairs={{0,128},{128,0},{1,129},{129,1},{2,130},{130,2},{3,131},{131,3},{4... | collective-permute-start | bytes 1572872 | tf_op jit(solution)/shard_map/ppermute | solution.py:229
  42.6 25.0 %copy-start.5 = (bf16[1,192,1024]{2,1,0:T(8,128)(2,1)S(1)}, bf16[1,192,1024]{2,1,0:T(8,128)(2,1)}, u32[]{:S(2)}) copy-start(bf16[1,192,1024]{2,1,0:T(8,128)(2,1)} %param.9) | copy-start | bytes 1179652
  42.7 1.9 %collective-permute-start = (s32[1,32]{1,0:T(1,128)S(1)}, s32[1,32]{1,0:T(1,128)S(1)}, u32[]{:S(2)}, u32[]{:S(2)}) collective-permute-start(s32[1,32]{1,0:T(1,128)S(1)} %bitcast.21), channel_id=1, source_target_pairs={{0,128},{128,0},{1,129},{129,1},{2,130},{130,2},{3,131},{131,3},{4... | collective-permute-start | bytes 392 | tf_op jit(solution)/shard_map/ppermute | solution.py:228
  61.3 19.2 %all-to-all-start.1 = ((bf16[64,32,256]{2,1,0:T(8,128)(2,1)}), bf16[64,32,256]{2,1,0:T(8,128)(2,1)S(1)}, u32[]{:S(2)}, u32[]{:S(2)}) async-start(bf16[64,32,256]{2,1,0:T(8,128)(2,1)} %place_blocks.1), calls=%async_computation.1 | async-start | bytes 2097152 | tf_op jit(solution)/shard_map/all_to_all | solution.py:231

commit v2 on v1

v2 whole, which is shorter than its diff:
```python
import math

import jax
import jax.numpy as jnp
from jax import lax
from jax.experimental import pallas as pl
from jax.experimental.pallas import tpu as pltpu
from jax.sharding import PartitionSpec as P

QUERY_PER_KEY = 8
HEAD_WIDTH = 128
SCORE_SCALE = 1.0 / math.sqrt(HEAD_WIDTH)
EXP2_SCALE = SCORE_SCALE * math.log2(math.e)
LOWEST = -3.0e38
SLOTS = 4
SIDE = 4

NT = (((1,), (1,)), ((), ()))
NN = (((1,), (0,)), ((), ()))


def dot(a, b, dims=NN):
    return lax.dot_general(a, b, dims, preferred_element_type=jnp.float32)


def prompt_kernel(shard_ref, q_ref, *refs):
    near, far, out_ref, keys, val, acc, top = refs[:2], refs[2:4], *refs[4:]
    shard = shard_ref[0]
    my_row, my_col = shard // SIDE, shard % SIDE
    length = q_ref.shape[0]
    half = length // 2
    chunk = SIDE * length
    val[:, HEAD_WIDTH:] = jnp.ones((chunk, HEAD_WIDTH), jnp.bfloat16)

    def step(at, first):
        for col in range(SIDE):
            low = near[at // 2][at % 2 * SIDE + col, :half]
            high = far[col // 2][col % 2 * SIDE + at]
            for base, part in ((0, low), (half, high)):
                place = slice(col * length + base, col * length + base + half)
                keys[place, :] = part[:, :HEAD_WIDTH]
                val[place, :HEAD_WIDTH] = part[:, HEAD_WIDTH:]
        if first:
            spot = lax.broadcasted_iota(jnp.int32, (length, chunk), 1)
            col = spot // length
            key_pos = (my_col ^ (col ^ (col // 2))) * length + spot - col * length
            query_pos = my_col * length + lax.broadcasted_iota(jnp.int32, (length, chunk), 0)
            visible = key_pos <= query_pos
        for head in range(QUERY_PER_KEY):
            rows = pl.ds(head * length, length)
            q = q_ref[:, head * HEAD_WIDTH : (head + 1) * HEAD_WIDTH]
            scores = dot(q, keys[...], NT)
            if first:
                scores = jnp.where(visible, scores, LOWEST)
            peak = jnp.max(scores, axis=1, keepdims=True)
            if not first:
                old = top[rows, :]
                peak = jnp.maximum(old[:, :1], peak)
            weights = jnp.exp2((scores - peak) * EXP2_SCALE).astype(jnp.bfloat16)
            part = dot(weights, val[...])
            if not first:
                part = acc[rows, :] * jnp.exp2((old[:, :1] - peak) * EXP2_SCALE) + part
            acc[rows, :] = part
            top[rows, :] = jnp.broadcast_to(peak, (length, HEAD_WIDTH))

    step(0, True)
    for at in range(1, SIDE):
        pl.when((my_row ^ at ^ (at // 2)) < my_row)(lambda at=at: step(at, False))
    for head in range(QUERY_PER_KEY):
        rows = pl.ds(head * length, length)
        out_ref[:, head * HEAD_WIDTH : (head + 1) * HEAD_WIDTH] = (
            acc[rows, :HEAD_WIDTH] / acc[rows, HEAD_WIDTH:]
        ).astype(jnp.bfloat16)


def prompt_attention(shard, q, near, far):
    length = q.shape[0]
    rows = QUERY_PER_KEY * length
    chunk = SIDE * length
    whole = pl.BlockSpec(memory_space=pltpu.VMEM)
    return pl.pallas_call(
        prompt_kernel,
        out_shape=jax.ShapeDtypeStruct(q.shape, jnp.bfloat16),
        in_specs=[pl.BlockSpec(memory_space=pltpu.SMEM)] + [whole] * 5,
        out_specs=whole,
        scratch_shapes=[
            pltpu.VMEM((chunk, HEAD_WIDTH), jnp.bfloat16),
            pltpu.VMEM((chunk, 2 * HEAD_WIDTH), jnp.bfloat16),
            pltpu.VMEM((rows, 2 * HEAD_WIDTH), jnp.float32),
            pltpu.VMEM((rows, HEAD_WIDTH), jnp.float32),
        ],
        compiler_params=pltpu.CompilerParams(vmem_limit_bytes=24 << 20),
        cost_estimate=pl.CostEstimate(
            flops=6 * rows * 16 * length * HEAD_WIDTH,
            bytes_accessed=2 * (2 * q.size + 16 * length * 2 * HEAD_WIDTH),
            transcendentals=rows * 16 * length,
        ),
        name="prompt_attention",
    )(shard, q, *near, *far)


def first_kernel(len_ref, kv_ref, q_ref, new_ref, cache_ref, near_ref, far_ref, *scratch):
    kv, q_in, new_in, cache, q_rows, fresh, out_rows, packed, sems = scratch
    copies = [
        pltpu.make_async_copy(src, dst, sems.at[i])
        for i, (src, dst) in enumerate(
            ((cache_ref, cache), (q_ref, q_in), (new_ref, new_in), (kv_ref, kv))
        )
    ]
    for copy in copies:
        copy.start()
    requests, steps, _ = q_in.shape
    capacity = cache.shape[1]
    rows = QUERY_PER_KEY * steps
    half = far_ref.shape[0]
    fresh[...] = jnp.zeros_like(fresh)
    for copy in copies[1:]:
        copy.wait()
    near_ref[:half, :] = kv[:half, :]
    far_ref[...] = kv[half:, :]
    copies[0].wait()
    for req in range(requests):
        for head in range(QUERY_PER_KEY):
            q_rows[head * steps : (head + 1) * steps, :] = q_in[
                req, :, head * HEAD_WIDTH : (head + 1) * HEAD_WIDTH
            ].astype(jnp.float32)
        q = q_rows[...].astype(jnp.bfloat16)
        fresh[:steps, :] = new_in[req].astype(jnp.float32)
        new = fresh[...].astype(jnp.bfloat16)
        held = cache[req]
        scores = dot(q, held[:, :HEAD_WIDTH], NT)
        position = lax.broadcasted_iota(jnp.int32, (rows, capacity), 1)
        scores = jnp.where(position < len_ref[0, req], scores, LOWEST)
        new_scores = dot(q, new[:, :HEAD_WIDTH], NT)
        new_pos = lax.broadcasted_iota(jnp.int32, (rows, new.shape[0]), 1)
        step = lax.broadcasted_iota(jnp.int32, (rows, new.shape[0]), 0) % steps
        new_scores = jnp.where(new_pos <= step, new_scores, LOWEST)
        peak = jnp.maximum(
            jnp.max(scores, axis=1, keepdims=True), jnp.max(new_scores, axis=1, keepdims=True)
        )
        weights = jnp.exp2((scores - peak) * EXP2_SCALE)
        new_weights = jnp.exp2((new_scores - peak) * EXP2_SCALE)
        total = jnp.sum(weights, axis=1, keepdims=True) + jnp.sum(new_weights, axis=1, keepdims=True)
        summed = dot(weights.astype(jnp.bfloat16), held[:, HEAD_WIDTH:])
        summed = summed + dot(new_weights.astype(jnp.bfloat16), new[:, HEAD_WIDTH:])
        result = summed / total
        for head in range(QUERY_PER_KEY):
            out_rows[
                req * steps : (req + 1) * steps, head * HEAD_WIDTH : (head + 1) * HEAD_WIDTH
            ] = result[head * steps : (head + 1) * steps, :]
    height, wide = requests * steps, packed.shape[1]
    for piece in range(packed.shape[0] // height):
        packed[piece * height : (piece + 1) * height, :] = out_rows[
            :, piece * wide : (piece + 1) * wide
        ]
    near_ref[half:, :] = packed[...].astype(jnp.bfloat16)


def first_step(lengths, kv, q, new, cache):
    requests, steps, width = q.shape
    half, wide = kv.shape[0] // 2, kv.shape[1]
    height = requests * steps * width // wide
    whole = pl.BlockSpec(memory_space=pltpu.VMEM)
    far_off = pl.BlockSpec(memory_space=pl.ANY)
    return pl.pallas_call(
        first_kernel,
        out_shape=(
            jax.ShapeDtypeStruct((half + height, wide), jnp.bfloat16),
            jax.ShapeDtypeStruct((half, wide), jnp.bfloat16),
        ),
        in_specs=[pl.BlockSpec(memory_space=pltpu.SMEM)] + [far_off] * 4,
        out_specs=(whole, whole),
        scratch_shapes=[
            pltpu.VMEM(kv.shape, jnp.bfloat16),
            pltpu.VMEM(q.shape, jnp.bfloat16),
            pltpu.VMEM(new.shape, jnp.bfloat16),
            pltpu.VMEM(cache.shape, jnp.bfloat16),
            pltpu.VMEM((QUERY_PER_KEY * steps, HEAD_WIDTH), jnp.float32),
            pltpu.VMEM((HEAD_WIDTH, 2 * HEAD_WIDTH), jnp.float32),
            pltpu.VMEM((requests * steps, width), jnp.float32),
            pltpu.VMEM((height, wide), jnp.float32),
            pltpu.SemaphoreType.DMA((4,)),
        ],
        compiler_params=pltpu.CompilerParams(vmem_limit_bytes=60 << 20),
        cost_estimate=pl.CostEstimate(
            flops=4 * q.size * cache.shape[1], bytes_accessed=2 * cache.size, transcendentals=0
        ),
        name="first_step",
    )(lengths, kv, q, new, cache)


def place_kernel(dest_ref, blocks_ref, out_ref, count):
    targets = out_ref.shape[0] // SLOTS
    for target in range(targets):
        count[target] = 0
    out_ref[...] = jnp.zeros_like(out_ref)

    @pl.loop(0, blocks_ref.shape[0])
    def _(block):
        target = dest_ref[0, block]
        rank = count[target]
        count[target] = rank + 1
        slot = jnp.minimum(target * SLOTS + rank, targets * SLOTS - 1)
        out_ref[pl.ds(slot, 1)] = blocks_ref[pl.ds(block, 1)]


def place_blocks(dest, blocks, targets):
    whole = pl.BlockSpec(memory_space=pltpu.VMEM)
    shape = (targets * SLOTS,) + blocks.shape[1:]
    return pl.pallas_call(
        place_kernel,
        out_shape=jax.ShapeDtypeStruct(shape, blocks.dtype),
        in_specs=[pl.BlockSpec(memory_space=pltpu.SMEM), whole],
        out_specs=whole,
        scratch_shapes=[pltpu.SMEM((targets,), jnp.int32)],
        compiler_params=pltpu.CompilerParams(vmem_limit_bytes=16 << 20),
        cost_estimate=pl.CostEstimate(flops=0, bytes_accessed=6 * blocks.size, transcendentals=0),
        name="place_blocks",
    )(dest, blocks)


def project_kernel(place_ref, weight_ref, low_ref, high_ref, out_ref, rows, sums):
    shard, rank = place_ref[0], place_ref[1]
    ranks, count, _ = out_ref.shape
    _, total, wide = low_ref.shape
    pieces = rows.shape[1] // wide
    height = rows.shape[0] // (SIDE * SIDE)
    first = total - pieces * height
    for at in range(SIDE):
        for col in range(SIDE):
            held = (low_ref, high_ref)[at // 2]
            packed = held[at % 2 * SIDE + col, first:].astype(jnp.float32)
            start = ((at ^ (at // 2)) * SIDE + (col ^ (col // 2))) * height
            for piece in range(pieces):
                rows[start : start + height, piece * wide : (piece + 1) * wide] = packed[
                    piece * height : (piece + 1) * height, :
                ]
    sums[...] = dot(rows[...].astype(jnp.bfloat16), weight_ref[...])
    for other in range(ranks):
        pair = (rank ^ other) ^ (shard // 2)
        part = sums[pl.ds(pl.multiple_of(pair * count, count), count), :]
        swapped = jnp.concatenate([part[height:], part[:height]], axis=0)
        out_ref[other] = jnp.where(shard % 2 == 1, swapped, part)


def project(place, weight, low, high, ranks, steps):
    width = weight.shape[1]
    height = SIDE * SIDE * steps
    whole = pl.BlockSpec(memory_space=pltpu.VMEM)
    return pl.pallas_call(
        project_kernel,
        out_shape=jax.ShapeDtypeStruct((ranks, height // ranks, width), jnp.float32),
        in_specs=[pl.BlockSpec(memory_space=pltpu.SMEM)] + [whole] * 3,
        out_specs=whole,
        scratch_shapes=[
            pltpu.VMEM((height, weight.shape[0]), jnp.float32),
            pltpu.VMEM((height, width), jnp.float32),
        ],
        compiler_params=pltpu.CompilerParams(vmem_limit_bytes=16 << 20),
        cost_estimate=pl.CostEstimate(
            flops=2 * height * weight.size, bytes_accessed=2 * weight.size, transcendentals=0
        ),
        name="project",
    )(place, weight, low, high)


def exchange(value, axis, size, other):
    return lax.ppermute(value, axis, [(i, i ^ other) for i in range(size)])


def per_device(
    prompt_q, prompt_kv, sectioned, handoff_dest, dec_q, dec_new, cache, cache_len, output_weight
):
    shards = SIDE * SIDE
    shard = lax.axis_index("row") * SIDE + lax.axis_index("col")
    ranks = lax.axis_size("head")
    place = jnp.stack([shard, lax.axis_index("head")])

    near, far = first_step(cache_len, prompt_kv[0], dec_q[0], dec_new[0], cache[0])
    near, far = near[None], far[None]
    for other, axes in ((1, ("col", "row")), (3, ("col", "row")), (1, ("row", "col"))):
        near = jnp.concatenate([near, exchange(near, axes[0], SIDE, other)])
        far = jnp.concatenate([far, exchange(far, axes[1], SIDE, other)])
    near = [near, exchange(near, "row", SIDE, 3)]
    far = [far, exchange(far, "col", SIDE, 3)]

    other_dest = exchange(handoff_dest.reshape(1, -1), "grp", 2, 1)
    other_blocks = exchange(sectioned[0], "grp", 2, 1)
    outgoing = place_blocks(other_dest, other_blocks, shards)
    near, far, outgoing = lax.optimization_barrier((near, far, outgoing))
    arrived = lax.all_to_all(outgoing, ("row", "col"), 0, 0, tiled=True)

    sums = project(place, output_weight, *near, ranks, dec_q.shape[1] * dec_q.shape[2])
    while sums.shape[0] > 1:
        middle = sums.shape[0] // 2
        sums = sums[:middle] + exchange(sums[middle:], "head", ranks, middle)
    decode_out = sums[0].astype(jnp.bfloat16)
    prompt_attn = prompt_attention(place, prompt_q[0], near, far)
    return (prompt_attn[None], arrived[None], decode_out[None])


def solution(mesh):
    shape = mesh.shape
    grid = jax.sharding.Mesh(
        mesh.devices.reshape(shape["grp"], SIDE, SIDE, shape["head"]), ("grp", "row", "col", "head")
    )
    seq = ("row", "col")
    placed = (
        P("grp", seq, "head"),
        P("grp", seq, "head"),
        P("grp", seq, None, "head"),
        P("grp", seq, None),
        P("grp", seq, None, "head"),
        P("grp", seq, None, "head"),
        P("grp", seq, None, "head"),
        P("grp", seq),
        P("head", seq),
    )
    return jax.shard_map(
        per_device,
        mesh=grid,
        in_specs=placed,
        out_specs=(P("grp", seq, "head"), P("grp", seq, None, "head"), P("grp", "head", seq)),
        check_vma=False,
    )
```

time: 82.3 us -> 65.6 us (0.80)
  blocking collectives: 29.7 us -> 0 us
  starting transfers between devices: 12.1 us -> 26.6 us
  local copies, waits for them, and re-layouts: 5.69 us -> 1.01 us
  Pallas kernels: 12.9 us -> 16.5 us
  other arithmetic: 0.61 us -> 1.68 us
    all_to_all x2 -> x0, blocking collectives: 29.7 us -> none  [the longest x1 16.6 us: per_device(): lax.all_to_all(partial.reshape(ranks, partial.shape[0] // ranks, partial....]
    ppermute x2 -> x13, starting transfers between devices: 0.57 us -> 20.7 us  [exchange(): return lax.ppermute(value, axis, [(i, i ^ other) for i in range(size)])]
    all_to_all x2 -> x1, waiting for transfers between devices: 18.2 us -> 0.01 us  [per_device(): arrived = lax.all_to_all(outgoing, ('row', 'col'), 0, 0, tiled=True)]
    ppermute x2 -> x13, waiting for transfers between devices: 1.4 us -> 18.8 us  [exchange(): return lax.ppermute(value, axis, [(i, i ^ other) for i in range(size)])]
    all_to_all x2 -> x1, starting transfers between devices: 11.6 us -> 5.95 us  [per_device(): arrived = lax.all_to_all(outgoing, ('row', 'col'), 0, 0, tiled=True)]
    unnamed x19 -> x11, local copies, waits for them, and re-layouts: 4.33 us -> 0.99 us
    pallas_call x2, Pallas kernels: 1.64 us -> 4.24 us  [the longest x1 3.38 us: first_step(): pl.pallas_call(first_kernel, out_shape=(jax.ShapeDtypeStruct((half + heig...]
    broadcast_in_dim x2 -> x0, local copies, waits for them, and re-layouts: 1.36 us -> none  [the longest x1 1.32 us: per_device(): spread = jnp.broadcast_to(prompt_kv, (shards,) + prompt_kv.shape[1:])]
  transfers between devices with their start and end apart: 4 -> 14, of which waited for: 3 -> 8; matrix products, arithmetic and copies ran while one was open for 1% -> 3% of each run, Pallas kernels for 14% -> 19%
where the time goes in v2:
time: 65.6 us; the launch traced here: 65.4 us
  starting transfers between devices  26.6 us (41%)
  waiting for transfers between devices  18.8 us (29%)
  Pallas kernels  16.5 us (25%)
  other arithmetic  1.68 us (3%)
  local copies, waits for them, and re-layouts  1.01 us (2%)
  between operations  0.74 us (1%)
    ppermute x13, starting transfers between devices, exchange(): return lax.ppermute(value, axis, [(i, i ^ other) for i in range(size)])  20.7 us
    ppermute x13, waiting for transfers between devices, exchange(): return lax.ppermute(value, axis, [(i, i ^ other) for i in range(size)])  18.8 us
    pallas_call x1, Pallas kernels, prompt_attention(): pl.pallas_call(prompt_kernel, out_shape=jax.ShapeDtypeStruct(q.shape, jnp...  10.3 us
    all_to_all x1, starting transfers between devices, per_device(): arrived = lax.all_to_all(outgoing, ('row', 'col'), 0, 0, tiled=True)  5.95 us
    pallas_call x1, Pallas kernels, first_step(): pl.pallas_call(first_kernel, out_shape=(jax.ShapeDtypeStruct((half + heig...  3.38 us
    pallas_call x1, Pallas kernels, place_blocks(): pl.pallas_call(place_kernel, out_shape=jax.ShapeDtypeStruct(shape, blocks...  1.93 us
  transfers between devices with their start and end apart: 14, of which 8 were waited for; matrix products, arithmetic and copies ran while one was open for 3% of the time, Pallas kernels for 19%

profile of v2, /device:TPU:6, one launch (start us, length us, event | category | flops | bytes accessed | tf_op | source)
XLA Modules:
  0.0 65.4 jit_solution(17041199507065011223)
XLA Ops:
  0.6 3.4 %first_step.1 = (bf16[112,256]{1,0:T(8,128)(2,1)}, bf16[96,256]{1,0:T(8,128)(2,1)}) custom-call(s32[1,2]{1,0:T(1,128)} %len_ref.1, bf16[192,256]{1,0:T(8,128)(2,1)} %bitcast.24, bf16[2,2,1024]{2,1,0:T(2,128)(2,1)} %bitcast.25, bf16[2,2,256]{2,1,0:T(2,128)(2,1)} %bitcast.26, bf16[2,1024,256]{2,1,0:T(8,128)(2,1)} %bitcast.15), custom_call_target="tpu_custom_call" | custom-call | flops 16777216 | bytes 1048576 | tf_op jit(solution)/shard_map/first_step/pallas_call | solution.py:165
  4.0 1.7 %collective-permute-start = (bf16[1,112,256]{2,1,0:T(8,128)(2,1)}, bf16[1,112,256]{2,1,0:T(8,128)(2,1)S(1)}, u32[]{:S(2)}, u32[]{:S(2)}) collective-permute-start(bf16[1,112,256]{2,1,0:T(8,128)(2,1)} %bitcast.16), channel_id=1, source_target_pairs={{0,8},{8,0},{16,24},{24,16},{1,9},{9,1},{17,25},{25,17},{2,10},{10... | collective-permute-start | bytes 172040 | tf_op jit(solution)/shard_map/ppermute | solution.py:268
  5.7 0.8 %collective-permute-start.4 = (bf16[1,96,256]{2,1,0:T(8,128)(2,1)}, bf16[1,96,256]{2,1,0:T(8,128)(2,1)S(1)}, u32[]{:S(2)}, u32[]{:S(2)}) collective-permute-start(bf16[1,96,256]{2,1,0:T(8,128)(2,1)} %bitcast.20), channel_id=1, source_target_pairs={{0,32},{32,0},{64,96},{96,64},{1,33},{33,1},{65,97},{97,65},{2,34}... | collective-permute-start | bytes 147464 | tf_op jit(solution)/shard_map/ppermute | solution.py:268
  6.5 2.0 %collective-permute-done = bf16[1,112,256]{2,1,0:T(8,128)(2,1)S(1)} collective-permute-done((bf16[1,112,256]{2,1,0:T(8,128)(2,1)}, bf16[1,112,256]{2,1,0:T(8,128)(2,1)S(1)}, u32[]{:S(2)}, u32[]{:S(2)}) %collective-permute-start) | collective-permute-done | bytes 57376 | tf_op jit(solution)/shard_map/ppermute | solution.py:268
  8.5 0.8 %pad_maximum_fusion.4 = bf16[2,112,256]{2,1,0:T(8,128)(2,1)S(1)} fusion(bf16[1,112,256]{2,1,0:T(8,128)(2,1)S(1)} %collective-permute-done, bf16[1,112,256]{2,1,0:T(8,128)(2,1)} %bitcast.17), kind=kLoop, calls=%fused_computation.4 | loop fusion | flops 57344 | bytes 229376 | tf_op jit(solution)/shard_map/concatenate | solution.py:282
  9.3 3.1 %collective-permute-start.1 = (bf16[2,112,256]{2,1,0:T(8,128)(2,1)S(1)}, bf16[2,112,256]{2,1,0:T(8,128)(2,1)S(1)}, u32[]{:S(2)}, u32[]{:S(2)}) collective-permute-start(bf16[2,112,256]{2,1,0:T(8,128)(2,1)S(1)} %pad_maximum_fusion.4), channel_id=1, source_target_pairs={{0,24},{8,16},{16,8},{24,0},{1,25},{9,17},{17,9},{25,1},{2,26},{10... | collective-permute-start | bytes 344072 | tf_op jit(solution)/shard_map/ppermute | solution.py:268
  13.0 2.4 %collective-permute-done.1 = bf16[2,112,256]{2,1,0:T(8,128)(2,1)S(1)} collective-permute-done((bf16[2,112,256]{2,1,0:T(8,128)(2,1)S(1)}, bf16[2,112,256]{2,1,0:T(8,128)(2,1)S(1)}, u32[]{:S(2)}, u32[]{:S(2)}) %collective-permute-start.1) | collective-permute-done | bytes 114720 | tf_op jit(solution)/shard_map/ppermute | solution.py:268
  15.5 0.9 %collective-permute-start.2 = (bf16[4,112,256]{2,1,0:T(8,128)(2,1)S(1)}, bf16[4,112,256]{2,1,0:T(8,128)(2,1)S(1)}, u32[]{:S(2)}, u32[]{:S(2)}) collective-permute-start(bf16[4,112,256]{2,1,0:T(8,128)(2,1)S(1)} %pad_maximum_fusion.2), channel_id=1, source_target_pairs={{0,32},{32,0},{64,96},{96,64},{1,33},{33,1},{65,97},{97,65},{2,34}... | collective-permute-start | bytes 688136 | tf_op jit(solution)/shard_map/ppermute | solution.py:268
  16.4 2.0 %collective-permute-done.5 = bf16[2,96,256]{2,1,0:T(8,128)(2,1)S(1)} collective-permute-done((bf16[2,96,256]{2,1,0:T(8,128)(2,1)S(1)}, bf16[2,96,256]{2,1,0:T(8,128)(2,1)S(1)}, u32[]{:S(2)}, u32[]{:S(2)}) %collective-permute-start.5) | collective-permute-done | bytes 98336 | tf_op jit(solution)/shard_map/ppermute | solution.py:268
  18.6 2.9 %collective-permute-done.2 = bf16[4,112,256]{2,1,0:T(8,128)(2,1)S(1)} collective-permute-done((bf16[4,112,256]{2,1,0:T(8,128)(2,1)S(1)}, bf16[4,112,256]{2,1,0:T(8,128)(2,1)S(1)}, u32[]{:S(2)}, u32[]{:S(2)}) %collective-permute-start.2) | collective-permute-done | bytes 229408 | tf_op jit(solution)/shard_map/ppermute | solution.py:268
  21.6 2.3 %collective-permute-start.3 = (bf16[8,112,256]{2,1,0:T(8,128)(2,1)S(1)}, bf16[8,112,256]{2,1,0:T(8,128)(2,1)S(1)}, u32[]{:S(2)}, u32[]{:S(2)}) collective-permute-start(bf16[8,112,256]{2,1,0:T(8,128)(2,1)S(1)} %pad_maximum_fusion.refs_0_.low_ref), channel_id=1, source_target_pairs={{0,96},{32,64},{64,32},{96,0},{1,97},{33,65},{65,33},{97,1},{2,98}... | collective-permute-start | bytes 1376264 | tf_op jit(solution)/shard_map/ppermute | solution.py:268
  24.2 1.1 %collective-permute-start.7 = (bf16[8,96,256]{2,1,0:T(8,128)(2,1)S(1)}, bf16[8,96,256]{2,1,0:T(8,128)(2,1)S(1)}, u32[]{:S(2)}, u32[]{:S(2)}) collective-permute-start(bf16[8,96,256]{2,1,0:T(8,128)(2,1)S(1)} %pad_maximum_fusion.1.refs_2_), channel_id=1, source_target_pairs={{0,24},{8,16},{16,8},{24,0},{1,25},{9,17},{17,9},{25,1},{2,26},{10... | collective-permute-start | bytes 1179656 | tf_op jit(solution)/shard_map/ppermute | solution.py:268
  25.4 1.0 %collective-permute-done.8.dest_ref = s32[1,32]{1,0:T(1,128)S(1)} collective-permute-done((s32[1,32]{1,0:T(1,128)S(1)}, s32[1,32]{1,0:T(1,128)S(1)}, u32[]{:S(2)}, u32[]{:S(2)}) %collective-permute-start.8) | collective-permute-done | bytes 160 | tf_op jit(solution)/shard_map/ppermute | solution.py:268
  26.5 1.9 %place_blocks.1 = bf16[64,32,256]{2,1,0:T(8,128)(2,1)} custom-call(s32[1,32]{1,0:T(1,128)S(1)} %collective-permute-done.8.dest_ref, bf16[32,32,256]{2,1,0:T(8,128)(2,1)S(1)} %collective-permute-done.9.blocks_ref), custom_call_target="tpu_custom_call" | custom-call | bytes 1572864 | tf_op jit(solution)/shard_map/place_blocks/pallas_call | solution.py:210
  28.4 4.9 %collective-permute-done.7.refs_3_ = bf16[8,96,256]{2,1,0:T(8,128)(2,1)S(1)} collective-permute-done((bf16[8,96,256]{2,1,0:T(8,128)(2,1)S(1)}, bf16[8,96,256]{2,1,0:T(8,128)(2,1)S(1)}, u32[]{:S(2)}, u32[]{:S(2)}) %collective-permute-start.7) | collective-permute-done | bytes 393248 | tf_op jit(solution)/shard_map/ppermute | solution.py:268
  33.3 0.9 %project.1 = f32[8,8,512]{2,1,0:T(8,128)S(1)} custom-call(s32[2]{0:T(128)S(1)} %pad_add_fusion.shard_ref.place_ref, bf16[1024,512]{1,0:T(8,128)(2,1)S(1)} %copy-done, bf16[8,112,256]{2,1,0:T(8,128)(2,1)S(1)} %pad_maximum_fusion.refs_0_.low_ref, bf16[8,112,256]{2,1,0:T(8,128)(2,1)S(1)} %collective-permute-done.3.refs_1_.high_ref), custom_call_target="tpu_custom_call" | custom-call | flops 67108864 | bytes 1048576 | tf_op jit(solution)/shard_map/project/pallas_call | solution.py:250
  34.2 7.3 %collective-permute-start.10 = (f32[4,8,512]{2,1,0:T(8,128)S(1)}, f32[4,8,512]{2,1,0:T(8,128)S(1)}, u32[]{:S(2)}, u32[]{:S(2)}) collective-permute-start(f32[4,8,512]{2,1,0:T(8,128)S(1)} %slice.25), channel_id=1, source_target_pairs={{0,4},{1,5},{2,6},{3,7},{4,0},{5,1},{6,2},{7,3},{8,12},{9,13},{10,... | collective-permute-start | bytes 196616 | tf_op jit(solution)/shard_map/ppermute | solution.py:268
  41.4 6.0 %all-to-all-start = ((bf16[64,32,256]{2,1,0:T(8,128)(2,1)}), bf16[64,32,256]{2,1,0:T(8,128)(2,1)S(1)}, u32[]{:S(2)}, u32[]{:S(2)}) async-start(bf16[64,32,256]{2,1,0:T(8,128)(2,1)} %place_blocks.1), calls=%async_computation | async-start | bytes 2097152 | tf_op jit(solution)/shard_map/all_to_all | solution.py:291
  47.5 1.6 %collective-permute-start.11 = (f32[2,8,512]{2,1,0:T(8,128)S(1)}, f32[2,8,512]{2,1,0:T(8,128)S(1)}, u32[]{:S(2)}, u32[]{:S(2)}) collective-permute-start(f32[2,8,512]{2,1,0:T(8,128)S(1)} %slice.27), channel_id=1, source_target_pairs={{0,2},{1,3},{2,0},{3,1},{4,6},{5,7},{6,4},{7,5},{8,10},{9,11},{10,... | collective-permute-start | bytes 98312 | tf_op jit(solution)/shard_map/ppermute | solution.py:268
  49.0 3.3 %collective-permute-done.11 = f32[2,8,512]{2,1,0:T(8,128)S(1)} collective-permute-done((f32[2,8,512]{2,1,0:T(8,128)S(1)}, f32[2,8,512]{2,1,0:T(8,128)S(1)}, u32[]{:S(2)}, u32[]{:S(2)}) %collective-permute-start.11) | collective-permute-done | bytes 32800 | tf_op jit(solution)/shard_map/ppermute | solution.py:268
  52.4 1.1 %collective-permute-start.12 = (f32[1,8,512]{2,1,0:T(8,128)S(1)}, f32[1,8,512]{2,1,0:T(8,128)S(1)}, u32[]{:S(2)}, u32[]{:S(2)}) collective-permute-start(f32[1,8,512]{2,1,0:T(8,128)S(1)} %slice.29), channel_id=1, source_target_pairs={{0,1},{1,0},{2,3},{3,2},{4,5},{5,4},{6,7},{7,6},{8,9},{9,8},{10,11... | collective-permute-start | bytes 49160 | tf_op jit(solution)/shard_map/ppermute | solution.py:268
  53.5 10.3 %prompt_attention.1 = bf16[192,1024]{1,0:T(8,128)(2,1)} custom-call(s32[2]{0:T(128)S(1)} %pad_add_fusion.shard_ref.place_ref, bf16[192,1024]{1,0:T(8,128)(2,1)S(1)} %bitcast.13, bf16[8,112,256]{2,1,0:T(8,128)(2,1)S(1)} %pad_maximum_fusion.refs_0_.low_ref, bf16[8,112,256]{2,1,0:T(8,128)(2,1)S(1)} %collective-permute-done.3.refs_1_.high_ref, ...), custom_call_target="tpu_custom_call" | custom-call | flops 3623878656 | bytes 2359296 | tf_op jit(solution)/shard_map/prompt_attention/pallas_call | solution.py:81
  63.8 0.6 fusion
  64.4 1.0 %copy.13 = bf16[1,64,32,256]{3,2,1,0:T(8,128)(2,1)} copy(bf16[1,64,32,256]{3,2,1,0:T(8,128)(2,1)S(1)} %bitcast.14) | data formatting | bytes 2097152
  (32 shorter events, 1.3 us)
Async XLA Ops:
  4.0 4.5 %collective-permute-start = (bf16[1,112,256]{2,1,0:T(8,128)(2,1)}, bf16[1,112,256]{2,1,0:T(8,128)(2,1)S(1)}, u32[]{:S(2)}, u32[]{:S(2)}) collective-permute-start(bf16[1,112,256]{2,1,0:T(8,128)(2,1)} %bitcast.16), channel_id=1, source_target_pairs={{0,8},{8,0},{16,24},{24,16},{1,9},{9,1},{17,25},{25,17},{2,10},{10... | collective-permute-start | bytes 172040 | tf_op jit(solution)/shard_map/ppermute | solution.py:268
  5.7 6.8 %copy-start.3 = (bf16[96,256]{1,0:T(8,128)(2,1)S(1)}, bf16[96,256]{1,0:T(8,128)(2,1)}, u32[]{:S(2)}) copy-start(bf16[96,256]{1,0:T(8,128)(2,1)} %get-tuple-element.11) | copy-start | bytes 147460
  5.7 6.8 %collective-permute-start.4 = (bf16[1,96,256]{2,1,0:T(8,128)(2,1)}, bf16[1,96,256]{2,1,0:T(8,128)(2,1)S(1)}, u32[]{:S(2)}, u32[]{:S(2)}) collective-permute-start(bf16[1,96,256]{2,1,0:T(8,128)(2,1)} %bitcast.20), channel_id=1, source_target_pairs={{0,32},{32,0},{64,96},{96,64},{1,33},{33,1},{65,97},{97,65},{2,34}... | collective-permute-start | bytes 147464 | tf_op jit(solution)/shard_map/ppermute | solution.py:268
  9.3 6.1 %copy-start.2 = (bf16[112,256]{1,0:T(8,128)(2,1)S(1)}, bf16[112,256]{1,0:T(8,128)(2,1)}, u32[]{:S(2)}) copy-start(bf16[112,256]{1,0:T(8,128)(2,1)} %get-tuple-element.10) | copy-start | bytes 172036
  9.3 6.1 %collective-permute-start.1 = (bf16[2,112,256]{2,1,0:T(8,128)(2,1)S(1)}, bf16[2,112,256]{2,1,0:T(8,128)(2,1)S(1)}, u32[]{:S(2)}, u32[]{:S(2)}) collective-permute-start(bf16[2,112,256]{2,1,0:T(8,128)(2,1)S(1)} %pad_maximum_fusion.4), channel_id=1, source_target_pairs={{0,24},{8,16},{16,8},{24,0},{1,25},{9,17},{17,9},{25,1},{2,26},{10... | collective-permute-start | bytes 344072 | tf_op jit(solution)/shard_map/ppermute | solution.py:268
  12.5 5.9 %collective-permute-start.5 = (bf16[2,96,256]{2,1,0:T(8,128)(2,1)S(1)}, bf16[2,96,256]{2,1,0:T(8,128)(2,1)S(1)}, u32[]{:S(2)}, u32[]{:S(2)}) collective-permute-start(bf16[2,96,256]{2,1,0:T(8,128)(2,1)S(1)} %pad_maximum_fusion.5), channel_id=1, source_target_pairs={{0,96},{32,64},{64,32},{96,0},{1,97},{33,65},{65,33},{97,1},{2,98}... | collective-permute-start | bytes 294920 | tf_op jit(solution)/shard_map/ppermute | solution.py:268
  15.5 6.1 %collective-permute-start.2 = (bf16[4,112,256]{2,1,0:T(8,128)(2,1)S(1)}, bf16[4,112,256]{2,1,0:T(8,128)(2,1)S(1)}, u32[]{:S(2)}, u32[]{:S(2)}) collective-permute-start(bf16[4,112,256]{2,1,0:T(8,128)(2,1)S(1)} %pad_maximum_fusion.2), channel_id=1, source_target_pairs={{0,32},{32,0},{64,96},{96,64},{1,33},{33,1},{65,97},{97,65},{2,34}... | collective-permute-start | bytes 688136 | tf_op jit(solution)/shard_map/ppermute | solution.py:268
  18.4 5.8 %collective-permute-start.6 = (bf16[4,96,256]{2,1,0:T(8,128)(2,1)S(1)}, bf16[4,96,256]{2,1,0:T(8,128)(2,1)S(1)}, u32[]{:S(2)}, u32[]{:S(2)}) collective-permute-start(bf16[4,96,256]{2,1,0:T(8,128)(2,1)S(1)} %pad_maximum_fusion.3), channel_id=1, source_target_pairs={{0,8},{8,0},{16,24},{24,16},{1,9},{9,1},{17,25},{25,17},{2,10},{10... | collective-permute-start | bytes 589832 | tf_op jit(solution)/shard_map/ppermute | solution.py:268
  18.6 7.8 %collective-permute-start.9 = (bf16[32,32,256]{2,1,0:T(8,128)(2,1)}, bf16[32,32,256]{2,1,0:T(8,128)(2,1)S(1)}, u32[]{:S(2)}, u32[]{:S(2)}) collective-permute-start(bf16[32,32,256]{2,1,0:T(8,128)(2,1)} %bitcast.10), channel_id=1, source_target_pairs={{0,128},{128,0},{1,129},{129,1},{2,130},{130,2},{3,131},{131,3},{4... | collective-permute-start | bytes 1572872 | tf_op jit(solution)/shard_map/ppermute | solution.py:268
  21.6 3.8 %copy-start.4 = (s32[1,32,1]{1,2,0:T(1,128)S(1)}, s32[1,32,1]{1,2,0:T(1,128)}, u32[]{:S(2)}) copy-start(s32[1,32,1]{1,2,0:T(1,128)} %param.12) | copy-start | bytes 388
  21.6 11.7 %copy-start = (bf16[1024,512]{1,0:T(8,128)(2,1)S(1)}, bf16[1024,512]{1,0:T(8,128)(2,1)}, u32[]{:S(2)}) copy-start(bf16[1024,512]{1,0:T(8,128)(2,1)} %weight_ref.1) | copy-start | bytes 3145732
  21.6 11.6 %collective-permute-start.3 = (bf16[8,112,256]{2,1,0:T(8,128)(2,1)S(1)}, bf16[8,112,256]{2,1,0:T(8,128)(2,1)S(1)}, u32[]{:S(2)}, u32[]{:S(2)}) collective-permute-start(bf16[8,112,256]{2,1,0:T(8,128)(2,1)S(1)} %pad_maximum_fusion.refs_0_.low_ref), channel_id=1, source_target_pairs={{0,96},{32,64},{64,32},{96,0},{1,97},{33,65},{65,33},{97,1},{2,98}... | collective-permute-start | bytes 1376264 | tf_op jit(solution)/shard_map/ppermute | solution.py:268
  24.2 9.1 %collective-permute-start.7 = (bf16[8,96,256]{2,1,0:T(8,128)(2,1)S(1)}, bf16[8,96,256]{2,1,0:T(8,128)(2,1)S(1)}, u32[]{:S(2)}, u32[]{:S(2)}) collective-permute-start(bf16[8,96,256]{2,1,0:T(8,128)(2,1)S(1)} %pad_maximum_fusion.1.refs_2_), channel_id=1, source_target_pairs={{0,24},{8,16},{16,8},{24,0},{1,25},{9,17},{17,9},{25,1},{2,26},{10... | collective-permute-start | bytes 1179656 | tf_op jit(solution)/shard_map/ppermute | solution.py:268
  25.4 1.1 %collective-permute-start.8 = (s32[1,32]{1,0:T(1,128)S(1)}, s32[1,32]{1,0:T(1,128)S(1)}, u32[]{:S(2)}, u32[]{:S(2)}) collective-permute-start(s32[1,32]{1,0:T(1,128)S(1)} %bitcast.27), channel_id=1, source_target_pairs={{0,128},{128,0},{1,129},{129,1},{2,130},{130,2},{3,131},{131,3},{4... | collective-permute-start | bytes 392 | tf_op jit(solution)/shard_map/ppermute | solution.py:268
  34.2 13.2 %collective-permute-start.10 = (f32[4,8,512]{2,1,0:T(8,128)S(1)}, f32[4,8,512]{2,1,0:T(8,128)S(1)}, u32[]{:S(2)}, u32[]{:S(2)}) collective-permute-start(f32[4,8,512]{2,1,0:T(8,128)S(1)} %slice.25), channel_id=1, source_target_pairs={{0,4},{1,5},{2,6},{3,7},{4,0},{5,1},{6,2},{7,3},{8,12},{9,13},{10,... | collective-permute-start | bytes 196616 | tf_op jit(solution)/shard_map/ppermute | solution.py:268
  41.4 23.0 %all-to-all-start = ((bf16[64,32,256]{2,1,0:T(8,128)(2,1)}), bf16[64,32,256]{2,1,0:T(8,128)(2,1)S(1)}, u32[]{:S(2)}, u32[]{:S(2)}) async-start(bf16[64,32,256]{2,1,0:T(8,128)(2,1)} %place_blocks.1), calls=%async_computation | async-start | bytes 2097152 | tf_op jit(solution)/shard_map/all_to_all | solution.py:291
  47.4 6.1 %copy-start.1 = (bf16[1,192,1024]{2,1,0:T(8,128)(2,1)S(1)}, bf16[1,192,1024]{2,1,0:T(8,128)(2,1)}, u32[]{:S(2)}) copy-start(bf16[1,192,1024]{2,1,0:T(8,128)(2,1)} %param.9) | copy-start | bytes 1179652
  47.5 4.9 %collective-permute-start.11 = (f32[2,8,512]{2,1,0:T(8,128)S(1)}, f32[2,8,512]{2,1,0:T(8,128)S(1)}, u32[]{:S(2)}, u32[]{:S(2)}) collective-permute-start(f32[2,8,512]{2,1,0:T(8,128)S(1)} %slice.27), channel_id=1, source_target_pairs={{0,2},{1,3},{2,0},{3,1},{4,6},{5,7},{6,4},{7,5},{8,10},{9,11},{10,... | collective-permute-start | bytes 98312 | tf_op jit(solution)/shard_map/ppermute | solution.py:268
  52.4 11.4 %collective-permute-start.12 = (f32[1,8,512]{2,1,0:T(8,128)S(1)}, f32[1,8,512]{2,1,0:T(8,128)S(1)}, u32[]{:S(2)}, u32[]{:S(2)}) collective-permute-start(f32[1,8,512]{2,1,0:T(8,128)S(1)} %slice.29), channel_id=1, source_target_pairs={{0,1},{1,0},{2,3},{3,2},{4,5},{5,4},{6,7},{7,6},{8,9},{9,8},{10,11... | collective-permute-start | bytes 49160 | tf_op jit(solution)/shard_map/ppermute | solution.py:268

commit v3 on v2

v3 whole, which is shorter than its diff:
```python
import math
from functools import partial

import jax
import jax.numpy as jnp
from jax import lax
from jax.experimental import pallas as pl
from jax.experimental.pallas import tpu as pltpu
from jax.sharding import PartitionSpec as P

QUERY_PER_KEY = 8
HEAD_WIDTH = 128
SCORE_SCALE = 1.0 / math.sqrt(HEAD_WIDTH)
EXP2_SCALE = SCORE_SCALE * math.log2(math.e)
LOWEST = -3.0e38
SLOTS = 4
SIDE = 4
EARLY = 3
TOP_LANE = HEAD_WIDTH + HEAD_WIDTH // 2

NT = (((1,), (1,)), ((), ()))
NN = (((1,), (0,)), ((), ()))


def dot(a, b, dims=NN):
    return lax.dot_general(a, b, dims, preferred_element_type=jnp.float32)


def gray(index):
    return index ^ (index // 2)


def prompt_kernel(outer, offset, kind, place_ref, q_ref, *refs):
    first, final = kind == "first", kind == "final"
    shard = place_ref[0]
    my_row, my_col = shard // SIDE, shard % SIDE
    if first:
        near_ref, far_ref, state_out, keys, key_cols, val = refs
        anchor_ref = near_ref
    elif final:
        anchor_ref, near_ref, far_ref, state_in, out_ref, keys, key_cols, val = refs[:8]
    else:
        anchor_ref, near_ref, far_ref, state_in, state_out, keys, key_cols, val = refs[:8]
    length = q_ref.shape[0]
    half = length // 2
    if kind in ("next", "final"):
        anchor, near, far, sems = refs[8:]
        copies = [
            pltpu.make_async_copy(anchor_ref.at[0:1, 0:16], anchor, sems.at[0]),
            pltpu.make_async_copy(near_ref.at[offset : offset + SIDE], near, sems.at[1]),
            pltpu.make_async_copy(far_ref.at[offset : offset + SIDE], far, sems.at[2]),
        ]
        for copy in copies:
            copy.start()
        for copy in copies:
            copy.wait()
        anchor_ref, near_ref, far_ref, offset = anchor, near, far, 0

    def run():
        own_key = jnp.broadcast_to(anchor_ref[0, :16, :HEAD_WIDTH][:1], (half, HEAD_WIDTH))
        for at in range(SIDE):
            for side, ref in enumerate((near_ref, far_ref)):
                part = ref[offset + at, :half]
                inner = gray(at)
                row, col = (my_row ^ outer, my_col ^ inner) if side == 0 else (my_row ^ inner, my_col ^ outer)
                seen = row * SIDE + col <= shard
                place = slice((2 * at + side) * half, (2 * at + side + 1) * half)
                keys[place, :] = jnp.where(seen, part[:, :HEAD_WIDTH], own_key)
                val[place, :HEAD_WIDTH] = jnp.where(seen, part[:, HEAD_WIDTH:], jnp.zeros_like(own_key))
                val[place, HEAD_WIDTH:] = jnp.where(seen, jnp.ones_like(own_key), jnp.zeros_like(own_key))
        turned = keys[...].T
        key_cols[:HEAD_WIDTH, :] = turned
        key_cols[HEAD_WIDTH:, :] = turned
        if first:
            masked = -(-length // HEAD_WIDTH) * HEAD_WIDTH
            spot = lax.broadcasted_iota(jnp.int32, (length, masked), 1)
            visible = (spot <= lax.broadcasted_iota(jnp.int32, (length, masked), 0)) | (spot >= length)

        lane = lax.broadcasted_iota(jnp.int32, (length, HEAD_WIDTH), 1)
        for head in range(QUERY_PER_KEY):
            rows = slice(head * length, (head + 1) * length)
            columns = slice(head * HEAD_WIDTH, (head + 1) * HEAD_WIDTH)
            scaled = q_ref[:, columns].astype(jnp.float32) * EXP2_SCALE
            high = scaled.astype(jnp.bfloat16)
            low = (scaled - high.astype(jnp.float32)).astype(jnp.bfloat16)
            scores = dot(jnp.concatenate([high, low], axis=1), key_cols[...])
            if first:
                scores = jnp.concatenate(
                    [jnp.where(visible, scores[:, :masked], LOWEST), scores[:, masked:]], axis=1
                )
            peak = jnp.max(scores, axis=1, keepdims=True)
            if not first:
                old = state_in[rows, TOP_LANE : TOP_LANE + 1]
                peak = jnp.maximum(old, peak)
            weights = jnp.exp2(scores - peak).astype(jnp.bfloat16)
            part = dot(weights, val[...])
            if not first:
                shrink = jnp.exp2(old - peak)
                total = state_in[rows, HEAD_WIDTH:]
                total = jnp.where(lane < TOP_LANE - HEAD_WIDTH, total, 0.0) * shrink + part[:, HEAD_WIDTH:]
                part = state_in[rows, :HEAD_WIDTH] * shrink + part[:, :HEAD_WIDTH]
            else:
                part, total = part[:, :HEAD_WIDTH], part[:, HEAD_WIDTH:]
            if final:
                out_ref[:, columns] = (part / total[:, :1]).astype(jnp.bfloat16)
            else:
                state_out[rows, :HEAD_WIDTH] = part
                state_out[rows, HEAD_WIDTH:] = jnp.where(lane < TOP_LANE - HEAD_WIDTH, total, peak)

    if kind == "ahead":
        pl.when(place_ref[1] < EARLY)(run)
    elif kind == "behind":
        pl.when(place_ref[1] >= EARLY)(run)
    else:
        run()


def prompt_part(place, outer, q, arrays, kind, state=None, offset=0):
    rows = QUERY_PER_KEY * q.shape[0]
    chunk = SIDE * q.shape[0]
    whole = pl.BlockSpec(memory_space=pltpu.VMEM)
    specs, fetched = [whole] * len(arrays), []
    if kind in ("next", "final"):
        arrays, specs = in_hbm(*arrays), [pl.BlockSpec(memory_space=pl.ANY)] * len(arrays)
        part = (SIDE,) + arrays[1].shape[1:]
        fetched = [
            pltpu.VMEM((1, 16, 2 * HEAD_WIDTH), jnp.bfloat16),
            pltpu.VMEM(part, jnp.bfloat16),
            pltpu.VMEM(part, jnp.bfloat16),
            pltpu.SemaphoreType.DMA((3,)),
        ]
    operands = arrays if state is None else (*arrays, state)
    specs = specs if state is None else specs + [whole]
    return pl.pallas_call(
        partial(prompt_kernel, outer, offset, kind),
        out_shape=jax.ShapeDtypeStruct(q.shape, jnp.bfloat16)
        if kind == "final"
        else pltpu.VMEM((rows, 2 * HEAD_WIDTH), jnp.float32),
        in_specs=[pl.BlockSpec(memory_space=pltpu.SMEM), whole] + specs,
        out_specs=whole,
        scratch_shapes=[
            pltpu.VMEM((chunk, HEAD_WIDTH), jnp.bfloat16),
            pltpu.VMEM((2 * HEAD_WIDTH, chunk), jnp.bfloat16),
            pltpu.VMEM((chunk, 2 * HEAD_WIDTH), jnp.bfloat16),
        ]
        + fetched,
        input_output_aliases={} if kind in ("first", "final") else {5: 0},
        compiler_params=pltpu.CompilerParams(vmem_limit_bytes=10 << 20),
        cost_estimate=pl.CostEstimate(
            flops=8 * rows * chunk * HEAD_WIDTH,
            bytes_accessed=4 * chunk * HEAD_WIDTH,
            transcendentals=rows * chunk,
        ),
        name="prompt_part",
    )(place, q, *operands)


def in_hbm(*arrays):
    return [pltpu.with_memory_space_constraint(array, pltpu.HBM) for array in arrays]


def first_kernel(len_hbm, kv_ref, q_ref, new_ref, cache_ref, near_ref, far_ref, *scratch):
    len_ref, kv, q_in, new_in, cache, q_rows, fresh, out_rows, packed, sems = scratch
    copies = [
        pltpu.make_async_copy(src, dst, sems.at[i])
        for i, (src, dst) in enumerate(
            ((cache_ref, cache), (kv_ref, kv), (q_ref, q_in), (new_ref, new_in), (len_hbm, len_ref))
        )
    ]
    for copy in copies:
        copy.start()
    requests, steps, _ = q_in.shape
    capacity = cache.shape[1]
    rows = QUERY_PER_KEY * steps
    half = far_ref.shape[0]
    fresh[...] = jnp.zeros_like(fresh)
    for copy in copies[1:]:
        copy.wait()
    near_ref[:half, :] = kv[:half, :]
    far_ref[...] = kv[half:, :]
    copies[0].wait()
    for req in range(requests):
        for head in range(QUERY_PER_KEY):
            q_rows[head * steps : (head + 1) * steps, :] = q_in[
                req, :, head * HEAD_WIDTH : (head + 1) * HEAD_WIDTH
            ].astype(jnp.float32)
        q = q_rows[...].astype(jnp.bfloat16)
        fresh[:steps, :] = new_in[req].astype(jnp.float32)
        new = fresh[...].astype(jnp.bfloat16)
        held = cache[req]
        scores = dot(q, held[:, :HEAD_WIDTH], NT)
        position = lax.broadcasted_iota(jnp.int32, (rows, capacity), 1)
        scores = jnp.where(position < len_ref[0, req], scores, LOWEST)
        new_scores = dot(q, new[:, :HEAD_WIDTH], NT)
        new_pos = lax.broadcasted_iota(jnp.int32, (rows, new.shape[0]), 1)
        step = lax.broadcasted_iota(jnp.int32, (rows, new.shape[0]), 0) % steps
        new_scores = jnp.where(new_pos <= step, new_scores, LOWEST)
        peak = jnp.maximum(
            jnp.max(scores, axis=1, keepdims=True), jnp.max(new_scores, axis=1, keepdims=True)
        )
        weights = jnp.exp2((scores - peak) * EXP2_SCALE)
        new_weights = jnp.exp2((new_scores - peak) * EXP2_SCALE)
        total = jnp.sum(weights, axis=1, keepdims=True) + jnp.sum(new_weights, axis=1, keepdims=True)
        summed = dot(weights.astype(jnp.bfloat16), held[:, HEAD_WIDTH:])
        summed = summed + dot(new_weights.astype(jnp.bfloat16), new[:, HEAD_WIDTH:])
        result = summed / total
        for head in range(QUERY_PER_KEY):
            out_rows[
                req * steps : (req + 1) * steps, head * HEAD_WIDTH : (head + 1) * HEAD_WIDTH
            ] = result[head * steps : (head + 1) * steps, :]
    height, wide = requests * steps, packed.shape[1]
    for piece in range(packed.shape[0] // height):
        packed[piece * height : (piece + 1) * height, :] = out_rows[
            :, piece * wide : (piece + 1) * wide
        ]
    near_ref[half:, :] = packed[...].astype(jnp.bfloat16)


def first_step(lengths, kv, q, new, cache):
    requests, steps, width = q.shape
    half, wide = kv.shape[0] // 2, kv.shape[1]
    height = requests * steps * width // wide
    whole = pl.BlockSpec(memory_space=pltpu.VMEM)
    far_off = pl.BlockSpec(memory_space=pl.ANY)
    return pl.pallas_call(
        first_kernel,
        out_shape=(
            pltpu.VMEM((half + height, wide), jnp.bfloat16),
            pltpu.VMEM((half, wide), jnp.bfloat16),
        ),
        in_specs=[far_off] * 5,
        out_specs=(whole, whole),
        scratch_shapes=[
            pltpu.SMEM(lengths.shape, jnp.int32),
            pltpu.VMEM(kv.shape, jnp.bfloat16),
            pltpu.VMEM(q.shape, jnp.bfloat16),
            pltpu.VMEM(new.shape, jnp.bfloat16),
            pltpu.VMEM(cache.shape, jnp.bfloat16),
            pltpu.VMEM((QUERY_PER_KEY * steps, HEAD_WIDTH), jnp.float32),
            pltpu.VMEM((HEAD_WIDTH, 2 * HEAD_WIDTH), jnp.float32),
            pltpu.VMEM((requests * steps, width), jnp.float32),
            pltpu.VMEM((height, wide), jnp.float32),
            pltpu.SemaphoreType.DMA((5,)),
        ],
        compiler_params=pltpu.CompilerParams(vmem_limit_bytes=16 << 20),
        cost_estimate=pl.CostEstimate(
            flops=4 * q.size * cache.shape[1], bytes_accessed=2 * cache.size, transcendentals=0
        ),
        name="first_step",
    )(*in_hbm(lengths, kv, q, new, cache))


def place_kernel(dest_hbm, blocks_hbm, out_ref, dest_ref, blocks_ref, count, sems):
    copies = [
        pltpu.make_async_copy(dest_hbm, dest_ref, sems.at[0]),
        pltpu.make_async_copy(blocks_hbm, blocks_ref, sems.at[1]),
    ]
    for copy in copies:
        copy.start()
    targets = out_ref.shape[0] // SLOTS
    for target in range(targets):
        count[target] = 0
    out_ref[...] = jnp.zeros_like(out_ref)
    for copy in copies:
        copy.wait()

    @pl.loop(0, blocks_ref.shape[0])
    def _(block):
        target = dest_ref[0, block]
        rank = count[target]
        count[target] = rank + 1
        slot = jnp.minimum(target * SLOTS + rank, targets * SLOTS - 1)
        out_ref[pl.ds(slot, 1)] = blocks_ref[pl.ds(block, 1)]


def place_blocks(dest, blocks, targets):
    shape = (targets * SLOTS,) + blocks.shape[1:]
    return pl.pallas_call(
        place_kernel,
        out_shape=jax.ShapeDtypeStruct(shape, blocks.dtype),
        in_specs=[pl.BlockSpec(memory_space=pl.ANY)] * 2,
        out_specs=pl.BlockSpec(memory_space=pltpu.VMEM),
        scratch_shapes=[
            pltpu.SMEM(dest.shape, jnp.int32),
            pltpu.VMEM(blocks.shape, blocks.dtype),
            pltpu.SMEM((targets,), jnp.int32),
            pltpu.SemaphoreType.DMA((2,)),
        ],
        compiler_params=pltpu.CompilerParams(vmem_limit_bytes=10 << 20),
        cost_estimate=pl.CostEstimate(flops=0, bytes_accessed=6 * blocks.size, transcendentals=0),
        name="place_blocks",
    )(*in_hbm(dest, blocks))


def project_kernel(place_ref, weight_ref, *refs):
    gathered, kept_ref, sent_ref, rows, sums = refs
    shard, rank = place_ref[0], place_ref[1]
    middle, count, _ = kept_ref.shape
    wide = gathered.shape[2]
    pieces = rows.shape[1] // wide
    height = rows.shape[0] // (SIDE * SIDE)
    for at in range(SIDE):
        for col in range(SIDE):
            packed = gathered[at * SIDE + col].astype(jnp.float32)
            start = (gray(at) * SIDE + gray(col)) * height
            for piece in range(pieces):
                rows[start : start + height, piece * wide : (piece + 1) * wide] = packed[
                    piece * height : (piece + 1) * height, :
                ]
    sums[...] = dot(rows[...].astype(jnp.bfloat16), weight_ref[...])
    for other in range(2 * middle):
        pair = (rank ^ other) ^ (shard // 2)
        part = sums[pl.ds(pl.multiple_of(pair * count, count), count), :]
        swapped = jnp.concatenate([part[height:], part[:height]], axis=0)
        part = jnp.where(shard % 2 == 1, swapped, part)
        if other < middle:
            kept_ref[other] = part
        else:
            sent_ref[other - middle] = part.astype(jnp.bfloat16)


def project(place, weight, gathered, ranks, steps):
    width = weight.shape[1]
    height = SIDE * SIDE * steps
    whole = pl.BlockSpec(memory_space=pltpu.VMEM)
    return pl.pallas_call(
        project_kernel,
        out_shape=(
            jax.ShapeDtypeStruct((ranks // 2, height // ranks, width), jnp.float32),
            jax.ShapeDtypeStruct((ranks // 2, height // ranks, width), jnp.bfloat16),
        ),
        in_specs=[pl.BlockSpec(memory_space=pltpu.SMEM)] + [whole] * 2,
        out_specs=(whole, whole),
        scratch_shapes=[
            pltpu.VMEM((height, weight.shape[0]), jnp.float32),
            pltpu.VMEM((height, width), jnp.float32),
        ],
        compiler_params=pltpu.CompilerParams(vmem_limit_bytes=16 << 20),
        cost_estimate=pl.CostEstimate(
            flops=2 * height * weight.size, bytes_accessed=2 * weight.size, transcendentals=0
        ),
        name="project",
    )(place, weight, gathered)


def exchange(value, axis, size, other):
    return lax.ppermute(value, axis, [(i, i ^ other) for i in range(size)])


def per_device(
    prompt_q, prompt_kv, sectioned, handoff_dest, dec_q, dec_new, cache, cache_len, output_weight
):
    shards = SIDE * SIDE
    shard = lax.axis_index("row") * SIDE + lax.axis_index("col")
    ranks = lax.axis_size("head")
    place = jnp.stack([shard, lax.axis_index("head")])
    q = prompt_q[0]
    half = prompt_kv.shape[1] // 2

    near, far = first_step(cache_len, prompt_kv[0], dec_q[0], dec_new[0], cache[0])
    near, far = near[None], far[None]
    near, far, blocks = lax.optimization_barrier((near, far, sectioned[0]))
    outgoing = place_blocks(handoff_dest.reshape(1, -1), blocks, shards)
    outgoing = exchange(outgoing, "grp", 2, 1)

    near = jnp.concatenate([near, exchange(near, "col", SIDE, 1)])
    far = jnp.concatenate([far, exchange(far, "row", SIDE, 1)])
    near_more, far_more = exchange(near, "col", SIDE, 3), exchange(far, "row", SIDE, 3)
    rows = jnp.concatenate([near[:, half:], near_more[:, half:]])
    near = jnp.concatenate([near[:, :half], near_more[:, :half]])
    far = jnp.concatenate([far, far_more])

    rows = jnp.concatenate([rows, exchange(rows, "row", SIDE, 1)])
    more = exchange(near, "row", SIDE, 1), exchange(far, "col", SIDE, 1)
    near, far, rows = lax.optimization_barrier((near, far, rows))
    rows = jnp.concatenate([rows, exchange(rows, "row", SIDE, 3)])
    state = prompt_part(place, 0, q, (near, far), "first")
    rows, more, state = lax.optimization_barrier((rows, more, state))
    wide = jnp.concatenate([near, more[0]]), jnp.concatenate([far, more[1]])
    last = exchange(wide[0], "row", SIDE, 3), exchange(wide[1], "col", SIDE, 3)

    steps = dec_q.shape[1] * dec_q.shape[2]
    sums, sent = project(place, output_weight, rows, ranks, steps)
    state = prompt_part(place, 1, q, (near, *more), "ahead", state)
    sums, sent, state = lax.optimization_barrier((sums, sent, state))
    sent = exchange(sent, "head", ranks, 4)
    state = prompt_part(place, 1, q, (near, *more), "behind", state)
    sent, last, state, outgoing = lax.optimization_barrier((sent, last, state, outgoing))
    arrived = lax.all_to_all(outgoing, ("row", "col"), 0, 0, tiled=True)

    sums = sums + sent.astype(jnp.float32)
    sums, state = lax.optimization_barrier((sums, state))
    sent = exchange(sums[2:], "head", ranks, 2)
    state = prompt_part(place, 3, q, (near, *last), "next", state)
    sent, state = lax.optimization_barrier((sent, state))
    sums = sums[:2] + sent
    sent = exchange(sums[1:], "head", ranks, 1)
    prompt_attn = prompt_part(place, 2, q, (near, *last), "final", state, offset=SIDE)
    sent, prompt_attn = lax.optimization_barrier((sent, prompt_attn))
    decode_out = (sums[0] + sent[0]).astype(jnp.bfloat16)
    return (prompt_attn[None], arrived[None], decode_out[None])


def solution(mesh):
    shape = mesh.shape
    grid = jax.sharding.Mesh(
        mesh.devices.reshape(shape["grp"], SIDE, SIDE, shape["head"]), ("grp", "row", "col", "head")
    )
    seq = ("row", "col")
    placed = (
        P("grp", seq, "head"),
        P("grp", seq, "head"),
        P("grp", seq, None, "head"),
        P("grp", seq, None),
        P("grp", seq, None, "head"),
        P("grp", seq, None, "head"),
        P("grp", seq, None, "head"),
        P("grp", seq),
        P("head", seq),
    )
    return jax.shard_map(
        per_device,
        mesh=grid,
        in_specs=placed,
        out_specs=(P("grp", seq, "head"), P("grp", seq, None, "head"), P("grp", "head", seq)),
        check_vma=False,
    )
```

time: 65.6 us -> 61.6 us (0.939)
  waiting for transfers between devices: 18.8 us -> 10.1 us
  Pallas kernels: 16.5 us -> 19.7 us
  starting transfers between devices: 26.6 us -> 28.7 us
  other arithmetic: 1.68 us -> 0.83 us
    ppermute x13 -> x14, waiting for transfers between devices: 18.8 us -> 10.1 us  [exchange(): return lax.ppermute(value, axis, [(i, i ^ other) for i in range(size)])]
    pallas_call x3 -> x7, Pallas kernels: 14.6 us -> 18.3 us  [the longest x5 15.3 us: prompt_part(): pl.pallas_call(partial(prompt_kernel, outer, offset, kind), out_shape=jax...]
    ppermute x13 -> x14, starting transfers between devices: 20.7 us -> 23.6 us  [exchange(): return lax.ppermute(value, axis, [(i, i ^ other) for i in range(size)])]
    all_to_all x1, starting transfers between devices: 5.95 us -> 5.04 us  [per_device(): arrived = lax.all_to_all(outgoing, ('row', 'col'), 0, 0, tiled=True)]
    concatenate x6 -> x7, other arithmetic: 0.98 us -> 0.13 us  [the longest x2 0.07 us: per_device(): wide = (jnp.concatenate([near, more[0]]), jnp.concatenate([far, more[1]]))]
  transfers between devices with their start and end apart: 14 -> 15, of which waited for: 8 -> 6; matrix products, arithmetic and copies ran while one was open for 3% -> 1% of each run, Pallas kernels for 19% -> 29%
where the time goes in v3:
time: 61.6 us; the launch traced here: 61.2 us
  starting transfers between devices  28.7 us (47%)
  Pallas kernels  19.7 us (32%)
  waiting for transfers between devices  10.1 us (16%)
  local copies, waits for them, and re-layouts  1.04 us (2%)
  between operations  0.87 us (1%)
  other arithmetic  0.83 us (1%)
    ppermute x14, starting transfers between devices, exchange(): return lax.ppermute(value, axis, [(i, i ^ other) for i in range(size)])  23.6 us
    pallas_call x5, Pallas kernels, prompt_part(): pl.pallas_call(partial(prompt_kernel, outer, offset, kind), out_shape=jax...  15.3 us
    ppermute x14, waiting for transfers between devices, exchange(): return lax.ppermute(value, axis, [(i, i ^ other) for i in range(size)])  10.1 us
    all_to_all x1, starting transfers between devices, per_device(): arrived = lax.all_to_all(outgoing, ('row', 'col'), 0, 0, tiled=True)  5.04 us
    pallas_call x1, Pallas kernels, first_step(): pl.pallas_call(first_kernel, out_shape=(pltpu.VMEM((half + height, wide),...  2.09 us
    pallas_call x1, Pallas kernels, place_blocks(): pl.pallas_call(place_kernel, out_shape=jax.ShapeDtypeStruct(shape, blocks...  1.42 us
  transfers between devices with their start and end apart: 15, of which 6 were waited for; matrix products, arithmetic and copies ran while one was open for 1% of the time, Pallas kernels for 29%

profile of v3, /device:TPU:6, one launch (start us, length us, event | category | flops | bytes accessed | tf_op | source)
XLA Modules:
  0.0 61.2 jit_solution(5270425468749817471)
XLA Ops:
  0.6 2.1 %first_step.1 = (bf16[112,256]{1,0:T(8,128)(2,1)S(1)}, bf16[96,256]{1,0:T(8,128)(2,1)S(1)}) custom-call(s32[1,2]{1,0:T(1,128)} %len_hbm.1, bf16[192,256]{1,0:T(8,128)(2,1)} %bitcast.26, bf16[2,2,1024]{2,1,0:T(2,128)(2,1)} %bitcast.27, bf16[2,2,256]{2,1,0:T(2,128)(2,1)} %bitcast.28, bf16[2,1024,256]{2,1,0:T(8,128)(2,1)} %bitcast.24), custom_call_target="tpu_custom_call" | custom-call | flops 16777216 | bytes 1048576 | tf_op jit(solution)/shard_map/first_step/pallas_call | solution.py:225
  2.7 1.7 %collective-permute-start = (bf16[1,112,256]{2,1,0:T(8,128)(2,1)S(1)}, bf16[1,112,256]{2,1,0:T(8,128)(2,1)S(1)}, u32[]{:S(2)}, u32[]{:S(2)}) collective-permute-start(bf16[1,112,256]{2,1,0:T(8,128)(2,1)S(1)} %bitcast.21), channel_id=1, source_target_pairs={{0,8},{8,0},{16,24},{24,16},{1,9},{9,1},{17,25},{25,17},{2,10},{10... | collective-permute-start | bytes 172040 | tf_op jit(solution)/shard_map/ppermute | solution.py:347
  4.4 0.8 %collective-permute-start.2 = (bf16[1,96,256]{2,1,0:T(8,128)(2,1)S(1)}, bf16[1,96,256]{2,1,0:T(8,128)(2,1)S(1)}, u32[]{:S(2)}, u32[]{:S(2)}) collective-permute-start(bf16[1,96,256]{2,1,0:T(8,128)(2,1)S(1)} %bitcast.18), channel_id=1, source_target_pairs={{0,32},{32,0},{64,96},{96,64},{1,33},{33,1},{65,97},{97,65},{2,34}... | collective-permute-start | bytes 147464 | tf_op jit(solution)/shard_map/ppermute | solution.py:347
  5.2 1.4 %place_blocks.1 = bf16[64,32,256]{2,1,0:T(8,128)(2,1)S(1)} custom-call(s32[1,32]{1,0:T(1,128)} %bitcast.29, bf16[32,32,256]{2,1,0:T(8,128)(2,1)} %bitcast.25), custom_call_target="tpu_custom_call" | custom-call | bytes 1572864 | tf_op jit(solution)/shard_map/place_blocks/pallas_call | solution.py:278
  6.9 1.6 %collective-permute-done.2 = bf16[1,96,256]{2,1,0:T(8,128)(2,1)S(1)} collective-permute-done((bf16[1,96,256]{2,1,0:T(8,128)(2,1)S(1)}, bf16[1,96,256]{2,1,0:T(8,128)(2,1)S(1)}, u32[]{:S(2)}, u32[]{:S(2)}) %collective-permute-start.2) | collective-permute-done | bytes 49184 | tf_op jit(solution)/shard_map/ppermute | solution.py:347
  8.5 0.8 %collective-permute-start.3 = (bf16[2,96,256]{2,1,0:T(8,128)(2,1)S(1)}, bf16[2,96,256]{2,1,0:T(8,128)(2,1)S(1)}, u32[]{:S(2)}, u32[]{:S(2)}) collective-permute-start(bf16[2,96,256]{2,1,0:T(8,128)(2,1)S(1)} %pad_maximum_fusion.4), channel_id=1, source_target_pairs={{0,96},{32,64},{64,32},{96,0},{1,97},{33,65},{65,33},{97,1},{2,98}... | collective-permute-start | bytes 294920 | tf_op jit(solution)/shard_map/ppermute | solution.py:347
  9.3 2.0 %collective-permute-start.1 = (bf16[2,112,256]{2,1,0:T(8,128)(2,1)S(1)}, bf16[2,112,256]{2,1,0:T(8,128)(2,1)S(1)}, u32[]{:S(2)}, u32[]{:S(2)}) collective-permute-start(bf16[2,112,256]{2,1,0:T(8,128)(2,1)S(1)} %constant_dynamic-update-slice_fusion), channel_id=1, source_target_pairs={{0,24},{8,16},{16,8},{24,0},{1,25},{9,17},{17,9},{25,1},{2,26},{10... | collective-permute-start | bytes 344072 | tf_op jit(solution)/shard_map/ppermute | solution.py:347
  11.4 3.0 %collective-permute-done.3 = bf16[2,96,256]{2,1,0:T(8,128)(2,1)S(1)} collective-permute-done((bf16[2,96,256]{2,1,0:T(8,128)(2,1)S(1)}, bf16[2,96,256]{2,1,0:T(8,128)(2,1)S(1)}, u32[]{:S(2)}, u32[]{:S(2)}) %collective-permute-start.3) | collective-permute-done | bytes 98336 | tf_op jit(solution)/shard_map/ppermute | solution.py:347
  16.2 1.5 %collective-permute-start.6 = (bf16[4,96,256]{2,1,0:T(8,128)(2,1)S(1)}, bf16[4,96,256]{2,1,0:T(8,128)(2,1)S(1)}, u32[]{:S(2)}, u32[]{:S(2)}) collective-permute-start(bf16[4,96,256]{2,1,0:T(8,128)(2,1)S(1)} %pad_maximum_fusion.2.refs_0_), channel_id=1, source_target_pairs={{0,32},{32,0},{64,96},{96,64},{1,33},{33,1},{65,97},{97,65},{2,34}... | collective-permute-start | bytes 589832 | tf_op jit(solution)/shard_map/ppermute | solution.py:347
  17.7 1.8 %collective-permute-done.4 = bf16[4,16,256]{2,1,0:T(8,128)(2,1)S(1)} collective-permute-done((bf16[4,16,256]{2,1,0:T(8,128)(2,1)S(1)}, bf16[4,16,256]{2,1,0:T(8,128)(2,1)S(1)}, u32[]{:S(2)}, u32[]{:S(2)}) %collective-permute-start.4) | collective-permute-done | bytes 32800 | tf_op jit(solution)/shard_map/ppermute | solution.py:347
  19.5 2.6 %collective-permute-start.5 = (bf16[8,16,256]{2,1,0:T(8,128)(2,1)S(1)}, bf16[8,16,256]{2,1,0:T(8,128)(2,1)S(1)}, u32[]{:S(2)}, u32[]{:S(2)}) collective-permute-start(bf16[8,16,256]{2,1,0:T(8,128)(2,1)S(1)} %pad_maximum_fusion.5), channel_id=1, source_target_pairs={{0,96},{32,64},{64,32},{96,0},{1,97},{33,65},{65,33},{97,1},{2,98}... | collective-permute-start | bytes 196616 | tf_op jit(solution)/shard_map/ppermute | solution.py:347
  22.0 2.4 %prompt_part.5.refs_3_ = f32[1536,256]{1,0:T(8,128)S(1)} custom-call(s32[2]{0:T(128)S(1)} %pad_add_fusion.place_ref, bf16[192,1024]{1,0:T(8,128)(2,1)S(1)} %bitcast.13, bf16[4,96,256]{2,1,0:T(8,128)(2,1)S(1)} %pad_maximum_fusion.2.refs_0_, bf16[4,96,256]{2,1,0:T(8,128)(2,1)S(1)} %constant_dynamic-update-slice_fusion.2.refs_1_), custom_call_target="tpu_custom_call" | custom-call | flops 1207959552 | bytes 393216 | tf_op jit(solution)/shard_map/prompt_part/pallas_call | solution.py:134
  25.1 2.6 %collective-permute-start.10 = (bf16[8,96,256]{2,1,0:T(8,128)(2,1)S(1)}, bf16[8,96,256]{2,1,0:T(8,128)(2,1)}, u32[]{:S(2)}, u32[]{:S(2)}) collective-permute-start(bf16[8,96,256]{2,1,0:T(8,128)(2,1)S(1)} %pad_maximum_fusion.1), channel_id=1, source_target_pairs={{0,24},{8,16},{16,8},{24,0},{1,25},{9,17},{17,9},{25,1},{2,26},{10... | collective-permute-start | bytes 1179656 | tf_op jit(solution)/shard_map/ppermute | solution.py:347
  27.8 2.2 %collective-permute-start.9 = (bf16[8,96,256]{2,1,0:T(8,128)(2,1)S(1)}, bf16[8,96,256]{2,1,0:T(8,128)(2,1)}, u32[]{:S(2)}, u32[]{:S(2)}) collective-permute-start(bf16[8,96,256]{2,1,0:T(8,128)(2,1)S(1)} %pad_maximum_fusion), channel_id=1, source_target_pairs={{0,96},{32,64},{64,32},{96,0},{1,97},{33,65},{65,33},{97,1},{2,98}... | collective-permute-start | bytes 1179656 | tf_op jit(solution)/shard_map/ppermute | solution.py:347
  30.0 0.9 %project.1 = (f32[4,8,512]{2,1,0:T(8,128)S(1)}, bf16[4,8,512]{2,1,0:T(8,128)(2,1)S(1)}) custom-call(s32[2]{0:T(128)S(1)} %pad_add_fusion.place_ref, bf16[1024,512]{1,0:T(8,128)(2,1)S(1)} %copy-done.1, bf16[16,16,256]{2,1,0:T(8,128)(2,1)S(1)} %pad_maximum_fusion.3.refs_0_), custom_call_target="tpu_custom_call" | custom-call | flops 67108864 | bytes 1048576 | tf_op jit(solution)/shard_map/project/pallas_call | solution.py:326
  30.9 3.3 %prompt_part.6.refs_3_ = f32[1536,256]{1,0:T(8,128)S(1)} custom-call(s32[2]{0:T(128)S(1)} %pad_add_fusion.place_ref, bf16[192,1024]{1,0:T(8,128)(2,1)S(1)} %bitcast.14, bf16[4,96,256]{2,1,0:T(8,128)(2,1)S(1)} %pad_maximum_fusion.2.refs_0_, bf16[4,96,256]{2,1,0:T(8,128)(2,1)S(1)} %collective-permute-done.6.refs_1_, ...), custom_call_target="tpu_custom_call", output_to_operand_aliasing={{}: (5, {})} | custom-call | flops 1207959552 | bytes 393216 | tf_op jit(solution)/shard_map/prompt_part/pallas_call | solution.py:134
  34.1 4.6 %collective-permute-start.8 = (bf16[4,8,512]{2,1,0:T(8,128)(2,1)S(1)}, bf16[4,8,512]{2,1,0:T(8,128)(2,1)S(1)}, u32[]{:S(2)}, u32[]{:S(2)}) collective-permute-start(bf16[4,8,512]{2,1,0:T(8,128)(2,1)S(1)} %get-tuple-element.45), channel_id=1, source_target_pairs={{0,4},{1,5},{2,6},{3,7},{4,0},{5,1},{6,2},{7,3},{8,12},{9,13},{10,... | collective-permute-start | bytes 98312 | tf_op jit(solution)/shard_map/ppermute | solution.py:347
  38.7 0.7 %prompt_part.7.refs_3_ = f32[1536,256]{1,0:T(8,128)S(1)} custom-call(s32[2]{0:T(128)S(1)} %pad_add_fusion.place_ref, bf16[192,1024]{1,0:T(8,128)(2,1)S(1)} %bitcast.15, bf16[4,96,256]{2,1,0:T(8,128)(2,1)S(1)} %pad_maximum_fusion.2.refs_0_, bf16[4,96,256]{2,1,0:T(8,128)(2,1)S(1)} %collective-permute-done.6.refs_1_, ...), custom_call_target="tpu_custom_call", output_to_operand_aliasing={{}: (5, {})} | custom-call | flops 1207959552 | bytes 393216 | tf_op jit(solution)/shard_map/prompt_part/pallas_call | solution.py:134
  39.4 2.6 %collective-permute-done.8 = bf16[4,8,512]{2,1,0:T(8,128)(2,1)S(1)} collective-permute-done((bf16[4,8,512]{2,1,0:T(8,128)(2,1)S(1)}, bf16[4,8,512]{2,1,0:T(8,128)(2,1)S(1)}, u32[]{:S(2)}, u32[]{:S(2)}) %collective-permute-start.8) | collective-permute-done | bytes 32800 | tf_op jit(solution)/shard_map/ppermute | solution.py:347
  42.1 5.0 %all-to-all-start = ((bf16[64,32,256]{2,1,0:T(8,128)(2,1)}), bf16[64,32,256]{2,1,0:T(8,128)(2,1)S(1)}, u32[]{:S(2)}, u32[]{:S(2)}) async-start(bf16[64,32,256]{2,1,0:T(8,128)(2,1)} %collective-permute-done.11), calls=%async_computation | async-start | bytes 2097152 | tf_op jit(solution)/shard_map/all_to_all | solution.py:389
  47.1 3.4 %collective-permute-start.12 = (f32[2,8,512]{2,1,0:T(8,128)S(1)}, f32[2,8,512]{2,1,0:T(8,128)S(1)}, u32[]{:S(2)}, u32[]{:S(2)}) collective-permute-start(f32[2,8,512]{2,1,0:T(8,128)S(1)} %slice.29), channel_id=1, source_target_pairs={{0,2},{1,3},{2,0},{3,1},{4,6},{5,7},{6,4},{7,5},{8,10},{9,11},{10,... | collective-permute-start | bytes 98312 | tf_op jit(solution)/shard_map/ppermute | solution.py:347
  50.5 4.3 %prompt_part.8.refs_3_ = f32[1536,256]{1,0:T(8,128)S(1)} custom-call(s32[2]{0:T(128)S(1)} %pad_add_fusion.place_ref, bf16[192,1024]{1,0:T(8,128)(2,1)S(1)} %bitcast.16, bf16[4,96,256]{2,1,0:T(8,128)(2,1)} %copy-done, bf16[8,96,256]{2,1,0:T(8,128)(2,1)} %collective-permute-done.9.refs_1_, ...), custom_call_target="tpu_custom_call", output_to_operand_aliasing={{}: (5, {})} | custom-call | flops 1207959552 | bytes 393216 | tf_op jit(solution)/shard_map/prompt_part/pallas_call | solution.py:134
  54.9 4.6 %prompt_part.9 = bf16[192,1024]{1,0:T(8,128)(2,1)} custom-call(s32[2]{0:T(128)S(1)} %pad_add_fusion.place_ref, bf16[192,1024]{1,0:T(8,128)(2,1)S(1)} %bitcast.17, bf16[4,96,256]{2,1,0:T(8,128)(2,1)} %copy-done, bf16[8,96,256]{2,1,0:T(8,128)(2,1)} %collective-permute-done.9.refs_1_, bf16[8,96,256]{2,1,0:T(8,128)(2,1)} %collective-permute-done.10.refs_2_, ...), custom_call_target="tpu_custom_call" | custom-call | flops 1207959552 | bytes 393216 | tf_op jit(solution)/shard_map/prompt_part/pallas_call | solution.py:134
  60.2 1.0 %copy.22 = bf16[1,64,32,256]{3,2,1,0:T(8,128)(2,1)} copy(bf16[1,64,32,256]{3,2,1,0:T(8,128)(2,1)S(1)} %bitcast.23) | data formatting | bytes 2097152
  (43 shorter events, 3.4 us)
Async XLA Ops:
  2.7 6.6 %collective-permute-start = (bf16[1,112,256]{2,1,0:T(8,128)(2,1)S(1)}, bf16[1,112,256]{2,1,0:T(8,128)(2,1)S(1)}, u32[]{:S(2)}, u32[]{:S(2)}) collective-permute-start(bf16[1,112,256]{2,1,0:T(8,128)(2,1)S(1)} %bitcast.21), channel_id=1, source_target_pairs={{0,8},{8,0},{16,24},{24,16},{1,9},{9,1},{17,25},{25,17},{2,10},{10... | collective-permute-start | bytes 172040 | tf_op jit(solution)/shard_map/ppermute | solution.py:347
  4.4 4.1 %collective-permute-start.2 = (bf16[1,96,256]{2,1,0:T(8,128)(2,1)S(1)}, bf16[1,96,256]{2,1,0:T(8,128)(2,1)S(1)}, u32[]{:S(2)}, u32[]{:S(2)}) collective-permute-start(bf16[1,96,256]{2,1,0:T(8,128)(2,1)S(1)} %bitcast.18), channel_id=1, source_target_pairs={{0,32},{32,0},{64,96},{96,64},{1,33},{33,1},{65,97},{97,65},{2,34}... | collective-permute-start | bytes 147464 | tf_op jit(solution)/shard_map/ppermute | solution.py:347
  5.2 16.8 %copy-start.2 = (bf16[1,192,1024]{2,1,0:T(8,128)(2,1)S(1)}, bf16[1,192,1024]{2,1,0:T(8,128)(2,1)}, u32[]{:S(2)}) copy-start(bf16[1,192,1024]{2,1,0:T(8,128)(2,1)} %param.9) | copy-start | bytes 1179652
  6.7 35.4 %collective-permute-start.11 = (bf16[64,32,256]{2,1,0:T(8,128)(2,1)S(1)}, bf16[64,32,256]{2,1,0:T(8,128)(2,1)}, u32[]{:S(2)}, u32[]{:S(2)}) collective-permute-start(bf16[64,32,256]{2,1,0:T(8,128)(2,1)S(1)} %place_blocks.1), channel_id=1, source_target_pairs={{0,128},{128,0},{1,129},{129,1},{2,130},{130,2},{3,131},{131,3},{4... | collective-permute-start | bytes 3145736 | tf_op jit(solution)/shard_map/ppermute | solution.py:347
  8.5 5.9 %collective-permute-start.3 = (bf16[2,96,256]{2,1,0:T(8,128)(2,1)S(1)}, bf16[2,96,256]{2,1,0:T(8,128)(2,1)S(1)}, u32[]{:S(2)}, u32[]{:S(2)}) collective-permute-start(bf16[2,96,256]{2,1,0:T(8,128)(2,1)S(1)} %pad_maximum_fusion.4), channel_id=1, source_target_pairs={{0,96},{32,64},{64,32},{96,0},{1,97},{33,65},{65,33},{97,1},{2,98}... | collective-permute-start | bytes 294920 | tf_op jit(solution)/shard_map/ppermute | solution.py:347
  9.3 6.1 %collective-permute-start.1 = (bf16[2,112,256]{2,1,0:T(8,128)(2,1)S(1)}, bf16[2,112,256]{2,1,0:T(8,128)(2,1)S(1)}, u32[]{:S(2)}, u32[]{:S(2)}) collective-permute-start(bf16[2,112,256]{2,1,0:T(8,128)(2,1)S(1)} %constant_dynamic-update-slice_fusion), channel_id=1, source_target_pairs={{0,24},{8,16},{16,8},{24,0},{1,25},{9,17},{17,9},{25,1},{2,26},{10... | collective-permute-start | bytes 344072 | tf_op jit(solution)/shard_map/ppermute | solution.py:347
  14.4 10.6 %collective-permute-start.7 = (bf16[4,96,256]{2,1,0:T(8,128)(2,1)S(1)}, bf16[4,96,256]{2,1,0:T(8,128)(2,1)S(1)}, u32[]{:S(2)}, u32[]{:S(2)}) collective-permute-start(bf16[4,96,256]{2,1,0:T(8,128)(2,1)S(1)} %constant_dynamic-update-slice_fusion.2.refs_1_), channel_id=1, source_target_pairs={{0,8},{8,0},{16,24},{24,16},{1,9},{9,1},{17,25},{25,17},{2,10},{10... | collective-permute-start | bytes 589832 | tf_op jit(solution)/shard_map/ppermute | solution.py:347
  15.4 4.0 %collective-permute-start.4 = (bf16[4,16,256]{2,1,0:T(8,128)(2,1)S(1)}, bf16[4,16,256]{2,1,0:T(8,128)(2,1)S(1)}, u32[]{:S(2)}, u32[]{:S(2)}) collective-permute-start(bf16[4,16,256]{2,1,0:T(8,128)(2,1)S(1)} %pad_maximum_fusion.6), channel_id=1, source_target_pairs={{0,32},{32,0},{64,96},{96,64},{1,33},{33,1},{65,97},{97,65},{2,34}... | collective-permute-start | bytes 98312 | tf_op jit(solution)/shard_map/ppermute | solution.py:347
  16.2 22.5 %copy-start = (bf16[4,96,256]{2,1,0:T(8,128)(2,1)}, bf16[4,96,256]{2,1,0:T(8,128)(2,1)S(1)}, u32[]{:S(2)}) copy-start(bf16[4,96,256]{2,1,0:T(8,128)(2,1)S(1)} %pad_maximum_fusion.2.refs_0_) | copy-start | bytes 589828
  16.2 8.9 %collective-permute-start.6 = (bf16[4,96,256]{2,1,0:T(8,128)(2,1)S(1)}, bf16[4,96,256]{2,1,0:T(8,128)(2,1)S(1)}, u32[]{:S(2)}, u32[]{:S(2)}) collective-permute-start(bf16[4,96,256]{2,1,0:T(8,128)(2,1)S(1)} %pad_maximum_fusion.2.refs_0_), channel_id=1, source_target_pairs={{0,32},{32,0},{64,96},{96,64},{1,33},{33,1},{65,97},{97,65},{2,34}... | collective-permute-start | bytes 589832 | tf_op jit(solution)/shard_map/ppermute | solution.py:347
  19.5 5.6 %collective-permute-start.5 = (bf16[8,16,256]{2,1,0:T(8,128)(2,1)S(1)}, bf16[8,16,256]{2,1,0:T(8,128)(2,1)S(1)}, u32[]{:S(2)}, u32[]{:S(2)}) collective-permute-start(bf16[8,16,256]{2,1,0:T(8,128)(2,1)S(1)} %pad_maximum_fusion.5), channel_id=1, source_target_pairs={{0,96},{32,64},{64,32},{96,0},{1,97},{33,65},{65,33},{97,1},{2,98}... | collective-permute-start | bytes 196616 | tf_op jit(solution)/shard_map/ppermute | solution.py:347
  24.4 5.6 %copy-start.1 = (bf16[1024,512]{1,0:T(8,128)(2,1)S(1)}, bf16[1024,512]{1,0:T(8,128)(2,1)}, u32[]{:S(2)}) copy-start(bf16[1024,512]{1,0:T(8,128)(2,1)} %weight_ref.1) | copy-start | bytes 3145732
  25.1 16.9 %collective-permute-start.10 = (bf16[8,96,256]{2,1,0:T(8,128)(2,1)S(1)}, bf16[8,96,256]{2,1,0:T(8,128)(2,1)}, u32[]{:S(2)}, u32[]{:S(2)}) collective-permute-start(bf16[8,96,256]{2,1,0:T(8,128)(2,1)S(1)} %pad_maximum_fusion.1), channel_id=1, source_target_pairs={{0,24},{8,16},{16,8},{24,0},{1,25},{9,17},{17,9},{25,1},{2,26},{10... | collective-permute-start | bytes 1179656 | tf_op jit(solution)/shard_map/ppermute | solution.py:347
  27.8 14.3 %collective-permute-start.9 = (bf16[8,96,256]{2,1,0:T(8,128)(2,1)S(1)}, bf16[8,96,256]{2,1,0:T(8,128)(2,1)}, u32[]{:S(2)}, u32[]{:S(2)}) collective-permute-start(bf16[8,96,256]{2,1,0:T(8,128)(2,1)S(1)} %pad_maximum_fusion), channel_id=1, source_target_pairs={{0,96},{32,64},{64,32},{96,0},{1,97},{33,65},{65,33},{97,1},{2,98}... | collective-permute-start | bytes 1179656 | tf_op jit(solution)/shard_map/ppermute | solution.py:347
  34.1 7.9 %collective-permute-start.8 = (bf16[4,8,512]{2,1,0:T(8,128)(2,1)S(1)}, bf16[4,8,512]{2,1,0:T(8,128)(2,1)S(1)}, u32[]{:S(2)}, u32[]{:S(2)}) collective-permute-start(bf16[4,8,512]{2,1,0:T(8,128)(2,1)S(1)} %get-tuple-element.45), channel_id=1, source_target_pairs={{0,4},{1,5},{2,6},{3,7},{4,0},{5,1},{6,2},{7,3},{8,12},{9,13},{10,... | collective-permute-start | bytes 98312 | tf_op jit(solution)/shard_map/ppermute | solution.py:347
  42.1 18.1 %all-to-all-start = ((bf16[64,32,256]{2,1,0:T(8,128)(2,1)}), bf16[64,32,256]{2,1,0:T(8,128)(2,1)S(1)}, u32[]{:S(2)}, u32[]{:S(2)}) async-start(bf16[64,32,256]{2,1,0:T(8,128)(2,1)} %collective-permute-done.11), calls=%async_computation | async-start | bytes 2097152 | tf_op jit(solution)/shard_map/all_to_all | solution.py:389
  47.1 7.7 %collective-permute-start.12 = (f32[2,8,512]{2,1,0:T(8,128)S(1)}, f32[2,8,512]{2,1,0:T(8,128)S(1)}, u32[]{:S(2)}, u32[]{:S(2)}) collective-permute-start(f32[2,8,512]{2,1,0:T(8,128)S(1)} %slice.29), channel_id=1, source_target_pairs={{0,2},{1,3},{2,0},{3,1},{4,6},{5,7},{6,4},{7,5},{8,10},{9,11},{10,... | collective-permute-start | bytes 98312 | tf_op jit(solution)/shard_map/ppermute | solution.py:347
  54.8 4.7 %collective-permute-start.13 = (f32[1,8,512]{2,1,0:T(8,128)S(1)}, f32[1,8,512]{2,1,0:T(8,128)S(1)}, u32[]{:S(2)}, u32[]{:S(2)}) collective-permute-start(f32[1,8,512]{2,1,0:T(8,128)S(1)} %slice.36), channel_id=1, source_target_pairs={{0,1},{1,0},{2,3},{3,2},{4,5},{5,4},{6,7},{7,6},{8,9},{9,8},{10,11... | collective-permute-start | bytes 49160 | tf_op jit(solution)/shard_map/ppermute | solution.py:347

commit v4 on v3

--- a/solution.py
+++ b/solution.py
@@ -30,7 +30,7 @@
     return index ^ (index // 2)
 
 
-def prompt_kernel(outer, offset, kind, place_ref, q_ref, *refs):
+def prompt_kernel(outers, offset, kind, place_ref, q_ref, *refs):
     first, final = kind == "first", kind == "final"
     shard = place_ref[0]
     my_row, my_col = shard // SIDE, shard % SIDE
@@ -43,25 +43,28 @@
         anchor_ref, near_ref, far_ref, state_in, state_out, keys, key_cols, val = refs[:8]
     length = q_ref.shape[0]
     half = length // 2
-    if kind in ("next", "final"):
-        anchor, near, far, sems = refs[8:]
-        copies = [
-            pltpu.make_async_copy(anchor_ref.at[0:1, 0:16], anchor, sems.at[0]),
-            pltpu.make_async_copy(near_ref.at[offset : offset + SIDE], near, sems.at[1]),
-            pltpu.make_async_copy(far_ref.at[offset : offset + SIDE], far, sems.at[2]),
-        ]
-        for copy in copies:
-            copy.start()
-        for copy in copies:
-            copy.wait()
-        anchor_ref, near_ref, far_ref, offset = anchor, near, far, 0
+    fetch = kind in ("behind", "final")
+    if fetch:
+        sources = near_ref, far_ref
+        anchor, near_ref, far_ref, sems = refs[8:]
+        count = near_ref.shape[0]
+        copies = [pltpu.make_async_copy(anchor_ref.at[0:1, 0:16], anchor, sems.at[2])]
+        for index, (source, held) in enumerate(zip(sources, (near_ref, far_ref))):
+            part = source.at[offset : offset + count]
+            copies.append(pltpu.make_async_copy(part, held, sems.at[index]))
+        anchor_ref = anchor
 
     def run():
+        if fetch:
+            for copy in copies:
+                copy.start()
+            for copy in copies:
+                copy.wait()
         own_key = jnp.broadcast_to(anchor_ref[0, :16, :HEAD_WIDTH][:1], (half, HEAD_WIDTH))
-        for at in range(SIDE):
+        for at in range(SIDE * len(outers)):
             for side, ref in enumerate((near_ref, far_ref)):
-                part = ref[offset + at, :half]
-                inner = gray(at)
+                part = ref[at, :half]
+                outer, inner = outers[at // SIDE], gray(at % SIDE)
                 row, col = (my_row ^ outer, my_col ^ inner) if side == 0 else (my_row ^ inner, my_col ^ outer)
                 seen = row * SIDE + col <= shard
                 place = slice((2 * at + side) * half, (2 * at + side + 1) * half)
@@ -115,14 +118,14 @@
         run()
 
 
-def prompt_part(place, outer, q, arrays, kind, state=None, offset=0):
+def prompt_part(place, outers, q, arrays, kind, state=None, offset=0):
     rows = QUERY_PER_KEY * q.shape[0]
-    chunk = SIDE * q.shape[0]
+    chunk = SIDE * len(outers) * q.shape[0]
     whole = pl.BlockSpec(memory_space=pltpu.VMEM)
     specs, fetched = [whole] * len(arrays), []
-    if kind in ("next", "final"):
+    if kind in ("behind", "final"):
         arrays, specs = in_hbm(*arrays), [pl.BlockSpec(memory_space=pl.ANY)] * len(arrays)
-        part = (SIDE,) + arrays[1].shape[1:]
+        part = (SIDE * len(outers),) + arrays[1].shape[1:]
         fetched = [
             pltpu.VMEM((1, 16, 2 * HEAD_WIDTH), jnp.bfloat16),
             pltpu.VMEM(part, jnp.bfloat16),
@@ -132,7 +135,7 @@
     operands = arrays if state is None else (*arrays, state)
     specs = specs if state is None else specs + [whole]
     return pl.pallas_call(
-        partial(prompt_kernel, outer, offset, kind),
+        partial(prompt_kernel, outers, offset, kind),
         out_shape=jax.ShapeDtypeStruct(q.shape, jnp.bfloat16)
         if kind == "final"
         else pltpu.VMEM((rows, 2 * HEAD_WIDTH), jnp.float32),
@@ -145,11 +148,11 @@
         ]
         + fetched,
         input_output_aliases={} if kind in ("first", "final") else {5: 0},
-        compiler_params=pltpu.CompilerParams(vmem_limit_bytes=10 << 20),
+        compiler_params=pltpu.CompilerParams(vmem_limit_bytes=12 << 20),
         cost_estimate=pl.CostEstimate(
-            flops=8 * rows * chunk * HEAD_WIDTH,
+            flops=(12 if kind == "final" else 8) * rows * chunk * HEAD_WIDTH,
             bytes_accessed=4 * chunk * HEAD_WIDTH,
-            transcendentals=rows * chunk,
+            transcendentals=(12 if kind == "final" else 8) * rows * chunk // 8,
         ),
         name="prompt_part",
     )(place, q, *operands)
@@ -343,6 +346,48 @@
     )(place, weight, gathered)
 
 
+def mark_kernel(value_ref, out_ref):
+    out_ref[...] = jnp.zeros_like(out_ref)
+
+
+def mark(value):
+    return pl.pallas_call(
+        mark_kernel,
+        out_shape=jax.ShapeDtypeStruct((8, HEAD_WIDTH), jnp.float32),
+        in_specs=[pl.BlockSpec(memory_space=pl.ANY)],
+        out_specs=pl.BlockSpec(memory_space=pltpu.VMEM),
+        cost_estimate=pl.CostEstimate(flops=1 << 33, bytes_accessed=1 << 12, transcendentals=0),
+        name="mark",
+    )(value)
+
+
+def join_kernel(*refs):
+    parts, outs, sems = refs[:4], refs[4:6], refs[6]
+    copies = []
+    for index, part in enumerate(parts):
+        count = part.shape[0]
+        place = outs[index // 2].at[pl.ds(index % 2 * count, count)]
+        copies.append(pltpu.make_async_copy(part, place, sems.at[index]))
+    for copy in copies:
+        copy.start()
+    for copy in copies:
+        copy.wait()
+
+
+def join(first, second):
+    whole = pl.BlockSpec(memory_space=pltpu.VMEM)
+    shape = (2 * first[0].shape[0],) + first[0].shape[1:]
+    return pl.pallas_call(
+        join_kernel,
+        out_shape=[pltpu.HBM(shape, first[0].dtype)] * 2,
+        in_specs=[whole] * 4,
+        out_specs=[pl.BlockSpec(memory_space=pl.ANY)] * 2,
+        scratch_shapes=[pltpu.SemaphoreType.DMA((4,))],
+        compiler_params=pltpu.CompilerParams(vmem_limit_bytes=4 << 20),
+        name="join",
+    )(*first, *second)
+
+
 def exchange(value, axis, size, other):
     return lax.ppermute(value, axis, [(i, i ^ other) for i in range(size)])
 
@@ -374,28 +419,29 @@
     more = exchange(near, "row", SIDE, 1), exchange(far, "col", SIDE, 1)
     near, far, rows = lax.optimization_barrier((near, far, rows))
     rows = jnp.concatenate([rows, exchange(rows, "row", SIDE, 3)])
-    state = prompt_part(place, 0, q, (near, far), "first")
+    state = prompt_part(place, (0,), q, (near, far), "first")
     rows, more, state = lax.optimization_barrier((rows, more, state))
-    wide = jnp.concatenate([near, more[0]]), jnp.concatenate([far, more[1]])
+    wide = join((near, more[0]), (far, more[1]))
     last = exchange(wide[0], "row", SIDE, 3), exchange(wide[1], "col", SIDE, 3)
 
     steps = dec_q.shape[1] * dec_q.shape[2]
     sums, sent = project(place, output_weight, rows, ranks, steps)
-    state = prompt_part(place, 1, q, (near, *more), "ahead", state)
+    state = prompt_part(place, (1,), q, (near, *more), "ahead", state)
+    near, far = wide
     sums, sent, state = lax.optimization_barrier((sums, sent, state))
+    token = mark(sums)
     sent = exchange(sent, "head", ranks, 4)
-    state = prompt_part(place, 1, q, (near, *more), "behind", state)
-    sent, last, state, outgoing = lax.optimization_barrier((sent, last, state, outgoing))
+    token, outgoing = lax.optimization_barrier((token, outgoing))
     arrived = lax.all_to_all(outgoing, ("row", "col"), 0, 0, tiled=True)
 
     sums = sums + sent.astype(jnp.float32)
-    sums, state = lax.optimization_barrier((sums, state))
+    sums, near, far, state = lax.optimization_barrier((sums, near, far, state))
     sent = exchange(sums[2:], "head", ranks, 2)
-    state = prompt_part(place, 3, q, (near, *last), "next", state)
-    sent, state = lax.optimization_barrier((sent, state))
+    state = prompt_part(place, (1,), q, (near, near, far), "behind", state, offset=SIDE)
+    sent, last, state = lax.optimization_barrier((sent, last, state))
     sums = sums[:2] + sent
     sent = exchange(sums[1:], "head", ranks, 1)
-    prompt_attn = prompt_part(place, 2, q, (near, *last), "final", state, offset=SIDE)
+    prompt_attn = prompt_part(place, (3, 2), q, (near, *last), "final", state)
     sent, prompt_attn = lax.optimization_barrier((sent, prompt_attn))
     decode_out = (sums[0] + sent[0]).astype(jnp.bfloat16)
     return (prompt_attn[None], arrived[None], decode_out[None])

time: 61.6 us -> 58.7 us (0.953)
  Pallas kernels: 19.7 us -> 17.7 us
  starting transfers between devices: 28.7 us -> 27.9 us
    pallas_call x5, Pallas kernels: 15.3 us -> 13.3 us  [the longest x4 12.4 us: prompt_part(): pl.pallas_call(partial(prompt_kernel, outers, offset, kind), out_shape=ja...]
    ppermute x14, starting transfers between devices: 23.6 us -> 22.8 us  [exchange(): return lax.ppermute(value, axis, [(i, i ^ other) for i in range(size)])]
  transfers between devices with their start and end apart: 15 -> 15, of which waited for: 6 -> 6; matrix products, arithmetic and copies ran while one was open for 1% -> 1% of each run, Pallas kernels for 29% -> 27%
where the time goes in v4:
time: 58.7 us; the launch traced here: 58.3 us
  starting transfers between devices  27.9 us (48%)
  Pallas kernels  17.7 us (30%)
  waiting for transfers between devices  10.2 us (17%)
  local copies, waits for them, and re-layouts  1.03 us (2%)
  between operations  0.83 us (1%)
  other arithmetic  0.76 us (1%)
    ppermute x14, starting transfers between devices, exchange(): return lax.ppermute(value, axis, [(i, i ^ other) for i in range(size)])  22.8 us
    pallas_call x4, Pallas kernels, prompt_part(): pl.pallas_call(partial(prompt_kernel, outers, offset, kind), out_shape=ja...  12.4 us
    ppermute x14, waiting for transfers between devices, exchange(): return lax.ppermute(value, axis, [(i, i ^ other) for i in range(size)])  10.2 us
    all_to_all x1, starting transfers between devices, per_device(): arrived = lax.all_to_all(outgoing, ('row', 'col'), 0, 0, tiled=True)  5.02 us
    pallas_call x1, Pallas kernels, first_step(): pl.pallas_call(first_kernel, out_shape=(pltpu.VMEM((half + height, wide),...  2.09 us
    pallas_call x1, Pallas kernels, place_blocks(): pl.pallas_call(place_kernel, out_shape=jax.ShapeDtypeStruct(shape, blocks...  1.42 us
  transfers between devices with their start and end apart: 15, of which 6 were waited for; matrix products, arithmetic and copies ran while one was open for 1% of the time, Pallas kernels for 27%

profile of v4, /device:TPU:6, one launch (start us, length us, event | category | flops | bytes accessed | tf_op | source)
XLA Modules:
  0.0 58.3 jit_solution(16941286815939283013)
XLA Ops:
  0.6 2.1 %first_step.1 = (bf16[112,256]{1,0:T(8,128)(2,1)S(1)}, bf16[96,256]{1,0:T(8,128)(2,1)S(1)}) custom-call(s32[1,2]{1,0:T(1,128)} %len_hbm.1, bf16[192,256]{1,0:T(8,128)(2,1)} %bitcast.25, bf16[2,2,1024]{2,1,0:T(2,128)(2,1)} %bitcast.26, bf16[2,2,256]{2,1,0:T(2,128)(2,1)} %bitcast.27, bf16[2,1024,256]{2,1,0:T(8,128)(2,1)} %bitcast.23), custom_call_target="tpu_custom_call" | custom-call | flops 16777216 | bytes 1048576 | tf_op jit(solution)/shard_map/first_step/pallas_call | solution.py:228
  2.7 1.7 %collective-permute-start = (bf16[1,112,256]{2,1,0:T(8,128)(2,1)S(1)}, bf16[1,112,256]{2,1,0:T(8,128)(2,1)S(1)}, u32[]{:S(2)}, u32[]{:S(2)}) collective-permute-start(bf16[1,112,256]{2,1,0:T(8,128)(2,1)S(1)} %bitcast.20), channel_id=1, source_target_pairs={{0,8},{8,0},{16,24},{24,16},{1,9},{9,1},{17,25},{25,17},{2,10},{10... | collective-permute-start | bytes 172040 | tf_op jit(solution)/shard_map/ppermute | solution.py:392
  4.4 0.8 %collective-permute-start.2 = (bf16[1,96,256]{2,1,0:T(8,128)(2,1)S(1)}, bf16[1,96,256]{2,1,0:T(8,128)(2,1)S(1)}, u32[]{:S(2)}, u32[]{:S(2)}) collective-permute-start(bf16[1,96,256]{2,1,0:T(8,128)(2,1)S(1)} %bitcast.17), channel_id=1, source_target_pairs={{0,32},{32,0},{64,96},{96,64},{1,33},{33,1},{65,97},{97,65},{2,34}... | collective-permute-start | bytes 147464 | tf_op jit(solution)/shard_map/ppermute | solution.py:392
  5.2 1.4 %place_blocks.1 = bf16[64,32,256]{2,1,0:T(8,128)(2,1)S(1)} custom-call(s32[1,32]{1,0:T(1,128)} %bitcast.28, bf16[32,32,256]{2,1,0:T(8,128)(2,1)} %bitcast.24), custom_call_target="tpu_custom_call" | custom-call | bytes 1572864 | tf_op jit(solution)/shard_map/place_blocks/pallas_call | solution.py:281
  6.9 1.6 %collective-permute-done.2 = bf16[1,96,256]{2,1,0:T(8,128)(2,1)S(1)} collective-permute-done((bf16[1,96,256]{2,1,0:T(8,128)(2,1)S(1)}, bf16[1,96,256]{2,1,0:T(8,128)(2,1)S(1)}, u32[]{:S(2)}, u32[]{:S(2)}) %collective-permute-start.2) | collective-permute-done | bytes 49184 | tf_op jit(solution)/shard_map/ppermute | solution.py:392
  8.5 0.8 %collective-permute-start.3 = (bf16[2,96,256]{2,1,0:T(8,128)(2,1)S(1)}, bf16[2,96,256]{2,1,0:T(8,128)(2,1)S(1)}, u32[]{:S(2)}, u32[]{:S(2)}) collective-permute-start(bf16[2,96,256]{2,1,0:T(8,128)(2,1)S(1)} %pad_maximum_fusion.2), channel_id=1, source_target_pairs={{0,96},{32,64},{64,32},{96,0},{1,97},{33,65},{65,33},{97,1},{2,98}... | collective-permute-start | bytes 294920 | tf_op jit(solution)/shard_map/ppermute | solution.py:392
  9.3 2.0 %collective-permute-start.1 = (bf16[2,112,256]{2,1,0:T(8,128)(2,1)S(1)}, bf16[2,112,256]{2,1,0:T(8,128)(2,1)S(1)}, u32[]{:S(2)}, u32[]{:S(2)}) collective-permute-start(bf16[2,112,256]{2,1,0:T(8,128)(2,1)S(1)} %constant_dynamic-update-slice_fusion), channel_id=1, source_target_pairs={{0,24},{8,16},{16,8},{24,0},{1,25},{9,17},{17,9},{25,1},{2,26},{10... | collective-permute-start | bytes 344072 | tf_op jit(solution)/shard_map/ppermute | solution.py:392
  11.4 3.0 %collective-permute-done.3 = bf16[2,96,256]{2,1,0:T(8,128)(2,1)S(1)} collective-permute-done((bf16[2,96,256]{2,1,0:T(8,128)(2,1)S(1)}, bf16[2,96,256]{2,1,0:T(8,128)(2,1)S(1)}, u32[]{:S(2)}, u32[]{:S(2)}) %collective-permute-start.3) | collective-permute-done | bytes 98336 | tf_op jit(solution)/shard_map/ppermute | solution.py:392
  16.2 1.5 %collective-permute-start.6 = (bf16[4,96,256]{2,1,0:T(8,128)(2,1)S(1)}, bf16[4,96,256]{2,1,0:T(8,128)(2,1)S(1)}, u32[]{:S(2)}, u32[]{:S(2)}) collective-permute-start(bf16[4,96,256]{2,1,0:T(8,128)(2,1)S(1)} %pad_maximum_fusion.refs_0_), channel_id=1, source_target_pairs={{0,32},{32,0},{64,96},{96,64},{1,33},{33,1},{65,97},{97,65},{2,34}... | collective-permute-start | bytes 589832 | tf_op jit(solution)/shard_map/ppermute | solution.py:392
  17.7 1.8 %collective-permute-done.4 = bf16[4,16,256]{2,1,0:T(8,128)(2,1)S(1)} collective-permute-done((bf16[4,16,256]{2,1,0:T(8,128)(2,1)S(1)}, bf16[4,16,256]{2,1,0:T(8,128)(2,1)S(1)}, u32[]{:S(2)}, u32[]{:S(2)}) %collective-permute-start.4) | collective-permute-done | bytes 32800 | tf_op jit(solution)/shard_map/ppermute | solution.py:392
  19.5 2.6 %collective-permute-start.5 = (bf16[8,16,256]{2,1,0:T(8,128)(2,1)S(1)}, bf16[8,16,256]{2,1,0:T(8,128)(2,1)S(1)}, u32[]{:S(2)}, u32[]{:S(2)}) collective-permute-start(bf16[8,16,256]{2,1,0:T(8,128)(2,1)S(1)} %pad_maximum_fusion.3), channel_id=1, source_target_pairs={{0,96},{32,64},{64,32},{96,0},{1,97},{33,65},{65,33},{97,1},{2,98}... | collective-permute-start | bytes 196616 | tf_op jit(solution)/shard_map/ppermute | solution.py:392
  22.0 2.4 %prompt_part.4.refs_3_ = f32[1536,256]{1,0:T(8,128)S(1)} custom-call(s32[2]{0:T(128)S(1)} %pad_add_fusion.place_ref, bf16[192,1024]{1,0:T(8,128)(2,1)S(1)} %bitcast.13, bf16[4,96,256]{2,1,0:T(8,128)(2,1)S(1)} %pad_maximum_fusion.refs_0_, bf16[4,96,256]{2,1,0:T(8,128)(2,1)S(1)} %constant_dynamic-update-slice_fusion.2.refs_1_.refs_2_), custom_call_target="tpu_custom_call" | custom-call | flops 1207959552 | bytes 393216 | tf_op jit(solution)/shard_map/prompt_part/pallas_call | solution.py:137
  25.1 0.9 %join.1 = (bf16[8,96,256]{2,1,0:T(8,128)(2,1)}, bf16[8,96,256]{2,1,0:T(8,128)(2,1)}) custom-call(bf16[4,96,256]{2,1,0:T(8,128)(2,1)S(1)} %pad_maximum_fusion.refs_0_, bf16[4,96,256]{2,1,0:T(8,128)(2,1)S(1)} %collective-permute-done.6.refs_1_, bf16[4,96,256]{2,1,0:T(8,128)(2,1)S(1)} %constant_dynamic-update-slice_fusion.2.refs_1_.refs_2_, ...), custom_call_target="tpu_custom_call" | custom-call | tf_op jit(solution)/shard_map/join/pallas_call | solution.py:380
  26.0 2.6 %collective-permute-start.10 = (bf16[8,96,256]{2,1,0:T(8,128)(2,1)}, bf16[8,96,256]{2,1,0:T(8,128)(2,1)}, u32[]{:S(2)}, u32[]{:S(2)}) collective-permute-start(bf16[8,96,256]{2,1,0:T(8,128)(2,1)} %get-tuple-element.51.refs_0_.refs_1_), channel_id=1, source_target_pairs={{0,96},{32,64},{64,32},{96,0},{1,97},{33,65},{65,33},{97,1},{2,98}... | collective-permute-start | bytes 1179656 | tf_op jit(solution)/shard_map/ppermute | solution.py:392
  28.6 2.2 %collective-permute-start.11 = (bf16[8,96,256]{2,1,0:T(8,128)(2,1)}, bf16[8,96,256]{2,1,0:T(8,128)(2,1)}, u32[]{:S(2)}, u32[]{:S(2)}) collective-permute-start(bf16[8,96,256]{2,1,0:T(8,128)(2,1)} %get-tuple-element.52.refs_2_), channel_id=1, source_target_pairs={{0,24},{8,16},{16,8},{24,0},{1,25},{9,17},{17,9},{25,1},{2,26},{10... | collective-permute-start | bytes 1179656 | tf_op jit(solution)/shard_map/ppermute | solution.py:392
  30.7 3.3 %prompt_part.5.refs_3_ = f32[1536,256]{1,0:T(8,128)S(1)} custom-call(s32[2]{0:T(128)S(1)} %pad_add_fusion.place_ref, bf16[192,1024]{1,0:T(8,128)(2,1)S(1)} %bitcast.14, bf16[4,96,256]{2,1,0:T(8,128)(2,1)S(1)} %pad_maximum_fusion.refs_0_, bf16[4,96,256]{2,1,0:T(8,128)(2,1)S(1)} %collective-permute-done.6.refs_1_, ...), custom_call_target="tpu_custom_call", output_to_operand_aliasing={{}: (5, {})} | custom-call | flops 1207959552 | bytes 393216 | tf_op jit(solution)/shard_map/prompt_part/pallas_call | solution.py:137
  34.0 0.9 %project.1 = (f32[4,8,512]{2,1,0:T(8,128)S(1)}, bf16[4,8,512]{2,1,0:T(8,128)(2,1)S(1)}) custom-call(s32[2]{0:T(128)S(1)} %pad_add_fusion.place_ref, bf16[1024,512]{1,0:T(8,128)(2,1)S(1)} %copy-done, bf16[16,16,256]{2,1,0:T(8,128)(2,1)S(1)} %pad_maximum_fusion.1.refs_0_), custom_call_target="tpu_custom_call" | custom-call | flops 67108864 | bytes 1048576 | tf_op jit(solution)/shard_map/project/pallas_call | solution.py:329
  34.9 4.6 %collective-permute-start.8 = (bf16[4,8,512]{2,1,0:T(8,128)(2,1)S(1)}, bf16[4,8,512]{2,1,0:T(8,128)(2,1)S(1)}, u32[]{:S(2)}, u32[]{:S(2)}) collective-permute-start(bf16[4,8,512]{2,1,0:T(8,128)(2,1)S(1)} %get-tuple-element.46), channel_id=1, source_target_pairs={{0,4},{1,5},{2,6},{3,7},{4,0},{5,1},{6,2},{7,3},{8,12},{9,13},{10,... | collective-permute-start | bytes 98312 | tf_op jit(solution)/shard_map/ppermute | solution.py:392
  39.5 5.0 %all-to-all-start = ((bf16[64,32,256]{2,1,0:T(8,128)(2,1)}), bf16[64,32,256]{2,1,0:T(8,128)(2,1)S(1)}, u32[]{:S(2)}, u32[]{:S(2)}) async-start(bf16[64,32,256]{2,1,0:T(8,128)(2,1)} %collective-permute-done.13), calls=%async_computation | async-start | bytes 2097152 | tf_op jit(solution)/shard_map/all_to_all | solution.py:435
  44.5 1.7 %collective-permute-start.9 = (f32[2,8,512]{2,1,0:T(8,128)S(1)}, f32[2,8,512]{2,1,0:T(8,128)S(1)}, u32[]{:S(2)}, u32[]{:S(2)}) collective-permute-start(f32[2,8,512]{2,1,0:T(8,128)S(1)} %slice.29), channel_id=1, source_target_pairs={{0,2},{1,3},{2,0},{3,1},{4,6},{5,7},{6,4},{7,5},{8,10},{9,11},{10,... | collective-permute-start | bytes 98312 | tf_op jit(solution)/shard_map/ppermute | solution.py:392
  46.8 2.7 %collective-permute-done.9 = f32[2,8,512]{2,1,0:T(8,128)S(1)} collective-permute-done((f32[2,8,512]{2,1,0:T(8,128)S(1)}, f32[2,8,512]{2,1,0:T(8,128)S(1)}, u32[]{:S(2)}, u32[]{:S(2)}) %collective-permute-start.9) | collective-permute-done | bytes 32800 | tf_op jit(solution)/shard_map/ppermute | solution.py:392
  49.5 1.1 %collective-permute-start.12 = (f32[1,8,512]{2,1,0:T(8,128)S(1)}, f32[1,8,512]{2,1,0:T(8,128)S(1)}, u32[]{:S(2)}, u32[]{:S(2)}) collective-permute-start(f32[1,8,512]{2,1,0:T(8,128)S(1)} %slice.36), channel_id=1, source_target_pairs={{0,1},{1,0},{2,3},{3,2},{4,5},{5,4},{6,7},{7,6},{8,9},{9,8},{10,11... | collective-permute-start | bytes 49160 | tf_op jit(solution)/shard_map/ppermute | solution.py:392
  50.6 6.2 %prompt_part.7 = bf16[192,1024]{1,0:T(8,128)(2,1)} custom-call(s32[2]{0:T(128)S(1)} %pad_add_fusion.place_ref, bf16[192,1024]{1,0:T(8,128)(2,1)S(1)} %bitcast.16, bf16[8,96,256]{2,1,0:T(8,128)(2,1)} %get-tuple-element.51.refs_0_.refs_1_, bf16[8,96,256]{2,1,0:T(8,128)(2,1)} %collective-permute-done.10.refs_1_, ...), custom_call_target="tpu_custom_call" | custom-call | flops 3623878656 | bytes 786432 | tf_op jit(solution)/shard_map/prompt_part/pallas_call | solution.py:137
  57.4 1.0 %copy.20 = bf16[1,64,32,256]{3,2,1,0:T(8,128)(2,1)} copy(bf16[1,64,32,256]{3,2,1,0:T(8,128)(2,1)S(1)} %bitcast.22) | data formatting | bytes 2097152
  (39 shorter events, 3.8 us)
Async XLA Ops:
  2.7 6.6 %collective-permute-start = (bf16[1,112,256]{2,1,0:T(8,128)(2,1)S(1)}, bf16[1,112,256]{2,1,0:T(8,128)(2,1)S(1)}, u32[]{:S(2)}, u32[]{:S(2)}) collective-permute-start(bf16[1,112,256]{2,1,0:T(8,128)(2,1)S(1)} %bitcast.20), channel_id=1, source_target_pairs={{0,8},{8,0},{16,24},{24,16},{1,9},{9,1},{17,25},{25,17},{2,10},{10... | collective-permute-start | bytes 172040 | tf_op jit(solution)/shard_map/ppermute | solution.py:392
  4.4 4.1 %collective-permute-start.2 = (bf16[1,96,256]{2,1,0:T(8,128)(2,1)S(1)}, bf16[1,96,256]{2,1,0:T(8,128)(2,1)S(1)}, u32[]{:S(2)}, u32[]{:S(2)}) collective-permute-start(bf16[1,96,256]{2,1,0:T(8,128)(2,1)S(1)} %bitcast.17), channel_id=1, source_target_pairs={{0,32},{32,0},{64,96},{96,64},{1,33},{33,1},{65,97},{97,65},{2,34}... | collective-permute-start | bytes 147464 | tf_op jit(solution)/shard_map/ppermute | solution.py:392
  5.2 16.8 %copy-start.1 = (bf16[1,192,1024]{2,1,0:T(8,128)(2,1)S(1)}, bf16[1,192,1024]{2,1,0:T(8,128)(2,1)}, u32[]{:S(2)}) copy-start(bf16[1,192,1024]{2,1,0:T(8,128)(2,1)} %param.9) | copy-start | bytes 1179652
  6.7 32.8 %collective-permute-start.13 = (bf16[64,32,256]{2,1,0:T(8,128)(2,1)S(1)}, bf16[64,32,256]{2,1,0:T(8,128)(2,1)}, u32[]{:S(2)}, u32[]{:S(2)}) collective-permute-start(bf16[64,32,256]{2,1,0:T(8,128)(2,1)S(1)} %place_blocks.1), channel_id=1, source_target_pairs={{0,128},{128,0},{1,129},{129,1},{2,130},{130,2},{3,131},{131,3},{4... | collective-permute-start | bytes 3145736 | tf_op jit(solution)/shard_map/ppermute | solution.py:392
  8.5 5.9 %collective-permute-start.3 = (bf16[2,96,256]{2,1,0:T(8,128)(2,1)S(1)}, bf16[2,96,256]{2,1,0:T(8,128)(2,1)S(1)}, u32[]{:S(2)}, u32[]{:S(2)}) collective-permute-start(bf16[2,96,256]{2,1,0:T(8,128)(2,1)S(1)} %pad_maximum_fusion.2), channel_id=1, source_target_pairs={{0,96},{32,64},{64,32},{96,0},{1,97},{33,65},{65,33},{97,1},{2,98}... | collective-permute-start | bytes 294920 | tf_op jit(solution)/shard_map/ppermute | solution.py:392
  9.3 6.1 %collective-permute-start.1 = (bf16[2,112,256]{2,1,0:T(8,128)(2,1)S(1)}, bf16[2,112,256]{2,1,0:T(8,128)(2,1)S(1)}, u32[]{:S(2)}, u32[]{:S(2)}) collective-permute-start(bf16[2,112,256]{2,1,0:T(8,128)(2,1)S(1)} %constant_dynamic-update-slice_fusion), channel_id=1, source_target_pairs={{0,24},{8,16},{16,8},{24,0},{1,25},{9,17},{17,9},{25,1},{2,26},{10... | collective-permute-start | bytes 344072 | tf_op jit(solution)/shard_map/ppermute | solution.py:392
  14.4 10.6 %collective-permute-start.7 = (bf16[4,96,256]{2,1,0:T(8,128)(2,1)S(1)}, bf16[4,96,256]{2,1,0:T(8,128)(2,1)S(1)}, u32[]{:S(2)}, u32[]{:S(2)}) collective-permute-start(bf16[4,96,256]{2,1,0:T(8,128)(2,1)S(1)} %constant_dynamic-update-slice_fusion.2.refs_1_.refs_2_), channel_id=1, source_target_pairs={{0,8},{8,0},{16,24},{24,16},{1,9},{9,1},{17,25},{25,17},{2,10},{10... | collective-permute-start | bytes 589832 | tf_op jit(solution)/shard_map/ppermute | solution.py:392
  15.4 4.0 %collective-permute-start.4 = (bf16[4,16,256]{2,1,0:T(8,128)(2,1)S(1)}, bf16[4,16,256]{2,1,0:T(8,128)(2,1)S(1)}, u32[]{:S(2)}, u32[]{:S(2)}) collective-permute-start(bf16[4,16,256]{2,1,0:T(8,128)(2,1)S(1)} %pad_maximum_fusion.4), channel_id=1, source_target_pairs={{0,32},{32,0},{64,96},{96,64},{1,33},{33,1},{65,97},{97,65},{2,34}... | collective-permute-start | bytes 98312 | tf_op jit(solution)/shard_map/ppermute | solution.py:392
  16.2 8.9 %collective-permute-start.6 = (bf16[4,96,256]{2,1,0:T(8,128)(2,1)S(1)}, bf16[4,96,256]{2,1,0:T(8,128)(2,1)S(1)}, u32[]{:S(2)}, u32[]{:S(2)}) collective-permute-start(bf16[4,96,256]{2,1,0:T(8,128)(2,1)S(1)} %pad_maximum_fusion.refs_0_), channel_id=1, source_target_pairs={{0,32},{32,0},{64,96},{96,64},{1,33},{33,1},{65,97},{97,65},{2,34}... | collective-permute-start | bytes 589832 | tf_op jit(solution)/shard_map/ppermute | solution.py:392
  19.5 5.6 %collective-permute-start.5 = (bf16[8,16,256]{2,1,0:T(8,128)(2,1)S(1)}, bf16[8,16,256]{2,1,0:T(8,128)(2,1)S(1)}, u32[]{:S(2)}, u32[]{:S(2)}) collective-permute-start(bf16[8,16,256]{2,1,0:T(8,128)(2,1)S(1)} %pad_maximum_fusion.3), channel_id=1, source_target_pairs={{0,96},{32,64},{64,32},{96,0},{1,97},{33,65},{65,33},{97,1},{2,98}... | collective-permute-start | bytes 196616 | tf_op jit(solution)/shard_map/ppermute | solution.py:392
  26.0 23.5 %collective-permute-start.10 = (bf16[8,96,256]{2,1,0:T(8,128)(2,1)}, bf16[8,96,256]{2,1,0:T(8,128)(2,1)}, u32[]{:S(2)}, u32[]{:S(2)}) collective-permute-start(bf16[8,96,256]{2,1,0:T(8,128)(2,1)} %get-tuple-element.51.refs_0_.refs_1_), channel_id=1, source_target_pairs={{0,96},{32,64},{64,32},{96,0},{1,97},{33,65},{65,33},{97,1},{2,98}... | collective-permute-start | bytes 1179656 | tf_op jit(solution)/shard_map/ppermute | solution.py:392
  28.6 5.4 %copy-start = (bf16[1024,512]{1,0:T(8,128)(2,1)S(1)}, bf16[1024,512]{1,0:T(8,128)(2,1)}, u32[]{:S(2)}) copy-start(bf16[1024,512]{1,0:T(8,128)(2,1)} %weight_ref.1) | copy-start | bytes 3145732
  28.6 20.9 %collective-permute-start.11 = (bf16[8,96,256]{2,1,0:T(8,128)(2,1)}, bf16[8,96,256]{2,1,0:T(8,128)(2,1)}, u32[]{:S(2)}, u32[]{:S(2)}) collective-permute-start(bf16[8,96,256]{2,1,0:T(8,128)(2,1)} %get-tuple-element.52.refs_2_), channel_id=1, source_target_pairs={{0,24},{8,16},{16,8},{24,0},{1,25},{9,17},{17,9},{25,1},{2,26},{10... | collective-permute-start | bytes 1179656 | tf_op jit(solution)/shard_map/ppermute | solution.py:392
  34.9 9.6 %collective-permute-start.8 = (bf16[4,8,512]{2,1,0:T(8,128)(2,1)S(1)}, bf16[4,8,512]{2,1,0:T(8,128)(2,1)S(1)}, u32[]{:S(2)}, u32[]{:S(2)}) collective-permute-start(bf16[4,8,512]{2,1,0:T(8,128)(2,1)S(1)} %get-tuple-element.46), channel_id=1, source_target_pairs={{0,4},{1,5},{2,6},{3,7},{4,0},{5,1},{6,2},{7,3},{8,12},{9,13},{10,... | collective-permute-start | bytes 98312 | tf_op jit(solution)/shard_map/ppermute | solution.py:392
  39.5 17.9 %all-to-all-start = ((bf16[64,32,256]{2,1,0:T(8,128)(2,1)}), bf16[64,32,256]{2,1,0:T(8,128)(2,1)S(1)}, u32[]{:S(2)}, u32[]{:S(2)}) async-start(bf16[64,32,256]{2,1,0:T(8,128)(2,1)} %collective-permute-done.13), calls=%async_computation | async-start | bytes 2097152 | tf_op jit(solution)/shard_map/all_to_all | solution.py:435
  44.5 4.9 %collective-permute-start.9 = (f32[2,8,512]{2,1,0:T(8,128)S(1)}, f32[2,8,512]{2,1,0:T(8,128)S(1)}, u32[]{:S(2)}, u32[]{:S(2)}) collective-permute-start(f32[2,8,512]{2,1,0:T(8,128)S(1)} %slice.29), channel_id=1, source_target_pairs={{0,2},{1,3},{2,0},{3,1},{4,6},{5,7},{6,4},{7,5},{8,10},{9,11},{10,... | collective-permute-start | bytes 98312 | tf_op jit(solution)/shard_map/ppermute | solution.py:392
  49.5 7.3 %collective-permute-start.12 = (f32[1,8,512]{2,1,0:T(8,128)S(1)}, f32[1,8,512]{2,1,0:T(8,128)S(1)}, u32[]{:S(2)}, u32[]{:S(2)}) collective-permute-start(f32[1,8,512]{2,1,0:T(8,128)S(1)} %slice.36), channel_id=1, source_target_pairs={{0,1},{1,0},{2,3},{3,2},{4,5},{5,4},{6,7},{7,6},{8,9},{9,8},{10,11... | collective-permute-start | bytes 49160 | tf_op jit(solution)/shard_map/ppermute | solution.py:392

commit v5 on v4

--- a/solution.py
+++ b/solution.py
@@ -58,11 +58,13 @@
         if fetch:
             for copy in copies:
                 copy.start()
-            for copy in copies:
+            for copy in copies[:2]:
                 copy.wait()
         own_key = jnp.broadcast_to(anchor_ref[0, :16, :HEAD_WIDTH][:1], (half, HEAD_WIDTH))
-        for at in range(SIDE * len(outers)):
-            for side, ref in enumerate((near_ref, far_ref)):
+        for side, ref in enumerate((near_ref, far_ref)):
+            if fetch and side == 1:
+                copies[2].wait()
+            for at in range(SIDE * len(outers)):
                 part = ref[at, :half]
                 outer, inner = outers[at // SIDE], gray(at % SIDE)
                 row, col = (my_row ^ outer, my_col ^ inner) if side == 0 else (my_row ^ inner, my_col ^ outer)
@@ -164,10 +166,12 @@
 
 def first_kernel(len_hbm, kv_ref, q_ref, new_ref, cache_ref, near_ref, far_ref, *scratch):
     len_ref, kv, q_in, new_in, cache, q_rows, fresh, out_rows, packed, sems = scratch
+    pairs = [(kv_ref, kv), (q_ref, q_in), (new_ref, new_in), (len_hbm, len_ref)]
+    pairs += [(cache_ref.at[req], cache.at[req]) for req in range(q_in.shape[0])]
     copies = [
         pltpu.make_async_copy(src, dst, sems.at[i])
         for i, (src, dst) in enumerate(
-            ((cache_ref, cache), (kv_ref, kv), (q_ref, q_in), (new_ref, new_in), (len_hbm, len_ref))
+            pairs
         )
     ]
     for copy in copies:
@@ -177,12 +181,12 @@
     rows = QUERY_PER_KEY * steps
     half = far_ref.shape[0]
     fresh[...] = jnp.zeros_like(fresh)
-    for copy in copies[1:]:
+    for copy in copies[:4]:
         copy.wait()
     near_ref[:half, :] = kv[:half, :]
     far_ref[...] = kv[half:, :]
-    copies[0].wait()
     for req in range(requests):
+        copies[4 + req].wait()
         for head in range(QUERY_PER_KEY):
             q_rows[head * steps : (head + 1) * steps, :] = q_in[
                 req, :, head * HEAD_WIDTH : (head + 1) * HEAD_WIDTH
@@ -243,7 +247,7 @@
             pltpu.VMEM((HEAD_WIDTH, 2 * HEAD_WIDTH), jnp.float32),
             pltpu.VMEM((requests * steps, width), jnp.float32),
             pltpu.VMEM((height, wide), jnp.float32),
-            pltpu.SemaphoreType.DMA((5,)),
+            pltpu.SemaphoreType.DMA((4 + requests,)),
         ],
         compiler_params=pltpu.CompilerParams(vmem_limit_bytes=16 << 20),
         cost_estimate=pl.CostEstimate(

time: 58.7 us -> 58.7 us (level)
  no operation moved by 1% of the time
where the time goes in v5:
time: 58.7 us; the launch traced here: 58.3 us
  starting transfers between devices  27.9 us (48%)
  Pallas kernels  17.7 us (30%)
  waiting for transfers between devices  10.2 us (17%)
  local copies, waits for them, and re-layouts  1.03 us (2%)
  between operations  0.83 us (1%)
  other arithmetic  0.76 us (1%)
    ppermute x14, starting transfers between devices, exchange(): return lax.ppermute(value, axis, [(i, i ^ other) for i in range(size)])  22.8 us
    pallas_call x4, Pallas kernels, prompt_part(): pl.pallas_call(partial(prompt_kernel, outers, offset, kind), out_shape=ja...  12.4 us
    ppermute x14, waiting for transfers between devices, exchange(): return lax.ppermute(value, axis, [(i, i ^ other) for i in range(size)])  10.2 us
    all_to_all x1, starting transfers between devices, per_device(): arrived = lax.all_to_all(outgoing, ('row', 'col'), 0, 0, tiled=True)  5.02 us
    pallas_call x1, Pallas kernels, first_step(): pl.pallas_call(first_kernel, out_shape=(pltpu.VMEM((half + height, wide),...  2.12 us
    pallas_call x1, Pallas kernels, place_blocks(): pl.pallas_call(place_kernel, out_shape=jax.ShapeDtypeStruct(shape, blocks...  1.42 us
  transfers between devices with their start and end apart: 15, of which 6 were waited for; matrix products, arithmetic and copies ran while one was open for 1% of the time, Pallas kernels for 27%

profile of v5, /device:TPU:6, one launch (start us, length us, event | category | flops | bytes accessed | tf_op | source)
XLA Modules:
  0.0 58.3 jit_solution(17154240154301030564)
XLA Ops:
  0.6 2.1 %first_step.1 = (bf16[112,256]{1,0:T(8,128)(2,1)S(1)}, bf16[96,256]{1,0:T(8,128)(2,1)S(1)}) custom-call(s32[1,2]{1,0:T(1,128)} %len_hbm.1, bf16[192,256]{1,0:T(8,128)(2,1)} %bitcast.25, bf16[2,2,1024]{2,1,0:T(2,128)(2,1)} %bitcast.26, bf16[2,2,256]{2,1,0:T(2,128)(2,1)} %bitcast.27, bf16[2,1024,256]{2,1,0:T(8,128)(2,1)} %bitcast.23), custom_call_target="tpu_custom_call" | custom-call | flops 16777216 | bytes 1048576 | tf_op jit(solution)/shard_map/first_step/pallas_call | solution.py:232
  2.8 1.7 %collective-permute-start = (bf16[1,112,256]{2,1,0:T(8,128)(2,1)S(1)}, bf16[1,112,256]{2,1,0:T(8,128)(2,1)S(1)}, u32[]{:S(2)}, u32[]{:S(2)}) collective-permute-start(bf16[1,112,256]{2,1,0:T(8,128)(2,1)S(1)} %bitcast.20), channel_id=1, source_target_pairs={{0,8},{8,0},{16,24},{24,16},{1,9},{9,1},{17,25},{25,17},{2,10},{10... | collective-permute-start | bytes 172040 | tf_op jit(solution)/shard_map/ppermute | solution.py:396
  4.4 0.8 %collective-permute-start.2 = (bf16[1,96,256]{2,1,0:T(8,128)(2,1)S(1)}, bf16[1,96,256]{2,1,0:T(8,128)(2,1)S(1)}, u32[]{:S(2)}, u32[]{:S(2)}) collective-permute-start(bf16[1,96,256]{2,1,0:T(8,128)(2,1)S(1)} %bitcast.17), channel_id=1, source_target_pairs={{0,32},{32,0},{64,96},{96,64},{1,33},{33,1},{65,97},{97,65},{2,34}... | collective-permute-start | bytes 147464 | tf_op jit(solution)/shard_map/ppermute | solution.py:396
  5.3 1.4 %place_blocks.1 = bf16[64,32,256]{2,1,0:T(8,128)(2,1)S(1)} custom-call(s32[1,32]{1,0:T(1,128)} %bitcast.28, bf16[32,32,256]{2,1,0:T(8,128)(2,1)} %bitcast.24), custom_call_target="tpu_custom_call" | custom-call | bytes 1572864 | tf_op jit(solution)/shard_map/place_blocks/pallas_call | solution.py:285
  6.9 1.6 %collective-permute-done.2 = bf16[1,96,256]{2,1,0:T(8,128)(2,1)S(1)} collective-permute-done((bf16[1,96,256]{2,1,0:T(8,128)(2,1)S(1)}, bf16[1,96,256]{2,1,0:T(8,128)(2,1)S(1)}, u32[]{:S(2)}, u32[]{:S(2)}) %collective-permute-start.2) | collective-permute-done | bytes 49184 | tf_op jit(solution)/shard_map/ppermute | solution.py:396
  8.5 0.8 %collective-permute-start.3 = (bf16[2,96,256]{2,1,0:T(8,128)(2,1)S(1)}, bf16[2,96,256]{2,1,0:T(8,128)(2,1)S(1)}, u32[]{:S(2)}, u32[]{:S(2)}) collective-permute-start(bf16[2,96,256]{2,1,0:T(8,128)(2,1)S(1)} %pad_maximum_fusion.2), channel_id=1, source_target_pairs={{0,96},{32,64},{64,32},{96,0},{1,97},{33,65},{65,33},{97,1},{2,98}... | collective-permute-start | bytes 294920 | tf_op jit(solution)/shard_map/ppermute | solution.py:396
  9.4 2.0 %collective-permute-start.1 = (bf16[2,112,256]{2,1,0:T(8,128)(2,1)S(1)}, bf16[2,112,256]{2,1,0:T(8,128)(2,1)S(1)}, u32[]{:S(2)}, u32[]{:S(2)}) collective-permute-start(bf16[2,112,256]{2,1,0:T(8,128)(2,1)S(1)} %constant_dynamic-update-slice_fusion), channel_id=1, source_target_pairs={{0,24},{8,16},{16,8},{24,0},{1,25},{9,17},{17,9},{25,1},{2,26},{10... | collective-permute-start | bytes 344072 | tf_op jit(solution)/shard_map/ppermute | solution.py:396
  11.4 3.0 %collective-permute-done.3 = bf16[2,96,256]{2,1,0:T(8,128)(2,1)S(1)} collective-permute-done((bf16[2,96,256]{2,1,0:T(8,128)(2,1)S(1)}, bf16[2,96,256]{2,1,0:T(8,128)(2,1)S(1)}, u32[]{:S(2)}, u32[]{:S(2)}) %collective-permute-start.3) | collective-permute-done | bytes 98336 | tf_op jit(solution)/shard_map/ppermute | solution.py:396
  16.2 1.5 %collective-permute-start.6 = (bf16[4,96,256]{2,1,0:T(8,128)(2,1)S(1)}, bf16[4,96,256]{2,1,0:T(8,128)(2,1)S(1)}, u32[]{:S(2)}, u32[]{:S(2)}) collective-permute-start(bf16[4,96,256]{2,1,0:T(8,128)(2,1)S(1)} %pad_maximum_fusion.refs_0_), channel_id=1, source_target_pairs={{0,32},{32,0},{64,96},{96,64},{1,33},{33,1},{65,97},{97,65},{2,34}... | collective-permute-start | bytes 589832 | tf_op jit(solution)/shard_map/ppermute | solution.py:396
  17.7 1.8 %collective-permute-done.4 = bf16[4,16,256]{2,1,0:T(8,128)(2,1)S(1)} collective-permute-done((bf16[4,16,256]{2,1,0:T(8,128)(2,1)S(1)}, bf16[4,16,256]{2,1,0:T(8,128)(2,1)S(1)}, u32[]{:S(2)}, u32[]{:S(2)}) %collective-permute-start.4) | collective-permute-done | bytes 32800 | tf_op jit(solution)/shard_map/ppermute | solution.py:396
  19.5 2.6 %collective-permute-start.5 = (bf16[8,16,256]{2,1,0:T(8,128)(2,1)S(1)}, bf16[8,16,256]{2,1,0:T(8,128)(2,1)S(1)}, u32[]{:S(2)}, u32[]{:S(2)}) collective-permute-start(bf16[8,16,256]{2,1,0:T(8,128)(2,1)S(1)} %pad_maximum_fusion.3), channel_id=1, source_target_pairs={{0,96},{32,64},{64,32},{96,0},{1,97},{33,65},{65,33},{97,1},{2,98}... | collective-permute-start | bytes 196616 | tf_op jit(solution)/shard_map/ppermute | solution.py:396
  22.1 2.4 %prompt_part.4.refs_3_ = f32[1536,256]{1,0:T(8,128)S(1)} custom-call(s32[2]{0:T(128)S(1)} %pad_add_fusion.place_ref, bf16[192,1024]{1,0:T(8,128)(2,1)S(1)} %bitcast.13, bf16[4,96,256]{2,1,0:T(8,128)(2,1)S(1)} %pad_maximum_fusion.refs_0_, bf16[4,96,256]{2,1,0:T(8,128)(2,1)S(1)} %constant_dynamic-update-slice_fusion.2.refs_1_.refs_2_), custom_call_target="tpu_custom_call" | custom-call | flops 1207959552 | bytes 393216 | tf_op jit(solution)/shard_map/prompt_part/pallas_call | solution.py:139
  25.1 0.9 %join.1 = (bf16[8,96,256]{2,1,0:T(8,128)(2,1)}, bf16[8,96,256]{2,1,0:T(8,128)(2,1)}) custom-call(bf16[4,96,256]{2,1,0:T(8,128)(2,1)S(1)} %pad_maximum_fusion.refs_0_, bf16[4,96,256]{2,1,0:T(8,128)(2,1)S(1)} %collective-permute-done.6.refs_1_, bf16[4,96,256]{2,1,0:T(8,128)(2,1)S(1)} %constant_dynamic-update-slice_fusion.2.refs_1_.refs_2_, ...), custom_call_target="tpu_custom_call" | custom-call | tf_op jit(solution)/shard_map/join/pallas_call | solution.py:384
  26.0 2.6 %collective-permute-start.10 = (bf16[8,96,256]{2,1,0:T(8,128)(2,1)}, bf16[8,96,256]{2,1,0:T(8,128)(2,1)}, u32[]{:S(2)}, u32[]{:S(2)}) collective-permute-start(bf16[8,96,256]{2,1,0:T(8,128)(2,1)} %get-tuple-element.51.refs_0_.refs_1_), channel_id=1, source_target_pairs={{0,96},{32,64},{64,32},{96,0},{1,97},{33,65},{65,33},{97,1},{2,98}... | collective-permute-start | bytes 1179656 | tf_op jit(solution)/shard_map/ppermute | solution.py:396
  28.6 2.2 %collective-permute-start.11 = (bf16[8,96,256]{2,1,0:T(8,128)(2,1)}, bf16[8,96,256]{2,1,0:T(8,128)(2,1)}, u32[]{:S(2)}, u32[]{:S(2)}) collective-permute-start(bf16[8,96,256]{2,1,0:T(8,128)(2,1)} %get-tuple-element.52.refs_2_), channel_id=1, source_target_pairs={{0,24},{8,16},{16,8},{24,0},{1,25},{9,17},{17,9},{25,1},{2,26},{10... | collective-permute-start | bytes 1179656 | tf_op jit(solution)/shard_map/ppermute | solution.py:396
  30.8 3.3 %prompt_part.5.refs_3_ = f32[1536,256]{1,0:T(8,128)S(1)} custom-call(s32[2]{0:T(128)S(1)} %pad_add_fusion.place_ref, bf16[192,1024]{1,0:T(8,128)(2,1)S(1)} %bitcast.14, bf16[4,96,256]{2,1,0:T(8,128)(2,1)S(1)} %pad_maximum_fusion.refs_0_, bf16[4,96,256]{2,1,0:T(8,128)(2,1)S(1)} %collective-permute-done.6.refs_1_, ...), custom_call_target="tpu_custom_call", output_to_operand_aliasing={{}: (5, {})} | custom-call | flops 1207959552 | bytes 393216 | tf_op jit(solution)/shard_map/prompt_part/pallas_call | solution.py:139
  34.0 0.9 %project.1 = (f32[4,8,512]{2,1,0:T(8,128)S(1)}, bf16[4,8,512]{2,1,0:T(8,128)(2,1)S(1)}) custom-call(s32[2]{0:T(128)S(1)} %pad_add_fusion.place_ref, bf16[1024,512]{1,0:T(8,128)(2,1)S(1)} %copy-done, bf16[16,16,256]{2,1,0:T(8,128)(2,1)S(1)} %pad_maximum_fusion.1.refs_0_), custom_call_target="tpu_custom_call" | custom-call | flops 67108864 | bytes 1048576 | tf_op jit(solution)/shard_map/project/pallas_call | solution.py:333
  34.9 4.6 %collective-permute-start.8 = (bf16[4,8,512]{2,1,0:T(8,128)(2,1)S(1)}, bf16[4,8,512]{2,1,0:T(8,128)(2,1)S(1)}, u32[]{:S(2)}, u32[]{:S(2)}) collective-permute-start(bf16[4,8,512]{2,1,0:T(8,128)(2,1)S(1)} %get-tuple-element.46), channel_id=1, source_target_pairs={{0,4},{1,5},{2,6},{3,7},{4,0},{5,1},{6,2},{7,3},{8,12},{9,13},{10,... | collective-permute-start | bytes 98312 | tf_op jit(solution)/shard_map/ppermute | solution.py:396
  39.5 5.0 %all-to-all-start = ((bf16[64,32,256]{2,1,0:T(8,128)(2,1)}), bf16[64,32,256]{2,1,0:T(8,128)(2,1)S(1)}, u32[]{:S(2)}, u32[]{:S(2)}) async-start(bf16[64,32,256]{2,1,0:T(8,128)(2,1)} %collective-permute-done.13), calls=%async_computation | async-start | bytes 2097152 | tf_op jit(solution)/shard_map/all_to_all | solution.py:439
  44.6 1.7 %collective-permute-start.9 = (f32[2,8,512]{2,1,0:T(8,128)S(1)}, f32[2,8,512]{2,1,0:T(8,128)S(1)}, u32[]{:S(2)}, u32[]{:S(2)}) collective-permute-start(f32[2,8,512]{2,1,0:T(8,128)S(1)} %slice.29), channel_id=1, source_target_pairs={{0,2},{1,3},{2,0},{3,1},{4,6},{5,7},{6,4},{7,5},{8,10},{9,11},{10,... | collective-permute-start | bytes 98312 | tf_op jit(solution)/shard_map/ppermute | solution.py:396
  46.8 2.7 %collective-permute-done.9 = f32[2,8,512]{2,1,0:T(8,128)S(1)} collective-permute-done((f32[2,8,512]{2,1,0:T(8,128)S(1)}, f32[2,8,512]{2,1,0:T(8,128)S(1)}, u32[]{:S(2)}, u32[]{:S(2)}) %collective-permute-start.9) | collective-permute-done | bytes 32800 | tf_op jit(solution)/shard_map/ppermute | solution.py:396
  49.5 1.1 %collective-permute-start.12 = (f32[1,8,512]{2,1,0:T(8,128)S(1)}, f32[1,8,512]{2,1,0:T(8,128)S(1)}, u32[]{:S(2)}, u32[]{:S(2)}) collective-permute-start(f32[1,8,512]{2,1,0:T(8,128)S(1)} %slice.36), channel_id=1, source_target_pairs={{0,1},{1,0},{2,3},{3,2},{4,5},{5,4},{6,7},{7,6},{8,9},{9,8},{10,11... | collective-permute-start | bytes 49160 | tf_op jit(solution)/shard_map/ppermute | solution.py:396
  50.6 6.1 %prompt_part.7 = bf16[192,1024]{1,0:T(8,128)(2,1)} custom-call(s32[2]{0:T(128)S(1)} %pad_add_fusion.place_ref, bf16[192,1024]{1,0:T(8,128)(2,1)S(1)} %bitcast.16, bf16[8,96,256]{2,1,0:T(8,128)(2,1)} %get-tuple-element.51.refs_0_.refs_1_, bf16[8,96,256]{2,1,0:T(8,128)(2,1)} %collective-permute-done.10.refs_1_, ...), custom_call_target="tpu_custom_call" | custom-call | flops 3623878656 | bytes 786432 | tf_op jit(solution)/shard_map/prompt_part/pallas_call | solution.py:139
  57.4 1.0 %copy.20 = bf16[1,64,32,256]{3,2,1,0:T(8,128)(2,1)} copy(bf16[1,64,32,256]{3,2,1,0:T(8,128)(2,1)S(1)} %bitcast.22) | data formatting | bytes 2097152
  (39 shorter events, 3.8 us)
Async XLA Ops:
  2.8 6.6 %collective-permute-start = (bf16[1,112,256]{2,1,0:T(8,128)(2,1)S(1)}, bf16[1,112,256]{2,1,0:T(8,128)(2,1)S(1)}, u32[]{:S(2)}, u32[]{:S(2)}) collective-permute-start(bf16[1,112,256]{2,1,0:T(8,128)(2,1)S(1)} %bitcast.20), channel_id=1, source_target_pairs={{0,8},{8,0},{16,24},{24,16},{1,9},{9,1},{17,25},{25,17},{2,10},{10... | collective-permute-start | bytes 172040 | tf_op jit(solution)/shard_map/ppermute | solution.py:396
  4.4 4.1 %collective-permute-start.2 = (bf16[1,96,256]{2,1,0:T(8,128)(2,1)S(1)}, bf16[1,96,256]{2,1,0:T(8,128)(2,1)S(1)}, u32[]{:S(2)}, u32[]{:S(2)}) collective-permute-start(bf16[1,96,256]{2,1,0:T(8,128)(2,1)S(1)} %bitcast.17), channel_id=1, source_target_pairs={{0,32},{32,0},{64,96},{96,64},{1,33},{33,1},{65,97},{97,65},{2,34}... | collective-permute-start | bytes 147464 | tf_op jit(solution)/shard_map/ppermute | solution.py:396
  5.3 16.8 %copy-start.1 = (bf16[1,192,1024]{2,1,0:T(8,128)(2,1)S(1)}, bf16[1,192,1024]{2,1,0:T(8,128)(2,1)}, u32[]{:S(2)}) copy-start(bf16[1,192,1024]{2,1,0:T(8,128)(2,1)} %param.9) | copy-start | bytes 1179652
  6.7 32.8 %collective-permute-start.13 = (bf16[64,32,256]{2,1,0:T(8,128)(2,1)S(1)}, bf16[64,32,256]{2,1,0:T(8,128)(2,1)}, u32[]{:S(2)}, u32[]{:S(2)}) collective-permute-start(bf16[64,32,256]{2,1,0:T(8,128)(2,1)S(1)} %place_blocks.1), channel_id=1, source_target_pairs={{0,128},{128,0},{1,129},{129,1},{2,130},{130,2},{3,131},{131,3},{4... | collective-permute-start | bytes 3145736 | tf_op jit(solution)/shard_map/ppermute | solution.py:396
  8.5 5.9 %collective-permute-start.3 = (bf16[2,96,256]{2,1,0:T(8,128)(2,1)S(1)}, bf16[2,96,256]{2,1,0:T(8,128)(2,1)S(1)}, u32[]{:S(2)}, u32[]{:S(2)}) collective-permute-start(bf16[2,96,256]{2,1,0:T(8,128)(2,1)S(1)} %pad_maximum_fusion.2), channel_id=1, source_target_pairs={{0,96},{32,64},{64,32},{96,0},{1,97},{33,65},{65,33},{97,1},{2,98}... | collective-permute-start | bytes 294920 | tf_op jit(solution)/shard_map/ppermute | solution.py:396
  9.4 6.1 %collective-permute-start.1 = (bf16[2,112,256]{2,1,0:T(8,128)(2,1)S(1)}, bf16[2,112,256]{2,1,0:T(8,128)(2,1)S(1)}, u32[]{:S(2)}, u32[]{:S(2)}) collective-permute-start(bf16[2,112,256]{2,1,0:T(8,128)(2,1)S(1)} %constant_dynamic-update-slice_fusion), channel_id=1, source_target_pairs={{0,24},{8,16},{16,8},{24,0},{1,25},{9,17},{17,9},{25,1},{2,26},{10... | collective-permute-start | bytes 344072 | tf_op jit(solution)/shard_map/ppermute | solution.py:396
  14.5 10.6 %collective-permute-start.7 = (bf16[4,96,256]{2,1,0:T(8,128)(2,1)S(1)}, bf16[4,96,256]{2,1,0:T(8,128)(2,1)S(1)}, u32[]{:S(2)}, u32[]{:S(2)}) collective-permute-start(bf16[4,96,256]{2,1,0:T(8,128)(2,1)S(1)} %constant_dynamic-update-slice_fusion.2.refs_1_.refs_2_), channel_id=1, source_target_pairs={{0,8},{8,0},{16,24},{24,16},{1,9},{9,1},{17,25},{25,17},{2,10},{10... | collective-permute-start | bytes 589832 | tf_op jit(solution)/shard_map/ppermute | solution.py:396
  15.5 4.0 %collective-permute-start.4 = (bf16[4,16,256]{2,1,0:T(8,128)(2,1)S(1)}, bf16[4,16,256]{2,1,0:T(8,128)(2,1)S(1)}, u32[]{:S(2)}, u32[]{:S(2)}) collective-permute-start(bf16[4,16,256]{2,1,0:T(8,128)(2,1)S(1)} %pad_maximum_fusion.4), channel_id=1, source_target_pairs={{0,32},{32,0},{64,96},{96,64},{1,33},{33,1},{65,97},{97,65},{2,34}... | collective-permute-start | bytes 98312 | tf_op jit(solution)/shard_map/ppermute | solution.py:396
  16.2 8.9 %collective-permute-start.6 = (bf16[4,96,256]{2,1,0:T(8,128)(2,1)S(1)}, bf16[4,96,256]{2,1,0:T(8,128)(2,1)S(1)}, u32[]{:S(2)}, u32[]{:S(2)}) collective-permute-start(bf16[4,96,256]{2,1,0:T(8,128)(2,1)S(1)} %pad_maximum_fusion.refs_0_), channel_id=1, source_target_pairs={{0,32},{32,0},{64,96},{96,64},{1,33},{33,1},{65,97},{97,65},{2,34}... | collective-permute-start | bytes 589832 | tf_op jit(solution)/shard_map/ppermute | solution.py:396
  19.5 5.6 %collective-permute-start.5 = (bf16[8,16,256]{2,1,0:T(8,128)(2,1)S(1)}, bf16[8,16,256]{2,1,0:T(8,128)(2,1)S(1)}, u32[]{:S(2)}, u32[]{:S(2)}) collective-permute-start(bf16[8,16,256]{2,1,0:T(8,128)(2,1)S(1)} %pad_maximum_fusion.3), channel_id=1, source_target_pairs={{0,96},{32,64},{64,32},{96,0},{1,97},{33,65},{65,33},{97,1},{2,98}... | collective-permute-start | bytes 196616 | tf_op jit(solution)/shard_map/ppermute | solution.py:396
  26.0 23.5 %collective-permute-start.10 = (bf16[8,96,256]{2,1,0:T(8,128)(2,1)}, bf16[8,96,256]{2,1,0:T(8,128)(2,1)}, u32[]{:S(2)}, u32[]{:S(2)}) collective-permute-start(bf16[8,96,256]{2,1,0:T(8,128)(2,1)} %get-tuple-element.51.refs_0_.refs_1_), channel_id=1, source_target_pairs={{0,96},{32,64},{64,32},{96,0},{1,97},{33,65},{65,33},{97,1},{2,98}... | collective-permute-start | bytes 1179656 | tf_op jit(solution)/shard_map/ppermute | solution.py:396
  28.6 5.4 %copy-start = (bf16[1024,512]{1,0:T(8,128)(2,1)S(1)}, bf16[1024,512]{1,0:T(8,128)(2,1)}, u32[]{:S(2)}) copy-start(bf16[1024,512]{1,0:T(8,128)(2,1)} %weight_ref.1) | copy-start | bytes 3145732
  28.6 20.9 %collective-permute-start.11 = (bf16[8,96,256]{2,1,0:T(8,128)(2,1)}, bf16[8,96,256]{2,1,0:T(8,128)(2,1)}, u32[]{:S(2)}, u32[]{:S(2)}) collective-permute-start(bf16[8,96,256]{2,1,0:T(8,128)(2,1)} %get-tuple-element.52.refs_2_), channel_id=1, source_target_pairs={{0,24},{8,16},{16,8},{24,0},{1,25},{9,17},{17,9},{25,1},{2,26},{10... | collective-permute-start | bytes 1179656 | tf_op jit(solution)/shard_map/ppermute | solution.py:396
  34.9 9.6 %collective-permute-start.8 = (bf16[4,8,512]{2,1,0:T(8,128)(2,1)S(1)}, bf16[4,8,512]{2,1,0:T(8,128)(2,1)S(1)}, u32[]{:S(2)}, u32[]{:S(2)}) collective-permute-start(bf16[4,8,512]{2,1,0:T(8,128)(2,1)S(1)} %get-tuple-element.46), channel_id=1, source_target_pairs={{0,4},{1,5},{2,6},{3,7},{4,0},{5,1},{6,2},{7,3},{8,12},{9,13},{10,... | collective-permute-start | bytes 98312 | tf_op jit(solution)/shard_map/ppermute | solution.py:396
  39.5 17.9 %all-to-all-start = ((bf16[64,32,256]{2,1,0:T(8,128)(2,1)}), bf16[64,32,256]{2,1,0:T(8,128)(2,1)S(1)}, u32[]{:S(2)}, u32[]{:S(2)}) async-start(bf16[64,32,256]{2,1,0:T(8,128)(2,1)} %collective-permute-done.13), calls=%async_computation | async-start | bytes 2097152 | tf_op jit(solution)/shard_map/all_to_all | solution.py:439
  44.6 4.9 %collective-permute-start.9 = (f32[2,8,512]{2,1,0:T(8,128)S(1)}, f32[2,8,512]{2,1,0:T(8,128)S(1)}, u32[]{:S(2)}, u32[]{:S(2)}) collective-permute-start(f32[2,8,512]{2,1,0:T(8,128)S(1)} %slice.29), channel_id=1, source_target_pairs={{0,2},{1,3},{2,0},{3,1},{4,6},{5,7},{6,4},{7,5},{8,10},{9,11},{10,... | collective-permute-start | bytes 98312 | tf_op jit(solution)/shard_map/ppermute | solution.py:396
  49.5 7.3 %collective-permute-start.12 = (f32[1,8,512]{2,1,0:T(8,128)S(1)}, f32[1,8,512]{2,1,0:T(8,128)S(1)}, u32[]{:S(2)}, u32[]{:S(2)}) collective-permute-start(f32[1,8,512]{2,1,0:T(8,128)S(1)} %slice.36), channel_id=1, source_target_pairs={{0,1},{1,0},{2,3},{3,2},{4,5},{5,4},{6,7},{7,6},{8,9},{9,8},{10,11... | collective-permute-start | bytes 49160 | tf_op jit(solution)/shard_map/ppermute | solution.py:396
